TPU v7x, 128 devices: a whole 4x4x4 slice. The times are simulated.
128 devices in a mesh: rep: 8 (over y, x_lo), shard: 16 (over z, x_hi, core).
Axes of the slice: x: 4 (x_hi: 2, x_lo: 2; x = x_hi * 2 + x_lo), y: 4, z: 4, core: 2. Of those that a mesh axis runs over, the one named last changes fastest.
Arguments:
- inputs: float32 [24576, 1024], P(('rep', 'shard')), may hold values from -6 to 6
- cotangent: float32 [24576, 1024], P(('rep', 'shard')), may hold values from -6 to 6
- lengths: int32 [128, 4], P(('rep', 'shard')), may hold values from 0 to 192, as said below
- ln_gain: bfloat16 [2, 1024], P(None, 'shard'), may hold values from 0.5 to 1.5
- ln_bias: bfloat16 [2, 1024], P(None, 'shard'), may hold values from -3 to 3
- w_qkv: bfloat16 [2, 1024, 3072], P(None, 'shard'), may hold values from -0.1875 to 0.1875
- w_attn_out: bfloat16 [2, 1024, 1024], P(None, 'shard'), may hold values from -1 to 1
- w_in: bfloat16 [2, 1024, 4096], P(None, 'shard'), may hold values from -0.1875 to 0.1875
- b_in: bfloat16 [2, 4096], P(None, 'shard'), may hold values from -3 to 3
- w_fc: bfloat16 [2, 4096, 1024], P(None, 'shard'), may hold values from -0.09375 to 0.09375
- b_fc: bfloat16 [2, 1024], P(None, 'shard'), may hold values from -3 to 3
Outputs:
- outputs: float32 [24576, 1024], P(('rep', 'shard'))
- input_grad: float32 [24576, 1024], P(('rep', 'shard'))
- ln_gain_grad: float32 [2, 1024], P(None, 'shard')
- ln_bias_grad: float32 [2, 1024], P(None, 'shard')
- w_qkv_grad: float32 [2, 1024, 3072], P(None, 'shard')
- w_attn_out_grad: float32 [2, 1024, 1024], P(None, 'shard')
- w_in_grad: float32 [2, 1024, 4096], P(None, 'shard')
- b_in_grad: float32 [2, 4096], P(None, 'shard')
- w_fc_grad: float32 [2, 4096, 1024], P(None, 'shard')
- b_fc_grad: float32 [2, 1024], P(None, 'shard')
Inputs may be any that keep to these rules, and one draw needn't show every extreme that they name: Row b gives, in order, the lengths of the sequences packed from the start of token buffer b; a length of 0 is an empty slot. A row's lengths sum to 96 or more and to 192 at most, and in every draw some row holds one sequence of exactly 192 tokens.
All inputs are finite; a program needn't handle non-finite values.
Results may differ from a plain program's by a relative error of at most 0.02.
Values may be sent and summed in bfloat16 or wider, within the bound.
A program may use at most 256 MiB of HBM per device.

v0:
```python
import math

import jax
import jax.numpy as jnp
from jax import lax
from jax.sharding import PartitionSpec as P

D = 1024
HEADS = 16
HEAD = 64
ROT = 32
LAYERS = 2
SLOTS = 4


EPSILON = 1e-05
NEGATIVE = -1e30


def layer_norm(values, gain_row, bias_row):
    centre = values - jnp.mean(values, axis=-1, keepdims=True)
    spread = jnp.mean(centre * centre, axis=-1, keepdims=True)
    return centre * lax.rsqrt(spread + EPSILON) * gain_row + bias_row


def rotate(values, cosine_table, sine_table):
    half_rot = ROT // 2
    first_half = values[..., :half_rot]
    second_half = values[..., half_rot:ROT]
    return jnp.concatenate(
        [
            first_half * cosine_table - second_half * sine_table,
            second_half * cosine_table + first_half * sine_table,
            values[..., ROT:],
        ],
        axis=-1,
    )


def unrotate(values, cosine_table, sine_table):
    half_rot = ROT // 2
    first_half = values[..., :half_rot]
    second_half = values[..., half_rot:ROT]
    return jnp.concatenate(
        [
            first_half * cosine_table + second_half * sine_table,
            second_half * cosine_table - first_half * sine_table,
            values[..., ROT:],
        ],
        axis=-1,
    )


def gelu_tanh(values):
    return (
        0.5
        * values
        * (1.0 + jnp.tanh(0.7978845608028654 * (values + 0.044715 * values * values * values)))
    )


def outer_sum(first_op, second_op):
    return lax.dot_general(
        first_op, second_op, (((0,), (0,)), ((), ())), preferred_element_type=jnp.float32
    )


def back_product(first_op, second_op):
    return lax.dot_general(
        first_op, second_op, (((1,), (1,)), ((), ())), preferred_element_type=jnp.float32
    )


def fetch_forward(depth_index, ln_gain, ln_bias, w_qkv, w_attn_out, w_in, b_in, w_fc, b_fc):
    return (
        lax.all_gather(ln_gain[depth_index], "shard", axis=0, tiled=True),
        lax.all_gather(ln_bias[depth_index], "shard", axis=0, tiled=True),
        lax.all_gather(w_qkv[depth_index], "shard", axis=0, tiled=True),
        lax.all_gather(w_attn_out[depth_index], "shard", axis=0, tiled=True),
        lax.all_gather(w_in[depth_index], "shard", axis=0, tiled=True),
        lax.all_gather(b_in[depth_index], "shard", axis=0, tiled=True),
        lax.all_gather(w_fc[depth_index], "shard", axis=0, tiled=True),
        lax.all_gather(b_fc[depth_index], "shard", axis=0, tiled=True),
    )


def fetch_backward(depth_index, ln_gain, ln_bias, w_qkv, w_attn_out, w_in, b_in, w_fc, b_fc):
    return (
        lax.all_gather(ln_gain[depth_index], "shard", axis=0, tiled=True),
        lax.all_gather(ln_bias[depth_index], "shard", axis=0, tiled=True),
        lax.all_gather(w_qkv[depth_index], "shard", axis=0, tiled=True),
        lax.all_gather(w_attn_out[depth_index], "shard", axis=0, tiled=True),
        lax.all_gather(w_in[depth_index], "shard", axis=0, tiled=True),
        lax.all_gather(b_in[depth_index], "shard", axis=0, tiled=True),
        lax.all_gather(w_fc[depth_index], "shard", axis=0, tiled=True),
        lax.all_gather(b_fc[depth_index], "shard", axis=0, tiled=True),
    )


def attention_weights(queries, key_rows, allowed):
    scores = jnp.einsum("qhd,khd->hqk", queries, key_rows, preferred_element_type=jnp.float32) * (
        1.0 / math.sqrt(HEAD)
    )
    return jnp.where(allowed[None], scores, NEGATIVE)


def layer_forward(layer_input, params, allowed, cosine_table, sine_table):
    gain_row, bias_row, qkv_weight, attn_weight, in_weight, in_bias, fc_weight, fc_bias = params
    row_count = layer_input.shape[0]
    normed = layer_norm(
        layer_input, gain_row.astype(jnp.float32), bias_row.astype(jnp.float32)
    ).astype(jnp.bfloat16)
    packed = jnp.dot(normed, qkv_weight, preferred_element_type=jnp.float32).reshape(
        row_count, 3, HEADS, HEAD
    )
    queries = rotate(packed[:, 0], cosine_table, sine_table).astype(jnp.bfloat16)
    key_rows = rotate(packed[:, 1], cosine_table, sine_table).astype(jnp.bfloat16)
    value_rows = packed[:, 2].astype(jnp.bfloat16)
    masked = attention_weights(queries, key_rows, allowed)
    row_peak = jnp.max(masked, axis=-1, keepdims=True)
    exponent = jnp.exp(masked - row_peak)
    row_total = jnp.sum(exponent, axis=-1, keepdims=True)
    soft_weights = exponent / row_total
    log_total = row_peak + jnp.log(row_total)
    attended = (
        jnp.einsum(
            "hqk,khd->qhd",
            soft_weights.astype(jnp.bfloat16),
            value_rows,
            preferred_element_type=jnp.float32,
        )
        .reshape(row_count, D)
        .astype(jnp.bfloat16)
    )
    pre_act = jnp.dot(normed, in_weight, preferred_element_type=jnp.float32) + in_bias.astype(
        jnp.float32
    )
    activated = gelu_tanh(pre_act).astype(jnp.bfloat16)
    branch = jnp.dot(attended, attn_weight, preferred_element_type=jnp.float32) + (
        jnp.dot(activated, fc_weight, preferred_element_type=jnp.float32)
        + fc_bias.astype(jnp.float32)
    )
    stored = (
        layer_input,
        normed,
        queries,
        key_rows,
        value_rows,
        log_total,
        attended,
        pre_act,
        activated,
    )
    return (layer_input + branch, stored)


def layer_backward(grad_out, params, stored, allowed, cosine_table, sine_table):
    gain_row, bias_row, qkv_weight, attn_weight, in_weight, in_bias, fc_weight, fc_bias = params
    layer_input, normed, queries, key_rows, value_rows, log_total, attended, pre_act, activated = (
        stored
    )
    row_count = layer_input.shape[0]
    grad_low = grad_out.astype(jnp.bfloat16)
    fc_grad = outer_sum(activated, grad_low)
    fc_bias_grad = jnp.sum(grad_low.astype(jnp.float32), axis=0)
    attn_grad = outer_sum(attended, grad_low)
    act_grad = back_product(grad_low, fc_weight)
    gelu_pull = jax.vjp(gelu_tanh, pre_act)[1]
    pre_grad = gelu_pull(act_grad)[0].astype(jnp.bfloat16)
    in_grad = outer_sum(normed, pre_grad)
    in_bias_grad = jnp.sum(pre_grad.astype(jnp.float32), axis=0)
    mixed_grad = (
        back_product(grad_low, attn_weight).astype(jnp.bfloat16).reshape(row_count, HEADS, HEAD)
    )
    masked = attention_weights(queries, key_rows, allowed)
    soft_weights = jnp.exp(masked - log_total)
    soft_grad = jnp.einsum(
        "qhd,khd->hqk", mixed_grad, value_rows, preferred_element_type=jnp.float32
    )
    value_grad = jnp.einsum(
        "hqk,qhd->khd",
        soft_weights.astype(jnp.bfloat16),
        mixed_grad,
        preferred_element_type=jnp.float32,
    )
    centred = soft_weights * (soft_grad - jnp.sum(soft_weights * soft_grad, axis=-1, keepdims=True))
    score_grad = centred.astype(jnp.bfloat16)
    query_grad = jnp.einsum(
        "hqk,khd->qhd", score_grad, key_rows, preferred_element_type=jnp.float32
    ) * (1.0 / math.sqrt(HEAD))
    key_grad = jnp.einsum(
        "hqk,qhd->khd", score_grad, queries, preferred_element_type=jnp.float32
    ) * (1.0 / math.sqrt(HEAD))
    packed_grad = (
        jnp.stack(
            [
                unrotate(query_grad, cosine_table, sine_table),
                unrotate(key_grad, cosine_table, sine_table),
                value_grad,
            ],
            axis=1,
        )
        .reshape(row_count, 3 * D)
        .astype(jnp.bfloat16)
    )
    qkv_grad = outer_sum(normed, packed_grad)
    normed_grad = back_product(pre_grad, in_weight) + back_product(packed_grad, qkv_weight)
    norm_pull = jax.vjp(
        layer_norm, layer_input, gain_row.astype(jnp.float32), bias_row.astype(jnp.float32)
    )[1]
    input_part, gain_grad, bias_grad = norm_pull(normed_grad)
    layer_grads = (
        gain_grad,
        bias_grad,
        qkv_grad,
        attn_grad,
        in_grad,
        in_bias_grad,
        fc_grad,
        fc_bias_grad,
    )
    return (grad_out + input_part, layer_grads)


def reduce_grads(layer_grads):
    partial_sums = (
        lax.psum_scatter(
            layer_grads[0].astype(jnp.bfloat16), "shard", scatter_dimension=0, tiled=True
        ).astype(jnp.float32),
        lax.psum_scatter(
            layer_grads[1].astype(jnp.bfloat16), "shard", scatter_dimension=0, tiled=True
        ).astype(jnp.float32),
        lax.psum_scatter(
            layer_grads[2].astype(jnp.bfloat16), "shard", scatter_dimension=0, tiled=True
        ).astype(jnp.float32),
        lax.psum_scatter(
            layer_grads[3].astype(jnp.bfloat16), "shard", scatter_dimension=0, tiled=True
        ).astype(jnp.float32),
        lax.psum_scatter(
            layer_grads[4].astype(jnp.bfloat16), "shard", scatter_dimension=0, tiled=True
        ).astype(jnp.float32),
        lax.psum_scatter(
            layer_grads[5].astype(jnp.bfloat16), "shard", scatter_dimension=0, tiled=True
        ).astype(jnp.float32),
        lax.psum_scatter(
            layer_grads[6].astype(jnp.bfloat16), "shard", scatter_dimension=0, tiled=True
        ).astype(jnp.float32),
        lax.psum_scatter(
            layer_grads[7].astype(jnp.bfloat16), "shard", scatter_dimension=0, tiled=True
        ).astype(jnp.float32),
    )
    return (
        lax.psum(partial_sums[0].astype(jnp.bfloat16), "rep").astype(jnp.float32),
        lax.psum(partial_sums[1].astype(jnp.bfloat16), "rep").astype(jnp.float32),
        lax.psum(partial_sums[2].astype(jnp.bfloat16), "rep").astype(jnp.float32),
        lax.psum(partial_sums[3].astype(jnp.bfloat16), "rep").astype(jnp.float32),
        lax.psum(partial_sums[4].astype(jnp.bfloat16), "rep").astype(jnp.float32),
        lax.psum(partial_sums[5].astype(jnp.bfloat16), "rep").astype(jnp.float32),
        lax.psum(partial_sums[6].astype(jnp.bfloat16), "rep").astype(jnp.float32),
        lax.psum(partial_sums[7].astype(jnp.bfloat16), "rep").astype(jnp.float32),
    )


def per_device(
    inputs, cotangent, lengths, ln_gain, ln_bias, w_qkv, w_attn_out, w_in, b_in, w_fc, b_fc
):
    row_count = inputs.shape[0]
    offsets = jnp.arange(row_count, dtype=jnp.int32)
    seq_ends = jnp.cumsum(lengths[0])
    passed = (offsets[:, None] >= seq_ends[None, :]).astype(jnp.int32)
    segment = jnp.sum(passed, axis=1)
    position = offsets - jnp.sum(passed * lengths[0][None, :], axis=1)
    allowed = (segment[:, None] == segment[None, :]) & (offsets[:, None] >= offsets[None, :])
    frequency = 10000.0 ** (-jnp.arange(ROT // 2, dtype=jnp.float32) * 2.0 / ROT)
    angles = position.astype(jnp.float32)[:, None, None] * frequency
    cosine_table = jnp.cos(angles)
    sine_table = jnp.sin(angles)
    valid_rows = (segment < SLOTS).astype(jnp.float32)[:, None]
    hidden = inputs
    saved = []
    fetched = []
    for depth_index in range(LAYERS):
        params = fetch_forward(
            depth_index, ln_gain, ln_bias, w_qkv, w_attn_out, w_in, b_in, w_fc, b_fc
        )
        hidden, stored = layer_forward(hidden, params, allowed, cosine_table, sine_table)
        saved.append(stored)
        fetched.append(params)
    grad_out = cotangent * valid_rows
    collected = []
    for depth_index in reversed(range(LAYERS)):
        params = fetch_backward(
            depth_index, ln_gain, ln_bias, w_qkv, w_attn_out, w_in, b_in, w_fc, b_fc
        )
        grad_out, layer_grads = layer_backward(
            grad_out, params, saved[depth_index], allowed, cosine_table, sine_table
        )
        collected.append(reduce_grads(layer_grads))
    collected = collected[::-1]
    stacked = [
        jnp.stack([collected[depth_index][member] for depth_index in range(LAYERS)])
        for member in range(8)
    ]
    return (
        hidden,
        grad_out,
        stacked[0],
        stacked[1],
        stacked[2],
        stacked[3],
        stacked[4],
        stacked[5],
        stacked[6],
        stacked[7],
    )


def solution(mesh):
    in_specs = (
        P(("rep", "shard"), None),
        P(("rep", "shard"), None),
        P(("rep", "shard"), None),
        P(None, "shard"),
        P(None, "shard"),
        P(None, "shard", None),
        P(None, "shard", None),
        P(None, "shard", None),
        P(None, "shard"),
        P(None, "shard", None),
        P(None, "shard"),
    )
    out_specs = (
        P(("rep", "shard"), None),
        P(("rep", "shard"), None),
        P(None, "shard"),
        P(None, "shard"),
        P(None, "shard", None),
        P(None, "shard", None),
        P(None, "shard", None),
        P(None, "shard"),
        P(None, "shard", None),
        P(None, "shard"),
    )
    return jax.shard_map(
        per_device, mesh=mesh, in_specs=in_specs, out_specs=out_specs, check_vma=False
    )
```

profile of v0, /device:TPU:32, one launch (start us, length us, event | category | flops | bytes accessed | tf_op | source)
XLA Modules:
  0.0 1456.5 jit_solution(17610005895142564542)
XLA Ops:
  19.2 62.2 %all-reduce.15 = (bf16[1024]{0:T(1024)(128)(2,1)S(1)}, bf16[1024]{0:T(1024)(128)(2,1)S(1)}, bf16[1024]{0:T(1024)(128)(2,1)S(1)}, bf16[1024]{0:T(1024)(128)(2,1)S(1)}, bf16[1024]{0:T(1024)(128)(2,1)S(1)}) all-reduce(bf16[1024]{0:T(1024)(128)(2,1)S(1)} %dynamic-update-slice.2, ...), channel_id=9, replica_groups=mesh['rep'=8,'shard'=16] {'shard'}, use_global_device_ids=true, to_apply=%add.2 | all-reduce | flops 5120 | bytes 20480
  83.2 25.2 %all-gather.13 = bf16[1,4096]{1,0:T(2,128)(2,1)S(1)} all-gather(bf16[1,256]{1,0:T(2,128)(2,1)S(1)} %get-tuple-element.94), channel_id=15, replica_groups=mesh['rep'=8,'shard'=16] {'shard'}, dimensions={1}, use_global_device_ids=true | all-gather | bytes 8704 | tf_op jit(solution)/shard_map/all_gather | solution.py:81
  109.0 22.6 %all-gather.5 = bf16[1,4096]{1,0:T(2,128)(2,1)S(1)} all-gather(bf16[1,256]{1,0:T(2,128)(2,1)S(1)} %get-tuple-element.95), channel_id=7, replica_groups=mesh['rep'=8,'shard'=16] {'shard'}, dimensions={1}, use_global_device_ids=true | all-gather | bytes 8704 | tf_op jit(solution)/shard_map/all_gather | solution.py:81
  138.9 5.6 fusion.22
  148.8 51.0 %all-gather.29.cloned.1.call-done = bf16[1,1024,4096]{2,1,0:T(8,128)(2,1)} async-done(((bf16[1,64,4096]{2,1,0:T(8,128)(2,1)}), bf16[1,1024,4096]{2,1,0:T(8,128)(2,1)}) %all-gather.29.cloned.1.call-update) | async-done | bytes 8388624 | tf_op jit(solution)/shard_map/all_gather | solution.py:80
  199.8 6.9 fusion.24
  206.7 66.9 %all-gather.31.cloned.1.call-done = bf16[1,4096,1024]{2,1,0:T(8,128)(2,1)} async-done(((bf16[1,256,1024]{2,1,0:T(8,128)(2,1)}), bf16[1,4096,1024]{2,1,0:T(8,128)(2,1)}) %all-gather.31.cloned.1.call-update) | async-done | bytes 8388624 | tf_op jit(solution)/shard_map/all_gather | solution.py:82
  273.6 7.3 fusion.96
  280.8 41.5 %all-gather.27.cloned.1.call-done = bf16[1,1024,1024]{2,1,0:T(8,128)(2,1)} async-done(((bf16[1,64,1024]{2,1,0:T(8,128)(2,1)}), bf16[1,1024,1024]{2,1,0:T(8,128)(2,1)}) %all-gather.27.cloned.1.call-update) | async-done | bytes 2097168 | tf_op jit(solution)/shard_map/all_gather | solution.py:79
  327.7 59.5 %all-gather.33.cloned.1.call-done = bf16[1,1024,3072]{2,1,0:T(8,128)(2,1)} async-done(((bf16[1,64,3072]{2,1,0:T(8,128)(2,1)}), bf16[1,1024,3072]{2,1,0:T(8,128)(2,1)}) %all-gather.33.cloned.1.call-update) | async-done | bytes 6291472 | tf_op jit(solution)/shard_map/all_gather | solution.py:78
  387.2 6.0 fusion.18
  403.7 56.8 %all-gather.37.cloned.1.call-done = bf16[1,1024,4096]{2,1,0:T(8,128)(2,1)} async-done(((bf16[1,64,4096]{2,1,0:T(8,128)(2,1)}), bf16[1,1024,4096]{2,1,0:T(8,128)(2,1)}) %all-gather.37.cloned.1.call-update) | async-done | bytes 8388624 | tf_op jit(solution)/shard_map/all_gather | solution.py:80
  460.5 6.9 fusion.27
  467.4 67.0 %all-gather.39.cloned.1.call-done = bf16[1,4096,1024]{2,1,0:T(8,128)(2,1)} async-done(((bf16[1,256,1024]{2,1,0:T(8,128)(2,1)}), bf16[1,4096,1024]{2,1,0:T(8,128)(2,1)}) %all-gather.39.cloned.1.call-update) | async-done | bytes 8388624 | tf_op jit(solution)/shard_map/all_gather | solution.py:82
  534.4 10.1 fusion.146
  586.4 7.6 convolution_convert_fusion.1
  595.0 7.7 convolution_convert_fusion
  603.8 7.1 convolution_convert_fusion.2
  610.9 9.2 fusion.147
  621.3 5.8 convolution_convert_fusion.3
  628.7 7.1 fusion.12
  635.9 5.9 multiply_reduce_fusion.3
  642.0 58.8 %all-reduce.14 = (bf16[1024]{0:T(1024)(128)(2,1)S(1)}, bf16[1024]{0:T(1024)(128)(2,1)S(1)}, bf16[1024]{0:T(1024)(128)(2,1)S(1)}, bf16[1024]{0:T(1024)(128)(2,1)S...) all-reduce(bf16[1024]{0:T(1024)(128)(2,1)S(1)} %dynamic-update-slic, ...), channel_id=17, replica_groups=mesh['rep'=8,'shard'=16] {'shard'}, use_global_device_ids=true, to_apply=%add.5 | all-reduce | flops 15360 | bytes 61440
  700.9 76.2 %reduce-scatter.9.cloned.1.call-done = bf16[64,3072]{1,0:T(8,128)(2,1)} async-done(((bf16[1024,3072]{1,0:T(8,128)(2,1)}), bf16[64,3072]{1,0:T(8,128)(2,1)}) %reduce-scatter.9.cloned.1.call-update) | async-done | bytes 393232 | tf_op jit(solution)/shard_map/reduce_scatter | solution.py:233
  777.0 93.2 %reduce-scatter.11.cloned.1.call-done = bf16[64,3072]{1,0:T(8,128)(2,1)} async-done(((bf16[1024,3072]{1,0:T(8,128)(2,1)}), bf16[64,3072]{1,0:T(8,128)(2,1)}) %reduce-scatter.11.cloned.1.call-update) | async-done | bytes 393232 | tf_op jit(solution)/shard_map/reduce_scatter | solution.py:233
  870.3 105.6 %reduce-scatter.21.cloned.1.call-done = bf16[256,1024]{1,0:T(8,128)(2,1)} async-done(((bf16[4096,1024]{1,0:T(8,128)(2,1)}), bf16[256,1024]{1,0:T(8,128)(2,1)}) %reduce-scatter.21.cloned.1.call-update) | async-done | bytes 524304 | tf_op jit(solution)/shard_map/reduce_scatter | solution.py:245
  975.8 105.4 %reduce-scatter.23.cloned.1.call-done = bf16[256,1024]{1,0:T(8,128)(2,1)} async-done(((bf16[4096,1024]{1,0:T(8,128)(2,1)}), bf16[256,1024]{1,0:T(8,128)(2,1)}) %reduce-scatter.23.cloned.1.call-update) | async-done | bytes 524304 | tf_op jit(solution)/shard_map/reduce_scatter | solution.py:245
  1081.2 105.4 %reduce-scatter.19.cloned.1.call-done = bf16[64,4096]{1,0:T(8,128)(2,1)} async-done(((bf16[1024,4096]{1,0:T(8,128)(2,1)}), bf16[64,4096]{1,0:T(8,128)(2,1)}) %reduce-scatter.19.cloned.1.call-update) | async-done | bytes 524304 | tf_op jit(solution)/shard_map/reduce_scatter | solution.py:239
  1186.6 105.3 %reduce-scatter.17.cloned.1.call-done = bf16[64,4096]{1,0:T(8,128)(2,1)} async-done(((bf16[1024,4096]{1,0:T(8,128)(2,1)}), bf16[64,4096]{1,0:T(8,128)(2,1)}) %reduce-scatter.17.cloned.1.call-update) | async-done | bytes 524304 | tf_op jit(solution)/shard_map/reduce_scatter | solution.py:239
  1292.5 19.6 %all-reduce.16 = (bf16[1,64]{1,0:T(2,128)(2,1)S(1)}, bf16[1,64]{1,0:T(2,128)(2,1)S(1)}, bf16[1,64]{1,0:T(2,128)(2,1)S(1)}, bf16[1,64]{1,0:T(2,128)(2,1)S(1)}, bf...) all-reduce(bf16[1,64]{1,0:T(2,128)(2,1)S(1)} %dynamic-slice_bitcast, ...), channel_id=1, replica_groups=mesh['rep'=8,'shard'=16] {'rep'}, use_global_device_ids=true, to_apply=%region_22.23 | all-reduce | flops 896 | bytes 3584 | tf_op jit(solution)/shard_map/psum | solution.py:253
  1316.0 5.7 fusion.99
  1323.2 119.3 %all-reduce.20.cloned.1.call-done = (bf16[1,64,3072]{2,1,0:T(8,128)(2,1)}, bf16[1,64,3072]{2,1,0:T(8,128)(2,1)}, bf16[1,64,1024]{2,1,0:T(8,128)(2,1)}, bf16[1,64...) async-done(((bf16[1,64,3072]{2,1,0:T(8,128)(2,1)}, ...) | async-done | bytes 3145744 | tf_op jit(solution)/shard_map/psum | solution.py:255
  (360 shorter events, 98.8 us)
Async XLA Ops:
  7.2 128.2 %all-gather.35.cloned.1.call-start = ((), (), s32[]{:S(2)}) async-start(), calls=%async_computation.21 | async-start | bytes 2228224 | tf_op jit(solution)/shard_map/all_gather | solution.py:79
  9.1 129.8 %all-gather.25.cloned.1.call-start = ((), (), s32[]{:S(2)}) async-start(), calls=%async_computation.16 | async-start | bytes 6684672 | tf_op jit(solution)/shard_map/all_gather | solution.py:78
  11.2 72.0 %copy-start.91 = (bf16[2,256]{1,0:T(2,128)(2,1)S(1)}, bf16[2,256]{1,0:T(2,128)(2,1)}, u32[]{:S(2)}) copy-start(bf16[2,256]{1,0:T(2,128)(2,1)} %param.19) | copy-start | bytes 3076
  11.3 121.0 %copy-start.96 = (s32[1,4]{1,0:T(1,128)S(1)}, s32[1,4]{1,0:T(1,128)}, u32[]{:S(2)}) copy-start(s32[1,4]{1,0:T(1,128)} %param.13) | copy-start | bytes 52
  11.3 121.2 %copy-start.5 = (f32[192,1024]{1,0:T(8,128)S(1)}, f32[192,1024]{1,0:T(8,128)}, u32[]{:S(2)}) copy-start(f32[192,1024]{1,0:T(8,128)} %param.11) | copy-start | bytes 2359300
  11.3 188.5 %all-gather.29.cloned.1.call-start = ((), (), s32[]{:S(2)}) async-start(), calls=%async_computation.18 | async-start | bytes 8912896 | tf_op jit(solution)/shard_map/all_gather | solution.py:80
  12.4 122.0 %copy-start.12 = (f32[192,1024]{1,0:T(8,128)S(1)}, f32[192,1024]{1,0:T(8,128)}, u32[]{:S(2)}) copy-start(f32[192,1024]{1,0:T(8,128)} %param.12) | copy-start | bytes 2359300
  12.4 261.1 %all-gather.31.cloned.1.call-start = ((), (), s32[]{:S(2)}) async-start(), calls=%async_computation.19 | async-start | bytes 8912896 | tf_op jit(solution)/shard_map/all_gather | solution.py:82
  13.5 308.8 %all-gather.27.cloned.1.call-start = ((), (), s32[]{:S(2)}) async-start(), calls=%async_computation.17 | async-start | bytes 2228224 | tf_op jit(solution)/shard_map/all_gather | solution.py:79
  14.1 373.0 %all-gather.33.cloned.1.call-start = ((), (), s32[]{:S(2)}) async-start(), calls=%async_computation.20 | async-start | bytes 6684672 | tf_op jit(solution)/shard_map/all_gather | solution.py:78
  14.7 445.8 %all-gather.37.cloned.1.call-start = ((), (), s32[]{:S(2)}) async-start(), calls=%async_computation.22 | async-start | bytes 8912896 | tf_op jit(solution)/shard_map/all_gather | solution.py:80
  15.4 519.0 %all-gather.39.cloned.1.call-start = ((), (), s32[]{:S(2)}) async-start(), calls=%async_computation.23 | async-start | bytes 8912896 | tf_op jit(solution)/shard_map/all_gather | solution.py:82
  16.2 684.7 %reduce-scatter.15.cloned.1.call-start = ((), (), s32[]{:S(2)}) async-start(), calls=%async_computation.11 | async-start | bytes 2228224 | tf_op jit(solution)/shard_map/reduce_scatter | solution.py:236
  82.0 53.4 %copy-start.60 = (f32[1024]{0:T(1024)}, f32[1024]{0:T(1024)S(1)}, u32[]{:S(2)}) copy-start(f32[1024]{0:T(1024)S(1)} %convert_element_type.278) | copy-start | bytes 12292
  133.7 11.1 copy-start.53
  403.7 297.2 %reduce-scatter.13.cloned.1.call-start = ((), (), s32[]{:S(2)}) async-start(), calls=%async_computation.10 | async-start | bytes 2228224 | tf_op jit(solution)/shard_map/reduce_scatter | solution.py:236
  534.4 10.1 copy-start.25
  534.4 10.1 copy-start.26
  534.4 10.1 copy-start.55
  560.7 216.3 %reduce-scatter.9.cloned.1.call-start = ((), (), s32[]{:S(2)}) async-start(), calls=%async_computation.8 | async-start | bytes 6684672 | tf_op jit(solution)/shard_map/reduce_scatter | solution.py:233
  578.5 291.8 %reduce-scatter.11.cloned.1.call-start = ((), (), s32[]{:S(2)}) async-start(), calls=%async_computation.9 | async-start | bytes 6684672 | tf_op jit(solution)/shard_map/reduce_scatter | solution.py:233
  585.4 390.4 %reduce-scatter.21.cloned.1.call-start = ((), (), s32[]{:S(2)}) async-start(), calls=%async_computation.14 | async-start | bytes 8912896 | tf_op jit(solution)/shard_map/reduce_scatter | solution.py:245
  594.1 487.2 %reduce-scatter.23.cloned.1.call-start = ((), (), s32[]{:S(2)}) async-start(), calls=%async_computation.15 | async-start | bytes 8912896 | tf_op jit(solution)/shard_map/reduce_scatter | solution.py:245
  602.8 583.9 %reduce-scatter.19.cloned.1.call-start = ((), (), s32[]{:S(2)}) async-start(), calls=%async_computation.13 | async-start | bytes 8912896 | tf_op jit(solution)/shard_map/reduce_scatter | solution.py:239
  610.9 681.1 %reduce-scatter.17.cloned.1.call-start = ((), (), s32[]{:S(2)}) async-start(), calls=%async_computation.12 | async-start | bytes 8912896 | tf_op jit(solution)/shard_map/reduce_scatter | solution.py:239
  627.1 815.5 %all-reduce.20.cloned.1.call-start = ((), (), s32[]{:S(2)}) async-start(), calls=%async_computation.24 | async-start | bytes 6291456 | tf_op jit(solution)/shard_map/psum | solution.py:255
  641.9 672.6 %copy-start.83 = (f32[192]{0:T(256)S(1)}, f32[192]{0:T(256)}, u32[]{:S(2)}) copy-start(f32[192]{0:T(256)} %copy-done.82) | copy-start | bytes 2308
  641.9 672.6 %copy-start.28 = (f32[192,1024]{1,0:T(8,128)S(1)}, f32[192,1024]{1,0:T(8,128)}, u32[]{:S(2)}) copy-start(f32[192,1024]{1,0:T(8,128)} %get-tuple-element.115) | copy-start | bytes 2359300
  641.9 672.9 %copy-start.14 = (f32[192,1024]{1,0:T(8,128)S(1)}, f32[192,1024]{1,0:T(8,128)}, u32[]{:S(2)}) copy-start(f32[192,1024]{1,0:T(8,128)} %param.12) | copy-start | bytes 2359300
  641.9 672.9 %copy-start.16 = (f32[192,1024]{1,0:T(8,128)S(1)}, f32[192,1024]{1,0:T(8,128)}, u32[]{:S(2)}) copy-start(f32[192,1024]{1,0:T(8,128)} %copy-done.15) | copy-start | bytes 2359300
  641.9 672.9 %copy-start.74 = (f32[192]{0:T(256)S(1)}, f32[192]{0:T(256)}, u32[]{:S(2)}) copy-start(f32[192]{0:T(256)} %copy-done.72) | copy-start | bytes 2308
  641.9 672.9 %copy-start.81 = (f32[192]{0:T(256)S(1)}, f32[192]{0:T(256)}, u32[]{:S(2)}) copy-start(f32[192]{0:T(256)} %copy-done.80) | copy-start | bytes 2308
  (85 other events, 263.7 us)
Sparse Core Ops, SparseCore 0:
  11.1 49.6 all-gather.34
  63.8 61.9 all-gather.24
  128.8 70.9 all-gather.28
  202.7 70.8 all-gather.30
  275.9 46.4 all-gather.26
  325.3 61.8 all-gather.32
  389.6 70.8 all-gather.36
  463.6 70.8 all-gather.38
  538.9 69.9 reduce-scatter.14
  613.7 70.2 reduce-scatter.12
  688.1 88.8 reduce-scatter.8
  781.7 88.5 reduce-scatter.10
  874.5 101.2 reduce-scatter.20
  980.0 101.2 reduce-scatter.22
  1085.4 101.2 reduce-scatter.18
  1190.8 101.1 reduce-scatter.16
  1294.9 147.5 all-reduce.19
where the time goes:
time: 1460 us
  waiting for transfers between devices  1060 us (73%)
  blocking collectives  188 us (13%)
  matrix products  141 us (10%)
  local copies, waits for them, and re-layouts  28.1 us (2%)
  other arithmetic  24.5 us (2%)
  between operations  17.3 us (1%)
    reduce_scatter x2, waiting for transfers between devices, reduce_grads(): lax.psum_scatter(layer_grads[6].astype(jnp.bfloat16), 'shard', scatter_di...  211 us
    reduce_scatter x2, waiting for transfers between devices, reduce_grads(): lax.psum_scatter(layer_grads[4].astype(jnp.bfloat16), 'shard', scatter_di...  211 us
    reduce_scatter x2, waiting for transfers between devices, reduce_grads(): lax.psum_scatter(layer_grads[2].astype(jnp.bfloat16), 'shard', scatter_di...  169 us
    all_gather x2, waiting for transfers between devices, fetch_forward(): lax.all_gather(w_fc[depth_index], 'shard', axis=0, tiled=True)  134 us
    unnamed x2, blocking collectives  121 us
    psum x1, waiting for transfers between devices, reduce_grads(): lax.psum(partial_sums[2].astype(jnp.bfloat16), 'rep').astype(jnp.float32)  119 us
    all_gather x2, waiting for transfers between devices, fetch_forward(): lax.all_gather(w_in[depth_index], 'shard', axis=0, tiled=True)  108 us
    all_gather x2, waiting for transfers between devices, fetch_forward(): lax.all_gather(w_qkv[depth_index], 'shard', axis=0, tiled=True)  59.5 us
  transfers between devices with their start and end apart: 17, of which 13 were waited for; matrix products, arithmetic and copies ran while one was open for 12% of the time, Pallas kernels for 0%

commit v1 on v0

v1 whole, which is shorter than its diff:
```python
import functools
import math

import jax
import jax.numpy as jnp
from jax import lax
from jax.experimental import pallas as pl
from jax.experimental.pallas import tpu as pltpu
from jax.sharding import Mesh
from jax.sharding import PartitionSpec as P

D = 1024
HEADS = 16
HEAD = 64
ROT = 32
FF = 4096
LAYERS = 2
SLOTS = 4
CAP = 192
LINE = 8
QKV = 384
HID = 512
WIDE = QKV + HID
DEEP = 128 + HID
EPSILON = 1e-05
NEGATIVE = -1e30
AXES = ("y", "xl", "z", "xh", "c")
BF = jnp.bfloat16
F32 = jnp.float32
MESH = pl.DeviceIdType.MESH
VMEM = pltpu.VMEM
DMA = pltpu.SemaphoreType.DMA
ANY = pl.BlockSpec(memory_space=pl.ANY)
INV = pl.BlockSpec(memory_space=pltpu.VMEM)
C0 = 0.7978845608028654
C1 = 0.044715


def div(a, b):
    return lax.div(a, jnp.int32(b))


def rem(a, b):
    return lax.rem(a, jnp.int32(b))


def place():
    y, xl, z, xh, c = (lax.axis_index(a) for a in AXES)
    return y, xl, z, xh, c


def send(src, dst, ss, rs, **dev):
    cp = pltpu.make_async_remote_copy(
        src_ref=src, dst_ref=dst, send_sem=ss, recv_sem=rs, device_id=dev, device_id_type=MESH
    )
    cp.start()


def local(src, dst, sem):
    pltpu.make_async_copy(src, dst, sem).start()


def landed(ref, sem):
    pltpu.make_async_copy(ref, ref, sem).wait()


def loop(n, body):
    lax.fori_loop(0, n, lambda i, _: (body(i), 0)[1], 0)


def signal(sem, **dev):
    pl.semaphore_signal(sem, inc=1, device_id=dev, device_id_type=MESH)


def greet_line(bar, z, c):
    for k in range(1, LINE):
        j = rem(2 * z + c + k, LINE)
        signal(bar, z=div(j, 2), c=rem(j, 2))


def greet_plane(bar, y, x):
    for k in range(1, 16):
        yy = rem(y + k // 4, 4)
        xx = rem(x + k % 4, 4)
        signal(bar, y=yy, xh=div(xx, 2), xl=rem(xx, 2))


def gather_kernel(
    wqkv, win, wo, wfc, sm, tab, w1, w2, sma, tabs,
    cs, cr, as_, ar, bs, br, ts, tr,
):
    y, xl, z, xh, c = place()
    x = 2 * xh + xl
    p = 4 * y + x
    j = 2 * z + c
    bar = pltpu.get_barrier_semaphore()
    greet_line(bar, z, c)
    greet_plane(bar, y, x)
    signal(bar, xl=1 - xl, xh=1 - xh, c=1 - c)
    pl.semaphore_wait(bar, 23)

    mine = pl.ds(pl.multiple_of(64 * p, 64), 64)
    for l in range(LAYERS):
        @pl.when((z == y) & (c == xl))
        def _():
            def to(jj):
                pairs = []
                for part in range(3):
                    cols = pl.ds(pl.multiple_of(part * D + jj * 128, 128), 128)
                    pairs.append((wqkv.at[l, :, cols], w1.at[l, mine, pl.ds(part * 128, 128)]))
                cols = pl.ds(pl.multiple_of(jj * HID, HID), HID)
                pairs.append((win.at[l, :, cols], w1.at[l, mine, pl.ds(QKV, HID)]))
                if l == 0:
                    pairs.append((sm, sma.at[p]))

                @pl.when(jj == j)
                def _():
                    for i, (src, dst) in enumerate(pairs):
                        local(src, dst, ar.at[l, i])

                @pl.when(jj != j)
                def _():
                    for i, (src, dst) in enumerate(pairs):
                        send(src, dst, as_.at[jj, l, i], ar.at[l, i], z=div(jj, 2), c=rem(jj, 2))

            loop(LINE, to)

        pieces = (
            (wo.at[l], w2.at[l, pl.ds(pl.multiple_of(64 * c, 64), 64)]),
            (wfc.at[l], w2.at[l, pl.ds(pl.multiple_of(128 + 256 * c, 64), 256)]),
        )
        for i, (src, dst) in enumerate(pieces):
            send(src, dst, cs.at[l, 0, i], cr.at[l, c, i], xl=1 - xl, xh=1 - xh, c=xh)

            @pl.when(c == xh)
            def _():
                local(src, dst, cr.at[l, c, i])

            @pl.when(c != xh)
            def _():
                send(src, dst, cs.at[l, 1, i], cr.at[l, c, i], c=xh)

    for k in range(1, LINE):
        jj = rem(j + k, LINE)
        send(tab, tabs.at[j], ts.at[k], tr.at[j], z=div(jj, 2), c=rem(jj, 2))
    local(tab, tabs.at[j], tr.at[j])

    for l in range(LAYERS):
        for part in range(3):
            landed(w1.at[l, mine, pl.ds(part * 128, 128)], ar.at[l, part])
        landed(w1.at[l, mine, pl.ds(QKV, HID)], ar.at[l, 3])
        if l == 0:
            landed(sma.at[p], ar.at[l, 4])

        def across(k):
            yy = rem(y + div(k, 4), 4)
            xx = rem(x + rem(k, 4), 4)
            dev = dict(y=yy, xh=div(xx, 2), xl=rem(xx, 2))
            send(w1.at[l, mine], w1.at[l, mine], bs.at[l, k, 0], br.at[l, p, 0], **dev)
            if l == 0:
                send(sma.at[p], sma.at[p], bs.at[l, k, 1], br.at[l, p, 1], **dev)

        loop(15, lambda k: across(k + 1))

    def arrive(l, k):
        q = rem(p + k, 16)
        rows = pl.ds(pl.multiple_of(64 * q, 64), 64)
        landed(w1.at[l, rows], br.at[l, q, 0])
        if l == 0:
            landed(sma.at[q], br.at[l, q, 1])

    for l in range(LAYERS):
        loop(15, lambda k: arrive(l, k + 1))
        for s in range(2):
            landed(w2.at[l, pl.ds(64 * s, 64)], cr.at[l, s, 0])
            landed(w2.at[l, pl.ds(128 + 256 * s, 256)], cr.at[l, s, 1])
    loop(LINE, lambda k: landed(tabs.at[k], tr.at[k]))

    for l in range(LAYERS):

        def left(k):
            landed(w1.at[l, mine], bs.at[l, k, 0])
            if l == 0:
                landed(sma.at[p], bs.at[l, k, 1])

        loop(15, lambda k: left(k + 1))
        landed(wo.at[l], cs.at[l, 0, 0])
        landed(wfc.at[l], cs.at[l, 0, 1])

        @pl.when(c != xh)
        def _():
            landed(wo.at[l], cs.at[l, 1, 0])
            landed(wfc.at[l], cs.at[l, 1, 1])

        @pl.when((z == y) & (c == xl))
        def _():
            def gone(jj):
                @pl.when(jj != j)
                def _():
                    for part in range(3):
                        landed(wqkv.at[l, :, pl.ds(part * D, 128)], as_.at[jj, l, part])
                    landed(win.at[l, :, pl.ds(0, HID)], as_.at[jj, l, 3])
                    if l == 0:
                        landed(sm, as_.at[jj, l, 4])

            loop(LINE, gone)

    for k in range(1, LINE):
        landed(tab, ts.at[k])


def gather_weights(wqkv, win, wo, wfc, sm, tab):
    return pl.pallas_call(
        gather_kernel,
        out_shape=(
            jax.ShapeDtypeStruct((LAYERS, D, WIDE), BF),
            jax.ShapeDtypeStruct((LAYERS, DEEP, D), BF),
            jax.ShapeDtypeStruct((16, 16, 256), BF),
            jax.ShapeDtypeStruct((LINE, CAP, 128), F32),
        ),
        in_specs=[ANY] * 6,
        out_specs=(ANY,) * 4,
        scratch_shapes=[
            DMA((LAYERS, 2, 2)), DMA((LAYERS, 2, 2)),
            DMA((LINE, LAYERS, 5)), DMA((LAYERS, 5)),
            DMA((LAYERS, 16, 2)), DMA((LAYERS, 16, 2)),
            DMA((LINE,)), DMA((LINE,)),
        ],
        compiler_params=pltpu.CompilerParams(collective_id=0, has_side_effects=True),
        name="gather_weights",
    )(wqkv, win, wo, wfc, sm, tab)


def slot_of(z, c, k):
    return 2 * rem(z + k, 4) + c


def rows_start(buf, z, c, ss, rs):
    own = buf.at[2 * z + c]
    send(own, own, ss.at[0], rs.at[0], c=1 - c)
    send(own, own, ss.at[1], rs.at[1], z=rem(z + 1, 4))
    send(own, own, ss.at[2], rs.at[2], z=rem(z + 3, 4))


def rows_near(buf, z, c, ss, rs):
    lo, hi = slot_of(z, c, 3), slot_of(z, c, 1)
    landed(buf.at[lo], rs.at[1])
    a = buf.at[lo, pl.ds(0, CAP // 2)]
    send(a, a, ss.at[3], rs.at[3], z=rem(z + 1, 4))
    send(buf.at[lo], buf.at[lo], ss.at[5], rs.at[5], c=1 - c)
    landed(buf.at[hi], rs.at[2])
    b = buf.at[hi, pl.ds(CAP // 2, CAP // 2)]
    send(b, b, ss.at[4], rs.at[4], z=rem(z + 3, 4))
    send(buf.at[hi], buf.at[hi], ss.at[6], rs.at[6], c=1 - c)


def rows_far(buf, z, c, ss, rs):
    far = slot_of(z, c, 2)
    landed(buf.at[far, pl.ds(0, CAP // 2)], rs.at[3])
    landed(buf.at[far, pl.ds(CAP // 2, CAP // 2)], rs.at[4])
    send(buf.at[far], buf.at[far], ss.at[7], rs.at[7], c=1 - c)


def rows_ready(k, buf, z, c, ss, rs):
    @pl.when(k == 0)
    def _():
        landed(buf.at[2 * z + 1 - c], rs.at[0])

    @pl.when(k == 1)
    def _():
        rows_near(buf, z, c, ss, rs)
        landed(buf.at[slot_of(z, 1 - c, 3)], rs.at[5])

    @pl.when(k == 2)
    def _():
        rows_far(buf, z, c, ss, rs)
        landed(buf.at[slot_of(z, 1 - c, 1)], rs.at[6])

    @pl.when(k == 3)
    def _():
        landed(buf.at[slot_of(z, 1 - c, 2)], rs.at[7])


def rows_left(buf, z, c, ss):
    for i in (0, 1, 2):
        landed(buf.at[2 * z + c], ss.at[i])
    landed(buf.at[0, pl.ds(0, CAP // 2)], ss.at[3])
    landed(buf.at[0, pl.ds(0, CAP // 2)], ss.at[4])
    for i in (5, 6, 7):
        landed(buf.at[0], ss.at[i])


def chip_of(z, k):
    return rem(z + jnp.where(k == 1, 3, jnp.where(k == 0, 0, k - 1)), 4)


def sums_send(k, zz, partial, c, own, sibout, sibin, out, inn, sbs, sbr, rss, rsr):
    sibout[k] = partial(2 * zz + 1 - c).astype(BF)
    send(sibout.at[k], sibin.at[k], sbs.at[k], sbr.at[k], c=1 - c)
    term = partial(2 * zz + c)
    landed(sibin.at[k], sbr.at[k])
    term = term + sibin[k].astype(F32)

    @pl.when(k == 0)
    def _():
        own[...] = term

    @pl.when(k > 0)
    def _():
        out[k - 1] = term.astype(BF)
        send(out.at[k - 1], inn.at[k - 1], rss.at[k - 1], rsr.at[k - 1], z=zz)


def sums_total(own, inn, rsr):
    total = own[...]
    for i in range(3):
        landed(inn.at[i], rsr.at[i])
        total = total + inn[i].astype(F32)
    return total


def sums_left(sibout, out, sbs, rss):
    for i in range(4):
        landed(sibout.at[i], sbs.at[i])
    for i in range(3):
        landed(out.at[i], rss.at[i])


ROW_SEMS = [DMA((8,)), DMA((8,)), DMA((4,)), DMA((4,)), DMA((3,)), DMA((3,))]
SUM_BUFFERS = [
    VMEM((CAP, D), F32),
    VMEM((4, CAP, D), BF),
    VMEM((4, CAP, D), BF),
    VMEM((3, CAP, D), BF),
    VMEM((3, CAP, D), BF),
]


def lanes(shape):
    return lax.broadcasted_iota(jnp.int32, shape, len(shape) - 1)


def turn(v, cos, sin):
    low = rem(lanes(v.shape), 64) < 16
    partner = jnp.where(low, pltpu.roll(v, 112, 1), pltpu.roll(v, 16, 1))
    return v * cos + partner * sin


def nt(a, b):
    return lax.dot_general(a, b, (((1,), (1,)), ((), ())), preferred_element_type=F32)


def tn(a, b):
    return lax.dot_general(a, b, (((0,), (0,)), ((), ())), preferred_element_type=F32)


def nn(a, b):
    return jnp.dot(a, b, preferred_element_type=F32)


def stats(x):
    centre = x - jnp.mean(x, axis=-1, keepdims=True)
    r = lax.rsqrt(jnp.mean(centre * centre, axis=-1, keepdims=True) + EPSILON)
    return centre, r


def forward_kernel(
    x_ref, ln_ref, bin_ref, w1, w2, tab,
    xn_ref, nall_o, qkv_o, p_o, a2_o, pre_o,
    nall, qkv, prob, a2, pre, raw,
    own, sibout, sibin, out, inn,
    ss, rs, sbs, sbr, rss, rsr, save,
):
    y, xl, z, xh, c = place()
    bar = pltpu.get_barrier_semaphore()
    greet_line(bar, z, c)
    centre, r = stats(x_ref[...])
    nall[2 * z + c] = (centre * r * ln_ref[0:1, :] + ln_ref[1:2, :]).astype(BF)
    pl.semaphore_wait(bar, LINE - 1)
    rows_start(nall, z, c, ss, rs)
    pairs = ((nall, nall_o), (qkv, qkv_o), (prob, p_o), (a2, a2_o), (pre, pre_o))

    def step(k):
        zz = chip_of(z, k)
        rows_ready(k, nall, z, c, ss, rs)
        two = pl.ds(2 * zz, 2)
        n = nall[two].reshape(2 * CAP, D)
        raw[...] = nn(n, w1[:, :QKV])
        pre[two] = (nn(n, w1[:, QKV:]) + bin_ref[0:1, :]).reshape(2, CAP, HID)

        def act(i):
            u, t = div(i, 6), rem(i, 6)
            rows = pl.ds(pl.multiple_of(t * 32, 32), 32)
            v = pre[2 * zz + u, rows, :]
            g = 0.5 * v * (1.0 + jnp.tanh(C0 * (v + C1 * v * v * v)))
            a2[2 * zz + u, rows, 128:] = g.astype(BF)

        loop(12, act)
        for u in range(2):
            s = 2 * zz + u
            rows = slice(u * CAP, (u + 1) * CAP)
            cos, sin = tab[s, :, 0:128], tab[s, :, 128:256]
            start = tab[s, :, 256:257]
            q = turn(raw[rows, 0:128], cos, sin).astype(BF)
            kk = turn(raw[rows, 128:256], cos, sin).astype(BF)
            v = raw[rows, 256:384].astype(BF)
            qkv[s, :, 0:128] = q
            qkv[s, :, 128:256] = kk
            qkv[s, :, 256:384] = v
            q = q * jnp.asarray(1.0 / math.sqrt(HEAD), BF)
            key_at = lanes((CAP, CAP))
            query_at = lax.broadcasted_iota(jnp.int32, (CAP, CAP), 0)
            allowed = (key_at >= start.astype(jnp.int32)) & (key_at <= query_at)
            head = lanes((CAP, 128)) < HEAD
            mixed = []
            for h in range(2):
                qh = jnp.where(head if h == 0 else ~head, q, jnp.zeros_like(q))
                score = jnp.where(allowed, nt(qh, kk), NEGATIVE)
                e = jnp.exp(score - jnp.max(score, axis=-1, keepdims=True))
                w = e / jnp.sum(e, axis=-1, keepdims=True)
                prob[2 * s + h] = w
                mixed.append(nn(w.astype(BF), v))
            a2[s, :, 0:128] = jnp.where(head, mixed[0], mixed[1]).astype(BF)

        for i, (src, dst) in enumerate(pairs):
            part = pl.ds(4 * zz, 4) if i == 2 else two
            local(src.at[part], dst.at[part], save.at[k, i])
        sums_send(
            k, zz, lambda s: nn(a2[s], w2[...]), c, own, sibout, sibin, out, inn, sbs, sbr, rss, rsr
        )

    loop(4, step)
    xn_ref[...] = x_ref[...] + (sums_total(own, inn, rsr) + ln_ref[2:3, :])
    for k in range(4):
        for i, (src, dst) in enumerate(pairs):
            part = pl.ds(0, 4) if i == 2 else pl.ds(0, 2)
            landed(src.at[part], save.at[k, i])
    rows_left(nall, z, c, ss)
    sums_left(sibout, out, sbs, rss)


SAVED = (
    ((LINE, CAP, D), BF),
    ((LINE, CAP, QKV), BF),
    ((2 * LINE, CAP, CAP), F32),
    ((LINE, CAP, DEEP), BF),
    ((LINE, CAP, HID), F32),
)


def forward_layer(l, x, ln, b_in, w1, w2, tab):
    return pl.pallas_call(
        forward_kernel,
        out_shape=(jax.ShapeDtypeStruct((CAP, D), F32),)
        + tuple(jax.ShapeDtypeStruct(s, t) for s, t in SAVED),
        in_specs=[INV] * 6,
        out_specs=(INV,) + (ANY,) * 5,
        scratch_shapes=[VMEM(s, t) for s, t in SAVED]
        + [VMEM((2 * CAP, QKV), F32)]
        + SUM_BUFFERS
        + ROW_SEMS
        + [DMA((4, 5))],
        compiler_params=pltpu.CompilerParams(
            collective_id=1 + l, has_side_effects=True, vmem_limit_bytes=56 * 2**20
        ),
        name=f"forward_{l}",
    )(x, ln, b_in, w1, w2, tab)


def backward_kernel(
    g_ref, x_ref, ln_ref, w1, w2, tab, nall_i, qkv_i, p_i, a2_i, pre_i,
    gn_ref, g1q, g1i, g2, lns, loc,
    gall, nall, qkv, prob, a2, pre, raw, dp,
    own, sibout, sibin, out, inn,
    ss, rs, sbs, sbr, rss, rsr, load,
):
    y, xl, z, xh, c = place()
    bar = pltpu.get_barrier_semaphore()
    greet_line(bar, z, c)
    pairs = ((nall_i, nall), (qkv_i, qkv), (p_i, prob), (a2_i, a2), (pre_i, pre))
    for i, (src, dst) in enumerate(pairs):
        local(src, dst, load.at[i])
    gall[2 * z + c] = g_ref[...].astype(BF)
    pl.semaphore_wait(bar, LINE - 1)
    rows_start(gall, z, c, ss, rs)
    for i in (1, 2, 4):
        landed(pairs[i][1], load.at[i])

    def step(k):
        zz = chip_of(z, k)
        rows_ready(k, gall, z, c, ss, rs)
        two = pl.ds(2 * zz, 2)
        g = gall[two].reshape(2 * CAP, D)
        raw[...] = nt(g, w2[...])

        def act(i):
            u, t = div(i, 12), rem(i, 12)
            rows = pl.ds(pl.multiple_of(t * 16, 16), 16)
            v = pre[2 * zz + u, rows, :]
            d = raw[pl.ds(pl.multiple_of(u * CAP + t * 16, 16), 16), 128:]
            t1 = jnp.tanh(C0 * (v + C1 * v * v * v))
            slope = 0.5 * (1.0 + t1) + 0.5 * v * (1.0 - t1 * t1) * (C0 + (3.0 * C0 * C1) * v * v)
            dp[2 * zz + u, rows, QKV:] = (d * slope).astype(BF)

        loop(24, act)
        for u in range(2):
            s = 2 * zz + u
            rows = slice(u * CAP, (u + 1) * CAP)
            cos, sin = tab[s, :, 0:128], tab[s, :, 128:256]
            m = raw[rows, 0:128].astype(BF)
            q, kk, v = qkv[s, :, 0:128], qkv[s, :, 128:256], qkv[s, :, 256:384]
            head = lanes((CAP, 128)) < HEAD
            dq, dk, dv = [], [], []
            for h in range(2):
                mine = head if h == 0 else ~head
                mh = jnp.where(mine, m, jnp.zeros_like(m))
                w = prob[2 * s + h]
                soft = nt(mh, v)
                dv.append(tn(w.astype(BF), mh))
                wd = w * soft
                ds = (wd - w * jnp.sum(wd, axis=-1, keepdims=True)).astype(BF)
                dq.append(nn(ds, kk))
                dk.append(tn(ds, jnp.where(mine, q, jnp.zeros_like(q))))
            scale = 1.0 / math.sqrt(HEAD)
            dq = jnp.where(head, dq[0], dq[1]) * scale
            dk = (dk[0] + dk[1]) * scale
            dp[s, :, 0:128] = turn(dq, cos, -sin).astype(BF)
            dp[s, :, 128:256] = turn(dk, cos, -sin).astype(BF)
            dp[s, :, 256:384] = (dv[0] + dv[1]).astype(BF)
        sums_send(
            k, zz, lambda s: nt(dp[s], w1[...]), c, own, sibout, sibin, out, inn, sbs, sbr, rss, rsr
        )

    loop(4, step)

    rows = LINE * CAP
    g = gall[...].reshape(rows, D)
    landed(a2, load.at[3])
    val = tn(a2[...].reshape(rows, DEEP), g)
    for s in range(2):
        for q in range(4):
            g2[s, q, 0:16, :] = val[64 * s + 16 * q : 64 * s + 16 * q + 16].astype(BF)
            base = 128 + 256 * s + 64 * q
            g2[s, q, 16:80, :] = val[base : base + 64].astype(BF)
    landed(nall, load.at[0])
    d = dp[...].reshape(rows, WIDE)
    for t in range(2):
        val = tn(nall[:, :, t * 512 : (t + 1) * 512].reshape(rows, 512), d).astype(BF)
        for s in range(8):
            sh = 8 * t + s
            zz, hh, cc = sh // 4, (sh // 2) % 2, sh % 2
            for q in range(4):
                part = val[64 * s + 16 * q : 64 * s + 16 * q + 16]
                at = (2 * zz + cc) * 16
                g1q[hh, q, at : at + 16, :] = part[:, :QKV]
                g1i[hh, q, at : at + 16, :] = part[:, QKV:]

    zero = jnp.zeros((1, 128), F32)
    col = pl.ds(pl.multiple_of((2 * z + c) * 128, 128), 128)
    bfc = jnp.zeros((1, 128), F32)
    b_in = jnp.zeros((1, HID), F32)
    for s in range(LINE):
        bfc = bfc + jnp.sum(gall[s, :, col].astype(F32), axis=0, keepdims=True)
        b_in = b_in + jnp.sum(dp[s, :, QKV:].astype(F32), axis=0, keepdims=True)
    loc[...] = jnp.concatenate(
        [zero, zero, bfc] + [b_in[:, 128 * i : 128 * i + 128] for i in range(4)] + [zero], axis=0
    )

    ngrad = sums_total(own, inn, rsr)
    centre, r = stats(x_ref[...])
    xhat = centre * r
    e = ngrad * ln_ref[0:1, :]
    ex = jnp.mean(e * xhat, axis=-1, keepdims=True)
    gn_ref[...] = g_ref[...] + r * (e - jnp.mean(e, axis=-1, keepdims=True) - xhat * ex)
    gain = jnp.sum(ngrad * xhat, axis=0, keepdims=True)
    bias = jnp.sum(ngrad, axis=0, keepdims=True)
    both = jnp.concatenate([gain, bias] + [jnp.zeros((6, D), F32)], axis=0)
    for i in range(LINE):
        lns[i] = both[:, 128 * i : 128 * i + 128]
    rows_left(gall, z, c, ss)
    sums_left(sibout, out, sbs, rss)


def backward_layer(l, g, x, ln, w1, w2, tab, saved):
    return pl.pallas_call(
        backward_kernel,
        out_shape=(
            jax.ShapeDtypeStruct((CAP, D), F32),
            jax.ShapeDtypeStruct((2, 4, 128, QKV), BF),
            jax.ShapeDtypeStruct((2, 4, 128, HID), BF),
            jax.ShapeDtypeStruct((2, 4, 80, D), BF),
            jax.ShapeDtypeStruct((LINE, 8, 128), F32),
            jax.ShapeDtypeStruct((8, 128), F32),
        ),
        in_specs=[INV] * 6 + [ANY] * 5,
        out_specs=(INV,) * 6,
        scratch_shapes=[VMEM((LINE, CAP, D), BF)]
        + [VMEM(s, t) for s, t in SAVED]
        + [VMEM((2 * CAP, DEEP), F32), VMEM((LINE, CAP, WIDE), BF)]
        + SUM_BUFFERS
        + ROW_SEMS
        + [DMA((5,))],
        compiler_params=pltpu.CompilerParams(
            collective_id=3 + l, has_side_effects=True, vmem_limit_bytes=60 * 2**20
        ),
        name=f"backward_{l}",
    )(g, x, ln, w1, w2, tab, *saved)


def reduce_kernel(
    g1q0, g1q1, g1i0, g1i1, g20, g21, lns0, lns1, loc0, loc1,
    fq, fi, fo, ff, fs,
    r1, r2, red1, red2, zs, ps, tot,
    s1, q1, s2, q2, s3, q3, s4, q4, s5, q5, s6, q6, s7, q7, s8, q8,
):
    y, xl, z, xh, c = place()
    x = 2 * xh + xl
    p = 4 * y + x
    j = 2 * z + c
    bar = pltpu.get_barrier_semaphore()
    greet_line(bar, z, c)
    greet_plane(bar, y, x)
    for k in range(1, 8):
        signal(bar, y=rem(y + k // 2, 4), xl=rem(xl + k % 2, 2), c=1 - c)
    pl.semaphore_wait(bar, 29)
    g1q, g1i, g2, lns, loc = (g1q0, g1q1), (g1i0, g1i1), (g20, g21), (lns0, lns1), (loc0, loc1)
    order = (1, 0)

    def member(jj):
        return dict(z=div(jj, 2), c=rem(jj, 2))

    for l in order:

        def small(k):
            jj = rem(j + k, LINE)
            send(lns[l].at[jj], zs.at[l, j], s5.at[l, k], q5.at[l, j], **member(jj))

        loop(LINE - 1, lambda k: small(k + 1))

    for l in order:

        def second(i):
            yy, cc = rem(y + div(i, 2), 4), rem(xl + rem(i, 2), 2)
            src, dst = g2[l].at[cc, yy], r2.at[l, p]
            here = (i == 0) & (xh == c)

            @pl.when(here)
            def _():
                local(src, dst, q2.at[l, p])

            @pl.when(jnp.logical_not(here))
            def _():
                send(src, dst, s2.at[l, i], q2.at[l, p], y=yy, xl=cc, xh=c)

        loop(8, second)

        def first(k):
            yy = rem(y + div(k, 4), 4)
            xx = rem(x + rem(k, 4), 4)
            hh, ll = div(xx, 2), rem(xx, 2)

            @pl.when(ll == 0)
            def _():
                dst = r1.at[l, p, :, pl.ds(0, QKV)]
                send(g1q[l].at[hh, yy], dst, s1.at[l, k], q1.at[l, p], y=yy, xh=hh, xl=ll)

            @pl.when(ll == 1)
            def _():
                send(g1i[l].at[hh, yy], r1.at[l, p], s1.at[l, k], q1.at[l, p], y=yy, xh=hh, xl=ll)

        loop(15, lambda k: first(k + 1))

        @pl.when(xl == 0)
        def _():
            local(g1q[l].at[xh, y], r1.at[l, p, :, pl.ds(0, QKV)], q1.at[l, p])

        @pl.when(xl == 1)
        def _():
            local(g1i[l].at[xh, y], r1.at[l, p], q1.at[l, p])

    for l in order:

        def small_in(k):
            jj = rem(j + k, LINE)
            landed(zs.at[l, jj], q5.at[l, jj])

        zs[l, j] = lns[l][j] + loc[l][...]
        loop(LINE - 1, lambda k: small_in(k + 1))
        total = zs[l, 0]
        for i in range(1, LINE):
            total = total + zs[l, i]
        ps[l, p] = total

        def spread(k):
            yy = rem(y + div(k, 4), 4)
            xx = rem(x + rem(k, 4), 4)
            dev = dict(y=yy, xh=div(xx, 2), xl=rem(xx, 2))
            send(ps.at[l, p], ps.at[l, p], s6.at[l, k], q6.at[l, p], **dev)

        loop(15, lambda k: spread(k + 1))

    row16 = pl.ds(pl.multiple_of(16 * y, 16), 16)
    row64 = pl.ds(pl.multiple_of(64 * y, 64), 64)
    for l in order:
        @pl.when(xh == c)
        def _():
            loop(16, lambda q: landed(r2.at[l, q], q2.at[l, q]))
            for t in range(5):
                rows = slice(16 * t, 16 * t + 16)
                acc = r2[l, 0, rows, :].astype(F32)
                for q in range(1, 16):
                    acc = acc + r2[l, q, rows, :].astype(F32)
                red2[l, rows, :] = acc.astype(BF)

            def out(i):
                yy, ll = rem(y + div(i, 2), 4), rem(xl + rem(i, 2), 2)
                here = (i == 0) & (xl == c)
                parts = (
                    (red2.at[l, pl.ds(0, 16)], fo.at[l, row16]),
                    (red2.at[l, pl.ds(16, 64)], ff.at[l, row64]),
                )
                for n, (src, dst) in enumerate(parts):

                    @pl.when(here)
                    def _():
                        local(src, dst, q4.at[l, y, n])

                    @pl.when(jnp.logical_not(here))
                    def _():
                        send(src, dst, s4.at[l, i, n], q4.at[l, y, n], y=yy, xl=ll, c=xl)

            loop(8, out)

        loop_in = functools.partial(arrive_first, l, xl, r1, q1)
        loop(16, loop_in)
        for t in range(8):
            rows = slice(16 * t, 16 * t + 16)
            acc = r1[l, 0, rows, :].astype(F32)
            for q in range(1, 16):
                acc = acc + r1[l, q, rows, :].astype(F32)
            red1[l, rows, :] = acc.astype(BF)

        def back(jj):
            rows = pl.ds(pl.multiple_of(16 * jj, 16), 16)
            cols = pl.ds(pl.multiple_of(HID * j, HID), HID)

            def move(src, dst, n):
                @pl.when(jj == j)
                def _():
                    local(src, dst, q3.at[l, j, n])

                @pl.when(jj != j)
                def _():
                    send(src, dst, s3.at[l, jj, n], q3.at[l, j, n], **member(jj))

            @pl.when(xl == 0)
            def _():
                for n in range(3):
                    at = pl.ds(pl.multiple_of(n * D + 128 * j, 128), 128)
                    move(red1.at[l, rows, pl.ds(128 * n, 128)], fq.at[l, row16, at], n)

            @pl.when(xl == 1)
            def _():
                move(red1.at[l, rows], fi.at[l, row16, cols], 0)

        loop(LINE, back)

    for l in order:

        def back_in(jj):
            @pl.when(xl == 0)
            def _():
                for n in range(3):
                    at = pl.ds(pl.multiple_of(n * D + 128 * jj, 128), 128)
                    landed(fq.at[l, row16, at], q3.at[l, jj, n])

            @pl.when(xl == 1)
            def _():
                at = pl.ds(pl.multiple_of(HID * jj, HID), HID)
                landed(fi.at[l, row16, at], q3.at[l, jj, 0])

        loop(LINE, back_in)

        def share(i):
            yy, ll = rem(y + div(i, 2), 4), rem(xl + rem(i, 2), 2)
            for v, f in ((0, fq), (1, fi)):

                @pl.when(xl == v)
                def _():
                    at = f.at[l, row16]
                    send(at, at, s7.at[l, i], q7.at[l, y, v], y=yy, xl=ll)

        loop(7, lambda i: share(i + 1))

    for l in order:

        def spread_in(k):
            q = rem(p + k, 16)
            landed(ps.at[l, q], q6.at[l, q])

        loop(15, lambda k: spread_in(k + 1))
        total = ps[l, 0]
        for i in range(1, 16):
            total = total + ps[l, i]
        tot[l, c] = total
        send(tot.at[l, c], tot.at[l, c], s8.at[l], q8.at[l], c=1 - c)
    for l in order:
        landed(tot.at[l, 1 - c], q8.at[l])
    fs[...] = tot[...]

    for l in order:
        for q in range(4):
            landed(fo.at[l, pl.ds(16 * q, 16)], q4.at[l, q, 0])
            landed(ff.at[l, pl.ds(64 * q, 64)], q4.at[l, q, 1])
            for v, f in ((0, fq), (1, fi)):

                @pl.when((xl != v) | (y != q))
                def _():
                    landed(f.at[l, pl.ds(16 * q, 16)], q7.at[l, q, v])

    for l in order:

        def left_line(k):
            landed(lns[l].at[0], s5.at[l, k])

        loop(LINE - 1, lambda k: left_line(k + 1))

        def left_second(i):
            @pl.when(jnp.logical_not((i == 0) & (xh == c)))
            def _():
                landed(r2.at[l, 0], s2.at[l, i])

            @pl.when((xh == c) & jnp.logical_not((i == 0) & (xl == c)))
            def _():
                landed(red2.at[l, pl.ds(0, 16)], s4.at[l, i, 0])
                landed(red2.at[l, pl.ds(16, 64)], s4.at[l, i, 1])

        loop(8, left_second)

        def left_first(k):
            ll = rem(rem(x + rem(k, 4), 4), 2)

            @pl.when(ll == 0)
            def _():
                landed(r1.at[l, 0, :, pl.ds(0, QKV)], s1.at[l, k])

            @pl.when(ll == 1)
            def _():
                landed(r1.at[l, 0], s1.at[l, k])

            landed(ps.at[l, 0], s6.at[l, k])

        loop(15, lambda k: left_first(k + 1))

        def left_back(jj):
            @pl.when((jj != j) & (xl == 0))
            def _():
                for n in range(3):
                    landed(red1.at[l, pl.ds(0, 16), pl.ds(0, 128)], s3.at[l, jj, n])

            @pl.when((jj != j) & (xl == 1))
            def _():
                landed(red1.at[l, pl.ds(0, 16)], s3.at[l, jj, 0])

        loop(LINE, left_back)

        def left_share(i):
            for v, f in ((0, fq), (1, fi)):

                @pl.when(xl == v)
                def _():
                    landed(f.at[l, row16], s7.at[l, i])

        loop(7, lambda i: left_share(i + 1))
        landed(tot.at[l, c], s8.at[l])


def arrive_first(l, xl, r1, q1, q):
    @pl.when(xl == 0)
    def _():
        landed(r1.at[l, q, :, pl.ds(0, QKV)], q1.at[l, q])

    @pl.when(xl == 1)
    def _():
        landed(r1.at[l, q], q1.at[l, q])


def reduce_all(first, second):
    args = [a for pair in zip(first, second) for a in pair]
    n = LAYERS
    return pl.pallas_call(
        reduce_kernel,
        out_shape=(
            jax.ShapeDtypeStruct((n, 64, 3 * D), BF),
            jax.ShapeDtypeStruct((n, 64, FF), BF),
            jax.ShapeDtypeStruct((n, 64, D), BF),
            jax.ShapeDtypeStruct((n, 256, D), BF),
            jax.ShapeDtypeStruct((n, 2, 8, 128), F32),
        ),
        in_specs=[ANY] * 6 + [INV] * 4,
        out_specs=(ANY,) * 4 + (INV,),
        scratch_shapes=[
            VMEM((n, 16, 128, HID), BF), VMEM((n, 16, 80, D), BF),
            VMEM((n, 128, HID), BF), VMEM((n, 80, D), BF),
            VMEM((n, LINE, 8, 128), F32), VMEM((n, 16, 8, 128), F32), VMEM((n, 2, 8, 128), F32),
            DMA((n, 16)), DMA((n, 16)),
            DMA((n, 8)), DMA((n, 16)),
            DMA((n, LINE, 3)), DMA((n, LINE, 3)),
            DMA((n, 8, 2)), DMA((n, 4, 2)),
            DMA((n, LINE)), DMA((n, LINE)),
            DMA((n, 16)), DMA((n, 16)),
            DMA((n, 8)), DMA((n, 4, 2)),
            DMA((n,)), DMA((n,)),
        ],
        compiler_params=pltpu.CompilerParams(
            collective_id=5, has_side_effects=True, vmem_limit_bytes=40 * 2**20
        ),
        name="reduce_all",
    )(*args)


def per_device(
    inputs, cotangent, lengths, ln_gain, ln_bias, w_qkv, w_attn_out, w_in, b_in, w_fc, b_fc
):
    z, xh, c = (lax.axis_index(a) for a in ("z", "xh", "c"))
    j = 2 * z + c
    offsets = jnp.arange(CAP, dtype=jnp.int32)
    seq_ends = jnp.cumsum(lengths[0])
    passed = (offsets[:, None] >= seq_ends[None, :]).astype(jnp.int32)
    segment = jnp.sum(passed, axis=1)
    start = jnp.sum(passed * lengths[0][None, :], axis=1)
    position = offsets - start
    frequency = 10000.0 ** (-jnp.arange(ROT // 2, dtype=F32) * 2.0 / ROT)
    angles = position.astype(F32)[:, None] * frequency
    cosine, sine = jnp.cos(angles), jnp.sin(angles)
    tab = jnp.concatenate(
        [cosine, cosine, -sine, sine, jnp.broadcast_to(start.astype(F32)[:, None], (CAP, 64))],
        axis=1,
    )
    wide = [jnp.pad(v, ((0, 0), (0, 256 - v.shape[1]))) for v in (ln_gain, ln_bias, b_fc, b_in)]
    sm = jnp.pad(jnp.stack(wide, axis=1), ((0, 0), (0, 4), (0, 0))).reshape(16, 256)

    w1, w2, sma, tabs = gather_weights(w_qkv, w_in, w_attn_out, w_fc, sm, tab)

    sma = sma.astype(F32)
    vec = sma.reshape(16, LAYERS, 8, 256)[:, :, :3, :64].transpose(1, 2, 0, 3).reshape(LAYERS, 3, D)
    vec = jnp.pad(vec, ((0, 0), (0, 5), (0, 0)))
    bins = lax.dynamic_slice(sma.reshape(16, LAYERS, 8, 256)[:, :, 3, :], (2 * j, 0, 0), (2, LAYERS, 256))
    bins = jnp.broadcast_to(bins.transpose(1, 0, 2).reshape(LAYERS, 1, HID), (LAYERS, 8, HID))
    one = jnp.ones((LINE, CAP, 32), F32)
    nil = jnp.zeros((LINE, CAP, 32), F32)
    cs, sn = tabs[:, :, 0:32], tabs[:, :, 32:64]
    table = jnp.concatenate(
        [cs, one, cs, one, sn, nil, sn, nil, tabs[:, :, 64:], tabs[:, :, 64:]], axis=-1
    )

    hidden = inputs
    kept = []
    for l in range(LAYERS):
        nxt, *saved = forward_layer(l, hidden, vec[l], bins[l], w1[l], w2[l], table)
        kept.append((hidden, saved))
        hidden = nxt
    grad = cotangent * (segment < SLOTS).astype(F32)[:, None]
    found = [None] * LAYERS
    for l in reversed(range(LAYERS)):
        grad, *found[l] = backward_layer(
            l, grad, kept[l][0], vec[l], w1[l], w2[l], table, kept[l][1]
        )
    fq, fi, fo, ff, fs = reduce_all(found[0], found[1])
    mine = lax.dynamic_index_in_dim(fs, xh, 1, keepdims=False)
    pick = lax.dynamic_slice(mine[:, 0:3], (0, 0, 64 * c), (LAYERS, 3, 64))
    b_in_grad = lax.dynamic_slice(mine[:, 3:7].reshape(LAYERS, HID), (0, 256 * c), (LAYERS, 256))
    return (
        hidden,
        grad,
        pick[:, 0],
        pick[:, 1],
        fq.astype(F32),
        fo.astype(F32),
        fi.astype(F32),
        b_in_grad,
        ff.astype(F32),
        pick[:, 2],
    )


def solution(mesh):
    fine = Mesh(mesh.devices.reshape(4, 2, 4, 2, 2), AXES)
    rows = P(AXES, None)
    shard = ("z", "xh", "c")
    vector, matrix = P(None, shard), P(None, shard, None)
    in_specs = (
        rows, rows, rows, vector, vector, matrix, matrix, matrix, vector, matrix, vector,
    )
    out_specs = (
        rows, rows, vector, vector, matrix, matrix, matrix, vector, matrix, vector,
    )
    return jax.shard_map(
        per_device, mesh=fine, in_specs=in_specs, out_specs=out_specs, check_vma=False
    )
```

time: 1460 us -> 446 us (0.31)
  waiting for transfers between devices: 1060 us -> 0 us
  Pallas kernels: 0 us -> 397 us
  blocking collectives: 188 us -> 0 us
  matrix products: 141 us -> 0 us
  between operations: 17.3 us -> 0.91 us
    reduce_scatter x8 -> x0, waiting for transfers between devices: 591 us -> none  [the longest x2 211 us: reduce_grads(): lax.psum_scatter(layer_grads[6].astype(jnp.bfloat16), 'shard', scatter_di...]
    pallas_call x0 -> x6, Pallas kernels: none -> 397 us  [the longest x1 121 us: reduce_all(): pl.pallas_call(reduce_kernel, out_shape=(jax.ShapeDtypeStruct((n, 64, 3 *...]
    all_gather x8 -> x0, waiting for transfers between devices: 343 us -> none  [the longest x2 134 us: fetch_forward(): lax.all_gather(w_fc[depth_index], 'shard', axis=0, tiled=True)]
    dot_general x36 -> x0, matrix products: 141 us -> none  [the longest x8 43.9 us: back_product(): lax.dot_general(first_op, second_op, (((1,), (1,)), ((), ())), preferred_...]
    unnamed x2 -> x0, blocking collectives: 121 us -> none
    psum x1 -> x0, waiting for transfers between devices: 119 us -> none  [reduce_grads(): lax.psum(partial_sums[2].astype(jnp.bfloat16), 'rep').astype(jnp.float32)]
    all_gather x2 -> x0, blocking collectives: 47.9 us -> none  [fetch_forward(): lax.all_gather(b_in[depth_index], 'shard', axis=0, tiled=True)]
    psum x1 -> x0, blocking collectives: 19.6 us -> none  [reduce_grads(): lax.psum(partial_sums[0].astype(jnp.bfloat16), 'rep').astype(jnp.float32)]
  transfers between devices with their start and end apart: 17 -> 0, of which waited for: 13 -> 0; matrix products, arithmetic and copies ran while one was open for 12% -> 0% of each run, Pallas kernels for 0% -> 0%
where the time goes in v1:
time: 446 us; the launch traced here: 440 us
  Pallas kernels  397 us (89%)
  local copies, waits for them, and re-layouts  30.9 us (7%)
  other arithmetic  11 us (2%)
    pallas_call x1, Pallas kernels, reduce_all(): pl.pallas_call(reduce_kernel, out_shape=(jax.ShapeDtypeStruct((n, 64, 3 *...  121 us
    pallas_call x2, Pallas kernels, backward_layer(): pl.pallas_call(backward_kernel, out_shape=(jax.ShapeDtypeStruct((CAP, D),...  104 us
    pallas_call x2, Pallas kernels, forward_layer(): pl.pallas_call(forward_kernel, out_shape=(jax.ShapeDtypeStruct((CAP, D),...  91.7 us
    pallas_call x1, Pallas kernels, gather_weights(): pl.pallas_call(gather_kernel, out_shape=(jax.ShapeDtypeStruct((LAYERS, D,...  80.5 us
    unnamed x43, local copies, waits for them, and re-layouts  10.9 us

profile of v1, /device:TPU:32, one launch (start us, length us, event | category | flops | bytes accessed | tf_op | source)
XLA Modules:
  0.0 439.8 jit_solution(3103505813549631023)
XLA Ops:
  0.6 0.7 pad_bitcast_fusion.1
  2.0 0.7 pad_maximum_fusion
  3.3 0.8 reduce-window.8
  4.1 0.7 convert_reduce_fusion
  5.4 0.8 concatenate.6.tab
  6.2 80.5 %gather_weights.1 = (bf16[2,1024,896]{2,1,0:T(8,128)(2,1)}, bf16[2,640,1024]{2,1,0:T(8,128)(2,1)}, bf16[16,16,256]{2,1,0:T(8,128)(2,1)}, f32[8,192,128]{2,1,0:T(8,128)}) custom-call(bf16[2,64,3072]{2,1,0:T(8,128)(2,1)} %wqkv.1, bf16[2,64,4096]{2,1,0:T(8,128)(2,1)} %win.1, bf16[2,64,1024]{2,1,0:T(8,128)(2,1)} %wo.1, bf16[2,256,1024]{2,1,0:T(8,128)(2,1)} %wfc.1, ...), custom_call_target="tpu_custom_call" | custom-call | tf_op jit(solution)/shard_map/gather_weights/pallas_call | solution.py:213
  86.7 0.9 bitcast_convert_fusion
  89.1 4.3 slice_bitcast_fusion
  93.5 1.8 slice_bitcast_fusion.2
  95.9 0.9 broadcast_in_dim.32
  96.8 6.4 %concatenate.7.tab = f32[8,192,384]{2,1,0:T(8,128)} concatenate(f32[8,192,32]{2,1,0:T(8,128)S(1)} %get-tuple-element.83, f32[8,192,32]{2,1,0:T(8,128)S(1)} %broadcast_in_dim.31, f32[8,192,32]{2,1,0:T(8,128)S(1)} %get-tuple-element.83, f32[8,192,32]{2,1,0:T(8,128)S(1)} %broadcast_in_dim.31, f32[8,192,32]{2,1,0:T(8,128)S(1)} %get-tuple-element.82, f32[8,192,32]{2,1,0:T(8,128)} %broadcast_in_dim.32, ...), dimensions={2} | concatenate | bytes 4718592 | tf_op jit(solution)/shard_map/concatenate | solution.py:953
  103.1 44.2 %forward_0.1 = (f32[192,1024]{1,0:T(8,128)}, bf16[8,192,1024]{2,1,0:T(8,128)(2,1)}, bf16[8,192,384]{2,1,0:T(8,128)(2,1)}, f32[16,192,192]{2,1,0:T(8,128)}, bf16[...) custom-call(f32[192,1024]{1,0:T(8,128)} %x_ref.3, f32[8,1024]{1,0:T(8,128)} %get-tuple-element.85.ln_ref, ...), custom_call_target="tpu_custom_call" | custom-call | tf_op jit(solution)/shard_map/forward_0/pallas_call | solution.py:452
  148.0 47.5 %forward_1.1 = (f32[192,1024]{1,0:T(8,128)}, bf16[8,192,1024]{2,1,0:T(8,128)(2,1)}, bf16[8,192,384]{2,1,0:T(8,128)(2,1)}, f32[16,192,192]{2,1,0:T(8,128)}, bf16[...) custom-call(f32[192,1024]{1,0:T(8,128)} %get-tuple-element.47.x_ref, f32[8,1024]{1,0:T(8,128)} %get-tuple-element.84.ln_ref, ...), custom_call_target="tpu_custom_call" | custom-call | tf_op jit(solution)/shard_map/forward_1/pallas_call | solution.py:452
  195.5 1.0 broadcast_multiply_fusion.g_ref
  196.5 52.9 %backward_1.1 = (f32[192,1024]{1,0:T(8,128)}, bf16[2,4,128,384]{3,2,1,0:T(8,128)(2,1)}, bf16[2,4,128,512]{3,2,1,0:T(8,128)(2,1)}, bf16[2,4,80,1024]{3,2,1,0:T(8,...) custom-call(f32[192,1024]{1,0:T(8,128)} %broadcast_multiply_fusion.g_ref, f32[192,1024]{1,0:T(8,128)} %get-tuple-element.47.x_ref, ...), custom_call_target="tpu_custom_call" | custom-call | tf_op jit(solution)/shard_map/backward_1/pallas_call | solution.py:585
  249.4 51.2 %backward_0.1 = (f32[192,1024]{1,0:T(8,128)}, bf16[2,4,128,384]{3,2,1,0:T(8,128)(2,1)}, bf16[2,4,128,512]{3,2,1,0:T(8,128)(2,1)}, bf16[2,4,80,1024]{3,2,1,0:T(8,...) custom-call(f32[192,1024]{1,0:T(8,128)} %get-tuple-element.54.g_ref, f32[192,1024]{1,0:T(8,128)} %x_ref.3, ...), custom_call_target="tpu_custom_call" | custom-call | tf_op jit(solution)/shard_map/backward_0/pallas_call | solution.py:585
  300.6 1.3 copy-done.1
  302.0 1.2 copy-done.2
  303.2 1.2 copy-done.3
  304.4 1.1 copy-done.4
  305.5 1.1 copy-done.5
  306.7 0.8 copy-done.10
  307.4 0.7 copy-done.12
  308.1 120.7 %reduce_all.1 = (bf16[2,64,3072]{2,1,0:T(8,128)(2,1)S(1)}, bf16[2,64,4096]{2,1,0:T(8,128)(2,1)S(1)}, bf16[2,64,1024]{2,1,0:T(8,128)(2,1)S(1)}, bf16[2,256,1024]{2,1,0:T(8,128)(2,1)S(1)}, f32[2,2,8,128]{3,2,1,0:T(8,128)S(1)}) custom-call(bf16[2,4,128,384]{3,2,1,0:T(8,128)(2,1)S(1)} %copy-done.5, bf16[2,4,128,384]{3,2,1,0:T(8,128)(2,1)S(1)} %copy-done.4, ...), custom_call_target="tpu_custom_call" | custom-call | tf_op jit(solution)/shard_map/reduce_all/pallas_call | solution.py:891
  428.8 0.9 copy-done.6
  429.7 0.7 copy-done.7
  431.1 2.4 convert_element_type.49
  433.5 0.8 convert_element_type.50
  434.3 1.5 convert_element_type.51
  436.5 1.6 convert_element_type.52
  438.0 0.9 copy.46
  438.9 0.9 copy.47
  (55 shorter events, 5.7 us)
Async XLA Ops:
  89.1 4.3 copy-start.14
  93.5 1.8 copy-start.13
  148.0 47.5 %copy-start.17 = (f32[192,1024]{1,0:T(8,128)S(1)}, f32[192,1024]{1,0:T(8,128)}, u32[]{:S(2)}) copy-start(f32[192,1024]{1,0:T(8,128)} %param.12) | copy-start | bytes 2359300
  249.4 51.2 %copy-start = (bf16[2,4,80,1024]{3,2,1,0:T(8,128)(2,1)S(1)}, bf16[2,4,80,1024]{3,2,1,0:T(8,128)(2,1)}, u32[]{:S(2)}) copy-start(bf16[2,4,80,1024]{3,2,1,0:T(8,128)(2,1)} %get-tuple-element.66.g21) | copy-start | bytes 3932164
  249.4 51.2 %copy-start.9 = (f32[8,8,128]{2,1,0:T(8,128)S(1)}, f32[8,8,128]{2,1,0:T(8,128)}, u32[]{:S(2)}) copy-start(f32[8,8,128]{2,1,0:T(8,128)} %get-tuple-element.68.lns1) | copy-start | bytes 98308
  249.4 51.2 %copy-start.11 = (f32[8,128]{1,0:T(8,128)S(1)}, f32[8,128]{1,0:T(8,128)}, u32[]{:S(2)}) copy-start(f32[8,128]{1,0:T(8,128)} %get-tuple-element.70.loc1) | copy-start | bytes 12292
  300.6 1.3 copy-start.1
  302.0 1.2 copy-start.2
  303.2 1.2 copy-start.3
  304.4 1.1 copy-start.4
  305.5 1.1 copy-start.5
  306.7 0.8 copy-start.10
  307.4 0.7 copy-start.12
  428.8 0.9 copy-start.6
  429.7 0.7 copy-start.7
  430.4 3.1 copy-start.8
  435.9 2.2 copy-start.15
  436.5 2.5 copy-start.16

commit v2 on v1

v2 whole, which is shorter than its diff:
```python
import functools
import math

import jax
import jax.numpy as jnp
from jax import lax
from jax.experimental import pallas as pl
from jax.experimental.pallas import tpu as pltpu
from jax.sharding import Mesh
from jax.sharding import PartitionSpec as P

D = 1024
HEADS = 16
HEAD = 64
ROT = 32
FF = 4096
LAYERS = 2
SLOTS = 4
CAP = 192
LINE = 8
QKV = 384
HID = 512
WIDE = QKV + HID
DEEP = 128 + HID
EPSILON = 1e-05
NEGATIVE = -1e30
AXES = ("y", "xl", "z", "xh", "c")
BF = jnp.bfloat16
F32 = jnp.float32
MESH = pl.DeviceIdType.MESH
VMEM = pltpu.VMEM
DMA = pltpu.SemaphoreType.DMA
ANY = pl.BlockSpec(memory_space=pl.ANY)
INV = pl.BlockSpec(memory_space=pltpu.VMEM)
C0 = 0.7978845608028654
C1 = 0.044715


def div(a, b):
    return lax.div(a, jnp.int32(b))


def rem(a, b):
    return lax.rem(a, jnp.int32(b))


def place():
    y, xl, z, xh, c = (lax.axis_index(a) for a in AXES)
    return y, xl, z, xh, c


def send(src, dst, ss, rs, **dev):
    cp = pltpu.make_async_remote_copy(
        src_ref=src, dst_ref=dst, send_sem=ss, recv_sem=rs, device_id=dev, device_id_type=MESH
    )
    cp.start()


def local(src, dst, sem):
    pltpu.make_async_copy(src, dst, sem).start()


def landed(ref, sem):
    pltpu.make_async_copy(ref, ref, sem).wait()


def loop(n, body):
    lax.fori_loop(0, n, lambda i, _: (body(i), 0)[1], 0)


def signal(sem, **dev):
    pl.semaphore_signal(sem, inc=1, device_id=dev, device_id_type=MESH)


def greet_line(bar, z, c):
    for k in range(1, LINE):
        j = rem(2 * z + c + k, LINE)
        signal(bar, z=div(j, 2), c=rem(j, 2))


def greet_plane(bar, y, x):
    for k in range(1, 16):
        yy = rem(y + k // 4, 4)
        xx = rem(x + k % 4, 4)
        signal(bar, y=yy, xh=div(xx, 2), xl=rem(xx, 2))


def gather_start(l, me, wqkv, win, wo, wfc, w1, w2, cs, cr, as_, ar):
    y, xl, z, xh, c, x, p, j = me
    mine = pl.ds(pl.multiple_of(64 * p, 64), 64)

    @pl.when((z == y) & (c == xl))
    def _():
        def to(jj):
            pairs = []
            for part in range(3):
                cols = pl.ds(pl.multiple_of(part * D + jj * 128, 128), 128)
                pairs.append((wqkv.at[l, :, cols], w1.at[l, mine, pl.ds(part * 128, 128)]))
            cols = pl.ds(pl.multiple_of(jj * HID, HID), HID)
            pairs.append((win.at[l, :, cols], w1.at[l, mine, pl.ds(QKV, HID)]))

            @pl.when(jj == j)
            def _():
                for i, (src, dst) in enumerate(pairs):
                    local(src, dst, ar.at[l, i])

            @pl.when(jj != j)
            def _():
                for i, (src, dst) in enumerate(pairs):
                    send(src, dst, as_.at[jj, l, i], ar.at[l, i], z=div(jj, 2), c=rem(jj, 2))

        loop(LINE, to)

    pieces = (
        (wo.at[l], w2.at[l, pl.ds(pl.multiple_of(64 * c, 64), 64)]),
        (wfc.at[l], w2.at[l, pl.ds(pl.multiple_of(128 + 256 * c, 64), 256)]),
    )
    for i, (src, dst) in enumerate(pieces):
        send(src, dst, cs.at[l, 0, i], cr.at[l, c, i], xl=1 - xl, xh=1 - xh, c=xh)

        @pl.when(c == xh)
        def _():
            local(src, dst, cr.at[l, c, i])

        @pl.when(c != xh)
        def _():
            send(src, dst, cs.at[l, 1, i], cr.at[l, c, i], c=xh)


def plane_member(y, x, k):
    xx = rem(x + rem(k, 4), 4)
    return dict(y=rem(y + div(k, 4), 4), xh=div(xx, 2), xl=rem(xx, 2))


def gather_plane(l, me, w1, ar, bs, br):
    y, xl, z, xh, c, x, p, j = me
    mine = pl.ds(pl.multiple_of(64 * p, 64), 64)
    for part in range(3):
        landed(w1.at[l, mine, pl.ds(part * 128, 128)], ar.at[l, part])
    landed(w1.at[l, mine, pl.ds(QKV, HID)], ar.at[l, 3])

    def across(k):
        block = w1.at[l, mine]
        send(block, block, bs.at[l, k], br.at[l, p], **plane_member(y, x, k))

    loop(15, lambda k: across(k + 1))


def gather_wait(l, me, w1, w2, cr, br):
    y, xl, z, xh, c, x, p, j = me

    def arrive(k):
        q = rem(p + k, 16)
        landed(w1.at[l, pl.ds(pl.multiple_of(64 * q, 64), 64)], br.at[l, q])

    loop(15, lambda k: arrive(k + 1))
    for s in range(2):
        landed(w2.at[l, pl.ds(64 * s, 64)], cr.at[l, s, 0])
        landed(w2.at[l, pl.ds(128 + 256 * s, 256)], cr.at[l, s, 1])


def gather_left(l, me, wqkv, win, wo, wfc, w1, cs, as_, bs):
    y, xl, z, xh, c, x, p, j = me
    loop(15, lambda k: landed(w1.at[l, pl.ds(0, 64)], bs.at[l, k + 1]))
    landed(wo.at[l], cs.at[l, 0, 0])
    landed(wfc.at[l], cs.at[l, 0, 1])

    @pl.when(c != xh)
    def _():
        landed(wo.at[l], cs.at[l, 1, 0])
        landed(wfc.at[l], cs.at[l, 1, 1])

    @pl.when((z == y) & (c == xl))
    def _():
        def gone(jj):
            @pl.when(jj != j)
            def _():
                for part in range(3):
                    landed(wqkv.at[l, :, pl.ds(part * D, 128)], as_.at[jj, l, part])
                landed(win.at[l, :, pl.ds(0, HID)], as_.at[jj, l, 3])

        loop(LINE, gone)


HALF = CAP // 2


def slot_of(z, c, k):
    return 2 * rem(z + k, 4) + c


def rows_start(buf, z, c, ss, rs):
    own = buf.at[2 * z + c]
    a, b = buf.at[2 * z + c, pl.ds(0, HALF)], buf.at[2 * z + c, pl.ds(HALF, HALF)]
    send(own, own, ss.at[0], rs.at[0], c=1 - c)
    up, down = dict(z=rem(z + 1, 4)), dict(z=rem(z + 3, 4))
    send(a, a, ss.at[1], rs.at[1], **up)
    send(b, b, ss.at[3], rs.at[3], **down)
    send(b, b, ss.at[2], rs.at[2], **up)
    send(a, a, ss.at[4], rs.at[4], **down)


def rows_near(buf, z, c, ss, rs):
    lo, hi = slot_of(z, c, 3), slot_of(z, c, 1)
    a = buf.at[lo, pl.ds(0, HALF)]
    b = buf.at[hi, pl.ds(HALF, HALF)]
    landed(a, rs.at[1])
    send(a, a, ss.at[5], rs.at[5], z=rem(z + 1, 4))
    landed(b, rs.at[3])
    send(b, b, ss.at[6], rs.at[6], z=rem(z + 3, 4))
    landed(b, rs.at[2])
    send(buf.at[lo], buf.at[lo], ss.at[7], rs.at[7], c=1 - c)
    landed(a, rs.at[4])
    send(buf.at[hi], buf.at[hi], ss.at[8], rs.at[8], c=1 - c)


def rows_far(buf, z, c, ss, rs):
    far = slot_of(z, c, 2)
    landed(buf.at[far, pl.ds(0, HALF)], rs.at[5])
    landed(buf.at[far, pl.ds(HALF, HALF)], rs.at[6])
    send(buf.at[far], buf.at[far], ss.at[9], rs.at[9], c=1 - c)


def rows_ready(k, buf, z, c, ss, rs):
    @pl.when(k == 0)
    def _():
        landed(buf.at[2 * z + 1 - c], rs.at[0])

    @pl.when(k == 1)
    def _():
        rows_near(buf, z, c, ss, rs)
        landed(buf.at[slot_of(z, 1 - c, 3)], rs.at[7])

    @pl.when(k == 2)
    def _():
        rows_far(buf, z, c, ss, rs)
        landed(buf.at[slot_of(z, 1 - c, 1)], rs.at[8])

    @pl.when(k == 3)
    def _():
        landed(buf.at[slot_of(z, 1 - c, 2)], rs.at[9])


def rows_left(buf, ss):
    for i in (0, 7, 8, 9):
        landed(buf.at[0], ss.at[i])
    for i in range(1, 7):
        landed(buf.at[0, pl.ds(0, HALF)], ss.at[i])


def chip_of(z, k):
    return rem(z + jnp.where(k == 1, 3, jnp.where(k == 0, 0, k - 1)), 4)


def sums_send(k, zz, partial, c, own, sibout, sibin, out, inn, sbs, sbr, rss, rsr):
    sibout[k] = partial(2 * zz + 1 - c).astype(BF)
    send(sibout.at[k], sibin.at[k], sbs.at[k], sbr.at[k], c=1 - c)
    term = partial(2 * zz + c)
    landed(sibin.at[k], sbr.at[k])
    term = term + sibin[k].astype(F32)

    @pl.when(k == 0)
    def _():
        own[...] = term

    @pl.when(k > 0)
    def _():
        out[k - 1] = term.astype(BF)
        send(out.at[k - 1], inn.at[k - 1], rss.at[k - 1], rsr.at[k - 1], z=zz)


def sums_total(own, inn, rsr):
    total = own[...]
    for i in range(3):
        landed(inn.at[i], rsr.at[i])
        total = total + inn[i].astype(F32)
    return total


def sums_left(sibout, out, sbs, rss):
    for i in range(4):
        landed(sibout.at[i], sbs.at[i])
    for i in range(3):
        landed(out.at[i], rss.at[i])


def lanes(shape):
    return lax.broadcasted_iota(jnp.int32, shape, len(shape) - 1)


def turn(v, cos, sin):
    low = rem(lanes(v.shape), 64) < 16
    partner = jnp.where(low, pltpu.roll(v, 112, 1), pltpu.roll(v, 16, 1))
    return v * cos + partner * sin


def nt(a, b):
    return lax.dot_general(a, b, (((1,), (1,)), ((), ())), preferred_element_type=F32)


def tn(a, b):
    return lax.dot_general(a, b, (((0,), (0,)), ((), ())), preferred_element_type=F32)


def nn(a, b):
    return jnp.dot(a, b, preferred_element_type=F32)


def stats(x):
    centre = x - jnp.mean(x, axis=-1, keepdims=True)
    r = lax.rsqrt(jnp.mean(centre * centre, axis=-1, keepdims=True) + EPSILON)
    return centre, r


def expand(t):
    lane = lanes(t.shape)
    rot = rem(lane, 64) < ROT
    first = lane < 64
    cos = jnp.where(rot, jnp.where(first, t, pltpu.roll(t, 64, 1)), 1.0)
    sin = jnp.where(rot, jnp.where(first, pltpu.roll(t, 96, 1), pltpu.roll(t, 32, 1)), 0.0)
    return cos, sin, t[:, 64:65]


def forward_pass(l, z, c, x, vec, bins, w1, w2, tabs, nall, qkv, prob, a2, pre, raw, sums, rows, spill):
    ss, rs = rows
    centre, r = stats(x[...])
    row = 8 * l
    nall[2 * z + c] = (centre * r * vec[row : row + 1, :] + vec[row + 1 : row + 2, :]).astype(BF)
    rows_start(nall, z, c, ss, rs)

    def step(k):
        zz = chip_of(z, k)
        rows_ready(k, nall, z, c, ss, rs)
        two = pl.ds(2 * zz, 2)
        n = nall[two].reshape(2 * CAP, D)
        raw[:, 0:QKV] = nn(n, w1[:, :QKV])
        pre[two] = (nn(n, w1[:, QKV:]) + bins[row : row + 1, :]).reshape(2, CAP, HID)

        def act(i):
            u, t = div(i, 6), rem(i, 6)
            at = pl.ds(pl.multiple_of(t * 32, 32), 32)
            v = pre[2 * zz + u, at, :]
            g = 0.5 * v * (1.0 + jnp.tanh(C0 * (v + C1 * v * v * v)))
            a2[2 * zz + u, at, 128:] = g.astype(BF)

        loop(12, act)
        for u in range(2):
            s = 2 * zz + u
            at = slice(u * CAP, (u + 1) * CAP)
            cos, sin, start = expand(tabs[s])
            q = turn(raw[at, 0:128], cos, sin).astype(BF)
            kk = turn(raw[at, 128:256], cos, sin).astype(BF)
            v = raw[at, 256:384].astype(BF)
            qkv[s, :, 0:128] = q
            qkv[s, :, 128:256] = kk
            qkv[s, :, 256:384] = v
            q = q * jnp.asarray(1.0 / math.sqrt(HEAD), BF)
            key_at = lanes((CAP, CAP))
            query_at = lax.broadcasted_iota(jnp.int32, (CAP, CAP), 0)
            allowed = (key_at >= start.astype(jnp.int32)) & (key_at <= query_at)
            head = lanes((CAP, 128)) < HEAD
            mixed = []
            for h in range(2):
                qh = jnp.where(head if h == 0 else ~head, q, jnp.zeros_like(q))
                score = jnp.where(allowed, nt(qh, kk), NEGATIVE)
                e = jnp.exp(score - jnp.max(score, axis=-1, keepdims=True))
                w = e / jnp.sum(e, axis=-1, keepdims=True)
                prob[2 * s + h] = w
                mixed.append(nn(w.astype(BF), v))
            a2[s, :, 0:128] = jnp.where(head, mixed[0], mixed[1]).astype(BF)
        if spill is not None:
            prob_o, pre_o, sem = spill
            local(prob.at[pl.ds(4 * zz, 4)], prob_o.at[pl.ds(4 * zz, 4)], sem.at[k, 0])
            local(pre.at[two], pre_o.at[two], sem.at[k, 1])
        sums_send(k, zz, lambda s: nn(a2[s], w2[...]), c, *sums)

    loop(4, step)
    own, _, _, out, inn, _, _, rss, rsr = sums
    return x[...] + (sums_total(own, inn, rsr) + vec[row + 2 : row + 3, :])


def backward_pass(
    l, z, c, g_ref, x, vec, w1, w2, tabs, nall, qkv, prob, a2, pre, raw, gall, dp,
    g1q, g1i, g2, lns, loc, sums, rows, hook,
):
    ss, rs = rows
    gall[2 * z + c] = g_ref[...].astype(BF)
    rows_start(gall, z, c, ss, rs)
    hook(0)

    def step(k):
        zz = chip_of(z, k)
        rows_ready(k, gall, z, c, ss, rs)
        two = pl.ds(2 * zz, 2)
        g = gall[two].reshape(2 * CAP, D)
        raw[...] = nt(g, w2[...])

        def act(i):
            u, t = div(i, 12), rem(i, 12)
            at = pl.ds(pl.multiple_of(t * 16, 16), 16)
            v = pre[2 * zz + u, at, :]
            d = raw[pl.ds(pl.multiple_of(u * CAP + t * 16, 16), 16), 128:]
            t1 = jnp.tanh(C0 * (v + C1 * v * v * v))
            slope = 0.5 * (1.0 + t1) + 0.5 * v * (1.0 - t1 * t1) * (C0 + (3.0 * C0 * C1) * v * v)
            dp[2 * zz + u, at, QKV:] = (d * slope).astype(BF)

        loop(24, act)
        for u in range(2):
            s = 2 * zz + u
            at = slice(u * CAP, (u + 1) * CAP)
            cos, sin, _ = expand(tabs[s])
            m = raw[at, 0:128].astype(BF)
            q, kk, v = qkv[s, :, 0:128], qkv[s, :, 128:256], qkv[s, :, 256:384]
            head = lanes((CAP, 128)) < HEAD
            dq, dk, dv = [], [], []
            for h in range(2):
                mine = head if h == 0 else ~head
                mh = jnp.where(mine, m, jnp.zeros_like(m))
                w = prob[2 * s + h]
                soft = nt(mh, v)
                dv.append(tn(w.astype(BF), mh))
                wd = w * soft
                ds = (wd - w * jnp.sum(wd, axis=-1, keepdims=True)).astype(BF)
                dq.append(nn(ds, kk))
                dk.append(tn(ds, jnp.where(mine, q, jnp.zeros_like(q))))
            scale = 1.0 / math.sqrt(HEAD)
            dq = jnp.where(head, dq[0], dq[1]) * scale
            dk = (dk[0] + dk[1]) * scale
            dp[s, :, 0:128] = turn(dq, cos, -sin).astype(BF)
            dp[s, :, 128:256] = turn(dk, cos, -sin).astype(BF)
            dp[s, :, 256:384] = (dv[0] + dv[1]).astype(BF)
        sums_send(k, zz, lambda s: nt(dp[s], w1[...]), c, *sums)

    loop(4, step)
    hook(1)

    rows = LINE * CAP
    g = gall[...].reshape(rows, D)
    val = tn(a2[...].reshape(rows, DEEP), g)
    for s in range(2):
        for q in range(4):
            g2[s, q, 0:16, :] = val[64 * s + 16 * q : 64 * s + 16 * q + 16].astype(BF)
            base = 128 + 256 * s + 64 * q
            g2[s, q, 16:80, :] = val[base : base + 64].astype(BF)
    hook(2)
    d = dp[...].reshape(rows, WIDE)
    for t in range(2):
        val = tn(nall[:, :, t * 512 : (t + 1) * 512].reshape(rows, 512), d).astype(BF)
        for s in range(8):
            sh = 8 * t + s
            zz, hh, cc = sh // 4, (sh // 2) % 2, sh % 2
            for q in range(4):
                part = val[64 * s + 16 * q : 64 * s + 16 * q + 16]
                at = (2 * zz + cc) * 16
                g1q[hh, q, at : at + 16, :] = part[:, :QKV]
                g1i[hh, q, at : at + 16, :] = part[:, QKV:]
    hook(3)

    zero = jnp.zeros((1, 128), F32)
    col = pl.ds(pl.multiple_of((2 * z + c) * 128, 128), 128)
    bfc = jnp.zeros((1, 128), F32)
    b_in = jnp.zeros((1, HID), F32)
    for s in range(LINE):
        bfc = bfc + jnp.sum(gall[s, :, col].astype(F32), axis=0, keepdims=True)
        b_in = b_in + jnp.sum(dp[s, :, QKV:].astype(F32), axis=0, keepdims=True)
    loc[...] = jnp.concatenate(
        [zero, zero, bfc] + [b_in[:, 128 * i : 128 * i + 128] for i in range(4)] + [zero], axis=0
    )
    own, _, _, out, inn, _, _, rss, rsr = sums
    ngrad = sums_total(own, inn, rsr)
    centre, r = stats(x[...])
    xhat = centre * r
    e = ngrad * vec[8 * l : 8 * l + 1, :]
    ex = jnp.mean(e * xhat, axis=-1, keepdims=True)
    gain = jnp.sum(ngrad * xhat, axis=0, keepdims=True)
    bias = jnp.sum(ngrad, axis=0, keepdims=True)
    both = jnp.concatenate([gain, bias] + [jnp.zeros((6, D), F32)], axis=0)
    for i in range(LINE):
        lns[i] = both[:, 128 * i : 128 * i + 128]
    return g_ref[...] + r * (e - jnp.mean(e, axis=-1, keepdims=True) - xhat * ex)


def member(jj):
    return dict(z=div(jj, 2), c=rem(jj, 2))


def small_start(l, me, lns, zs, s5, q5):
    j = me[7]

    def go(k):
        jj = rem(j + k, LINE)
        send(lns.at[l, jj], zs.at[l, j], s5.at[l, k], q5.at[l, j], **member(jj))

    loop(LINE - 1, lambda k: go(k + 1))


def small_spread(l, me, lns, loc, zs, ps, q5, s6, q6):
    y, xl, z, xh, c, x, p, j = me

    def small_in(k):
        jj = rem(j + k, LINE)
        landed(zs.at[l, jj], q5.at[l, jj])

    loop(LINE - 1, lambda k: small_in(k + 1))
    zs[l, j] = lns[l, j] + loc[l]
    total = zs[l, 0]
    for i in range(1, LINE):
        total = total + zs[l, i]
    ps[l, p] = total

    def spread(k):
        send(ps.at[l, p], ps.at[l, p], s6.at[l, k], q6.at[l, p], **plane_member(y, x, k))

    loop(15, lambda k: spread(k + 1))


def small_last(l, me, ps, tot, q6, s8, q8):
    y, xl, z, xh, c, x, p, j = me

    def spread_in(k):
        q = rem(p + k, 16)
        landed(ps.at[l, q], q6.at[l, q])

    loop(15, lambda k: spread_in(k + 1))
    total = ps[l, 0]
    for i in range(1, 16):
        total = total + ps[l, i]
    tot[l, c] = total
    send(tot.at[l, c], tot.at[l, c], s8.at[l], q8.at[l], c=1 - c)


def second_start(l, me, g2, r2, s2, q2):
    y, xl, z, xh, c, x, p, j = me

    def second(i):
        yy, cc = rem(y + div(i, 2), 4), rem(xl + rem(i, 2), 2)
        src, dst = g2.at[cc, yy], r2.at[l, p]
        here = (i == 0) & (xh == c)

        @pl.when(here)
        def _():
            local(src, dst, q2.at[l, p])

        @pl.when(jnp.logical_not(here))
        def _():
            send(src, dst, s2.at[l, i], q2.at[l, p], y=yy, xl=cc, xh=c)

    loop(8, second)


def first_start(l, me, g1q, g1i, r1, s1, q1):
    y, xl, z, xh, c, x, p, j = me

    def first(k):
        yy = rem(y + div(k, 4), 4)
        xx = rem(x + rem(k, 4), 4)
        hh, ll = div(xx, 2), rem(xx, 2)

        @pl.when(ll == 0)
        def _():
            dst = r1.at[l, p, :, pl.ds(0, QKV)]
            send(g1q.at[hh, yy], dst, s1.at[l, k], q1.at[l, p], y=yy, xh=hh, xl=ll)

        @pl.when(ll == 1)
        def _():
            send(g1i.at[hh, yy], r1.at[l, p], s1.at[l, k], q1.at[l, p], y=yy, xh=hh, xl=ll)

    loop(15, lambda k: first(k + 1))

    @pl.when(xl == 0)
    def _():
        local(g1q.at[xh, y], r1.at[l, p, :, pl.ds(0, QKV)], q1.at[l, p])

    @pl.when(xl == 1)
    def _():
        local(g1i.at[xh, y], r1.at[l, p], q1.at[l, p])


def second_sum(l, me, r2, red2, fo, ff, q2, s4, q4):
    y, xl, z, xh, c, x, p, j = me
    row16 = pl.ds(pl.multiple_of(16 * y, 16), 16)
    row64 = pl.ds(pl.multiple_of(64 * y, 64), 64)

    @pl.when(xh == c)
    def _():
        loop(16, lambda q: landed(r2.at[l, q], q2.at[l, q]))

        def add(t):
            at = pl.ds(pl.multiple_of(16 * t, 16), 16)
            acc = r2[l, 0, at, :].astype(F32)
            for q in range(1, 16):
                acc = acc + r2[l, q, at, :].astype(F32)
            red2[l, at, :] = acc.astype(BF)

        loop(5, add)

        def out(i):
            yy, ll = rem(y + div(i, 2), 4), rem(xl + rem(i, 2), 2)
            here = (i == 0) & (xl == c)
            parts = (
                (red2.at[l, pl.ds(0, 16)], fo.at[l, row16]),
                (red2.at[l, pl.ds(16, 64)], ff.at[l, row64]),
            )
            for n, (src, dst) in enumerate(parts):

                @pl.when(here)
                def _():
                    local(src, dst, q4.at[l, y, n])

                @pl.when(jnp.logical_not(here))
                def _():
                    send(src, dst, s4.at[l, i, n], q4.at[l, y, n], y=yy, xl=ll, c=xl)

        loop(8, out)


def first_sum(l, me, r1, red1, fq, fi, q1, s3, q3):
    y, xl, z, xh, c, x, p, j = me
    row16 = pl.ds(pl.multiple_of(16 * y, 16), 16)

    def arrive(q):
        @pl.when(xl == 0)
        def _():
            landed(r1.at[l, q, :, pl.ds(0, QKV)], q1.at[l, q])

        @pl.when(xl == 1)
        def _():
            landed(r1.at[l, q], q1.at[l, q])

    loop(16, arrive)

    def add(t):
        at = pl.ds(pl.multiple_of(16 * t, 16), 16)
        acc = r1[l, 0, at, :].astype(F32)
        for q in range(1, 16):
            acc = acc + r1[l, q, at, :].astype(F32)
        red1[l, at, :] = acc.astype(BF)

    loop(8, add)

    def back(jj):
        at = pl.ds(pl.multiple_of(16 * jj, 16), 16)

        def move(src, dst, n):
            @pl.when(jj == j)
            def _():
                local(src, dst, q3.at[l, j, n])

            @pl.when(jj != j)
            def _():
                send(src, dst, s3.at[l, jj, n], q3.at[l, j, n], **member(jj))

        @pl.when(xl == 0)
        def _():
            for n in range(3):
                cols = pl.ds(pl.multiple_of(n * D + 128 * j, 128), 128)
                move(red1.at[l, at, pl.ds(128 * n, 128)], fq.at[l, row16, cols], n)

        @pl.when(xl == 1)
        def _():
            cols = pl.ds(pl.multiple_of(HID * j, HID), HID)
            move(red1.at[l, at], fi.at[l, row16, cols], 0)

    loop(LINE, back)


def first_share(l, me, fq, fi, q3, s7, q7):
    y, xl, z, xh, c, x, p, j = me
    row16 = pl.ds(pl.multiple_of(16 * y, 16), 16)

    def back_in(jj):
        @pl.when(xl == 0)
        def _():
            for n in range(3):
                at = pl.ds(pl.multiple_of(n * D + 128 * jj, 128), 128)
                landed(fq.at[l, row16, at], q3.at[l, jj, n])

        @pl.when(xl == 1)
        def _():
            at = pl.ds(pl.multiple_of(HID * jj, HID), HID)
            landed(fi.at[l, row16, at], q3.at[l, jj, 0])

    loop(LINE, back_in)

    def share(i):
        yy, ll = rem(y + div(i, 2), 4), rem(xl + rem(i, 2), 2)
        for v, f in ((0, fq), (1, fi)):

            @pl.when(xl == v)
            def _():
                at = f.at[l, row16]
                send(at, at, s7.at[l, i], q7.at[l, y, v], y=yy, xl=ll)

    loop(7, lambda i: share(i + 1))


def owners_in(l, me, fq, fi, fo, ff, q4, q7):
    y, xl, z, xh, c, x, p, j = me
    for q in range(4):
        landed(fo.at[l, pl.ds(16 * q, 16)], q4.at[l, q, 0])
        landed(ff.at[l, pl.ds(64 * q, 64)], q4.at[l, q, 1])
        for v, f in ((0, fq), (1, fi)):

            @pl.when((xl != v) | (y != q))
            def _():
                landed(f.at[l, pl.ds(16 * q, 16)], q7.at[l, q, v])


def first_left(l, me, r1, s1):
    x = me[5]

    def go(k):
        ll = rem(rem(x + rem(k, 4), 4), 2)

        @pl.when(ll == 0)
        def _():
            landed(r1.at[l, 0, :, pl.ds(0, QKV)], s1.at[l, k])

        @pl.when(ll == 1)
        def _():
            landed(r1.at[l, 0], s1.at[l, k])

    loop(15, lambda k: go(k + 1))


def second_left(l, me, r2, s2):
    y, xl, z, xh, c, x, p, j = me

    def go(i):
        @pl.when(jnp.logical_not((i == 0) & (xh == c)))
        def _():
            landed(r2.at[l, 0], s2.at[l, i])

    loop(8, go)


def owners_left(l, me, lns, ps, tot, red1, red2, fq, fi, s3, s4, s5, s6, s7, s8):
    y, xl, z, xh, c, x, p, j = me
    row16 = pl.ds(pl.multiple_of(16 * y, 16), 16)
    loop(LINE - 1, lambda k: landed(lns.at[l, 0], s5.at[l, k + 1]))
    loop(15, lambda k: landed(ps.at[l, 0], s6.at[l, k + 1]))

    def left_second(i):
        @pl.when((xh == c) & jnp.logical_not((i == 0) & (xl == c)))
        def _():
            landed(red2.at[l, pl.ds(0, 16)], s4.at[l, i, 0])
            landed(red2.at[l, pl.ds(16, 64)], s4.at[l, i, 1])

    loop(8, left_second)

    def left_back(jj):
        @pl.when((jj != j) & (xl == 0))
        def _():
            for n in range(3):
                landed(red1.at[l, pl.ds(0, 16), pl.ds(0, 128)], s3.at[l, jj, n])

        @pl.when((jj != j) & (xl == 1))
        def _():
            landed(red1.at[l, pl.ds(0, 16)], s3.at[l, jj, 0])

    loop(LINE, left_back)

    def left_share(i):
        for v, f in ((0, fq), (1, fi)):

            @pl.when(xl == v)
            def _():
                landed(f.at[l, row16], s7.at[l, i])

    loop(7, lambda i: left_share(i + 1))
    landed(tot.at[l, c], s8.at[l])


def whole_kernel(
    wqkv, win, wo, wfc, sm, tab, x0, cot,
    x2_ref, g0_ref, fs_ref, fq, fi, fo, ff, prob_o, pre_o,
    w1, w2, sma, tabs, vec, bins,
    nall, qkv, a2, prob, pre, raw, gall, dp, x1,
    own, sibout, sibin, out, inn,
    g1q, g1i, g2, lns, loc, r1, r2, red1, red2, zs, ps, tot,
    cs, cr, as_, ar, bs, br, ts, tr, ms, mr, ns, nr,
    rows_s, rows_r, sbs, sbr, rss, rsr, spill, fill,
    s1, q1, s2, q2, s3, q3, s4, q4, s5, q5, s6, q6, s7, q7, s8, q8,
):
    y, xl, z, xh, c = place()
    x = 2 * xh + xl
    p = 4 * y + x
    j = 2 * z + c
    me = (y, xl, z, xh, c, x, p, j)
    bar = pltpu.get_barrier_semaphore()
    greet_line(bar, z, c)
    greet_plane(bar, y, x)
    for k in range(1, 8):
        signal(bar, y=rem(y + k // 2, 4), xl=rem(xl + k % 2, 2), c=1 - c)
    signal(bar, xl=1 - xl, xh=1 - xh, c=1 - c)
    pl.semaphore_wait(bar, 30)

    source = (z == y) & (c == xl)

    @pl.when(source)
    def _():
        def to(jj):
            @pl.when(jj == j)
            def _():
                local(sm, sma.at[p], mr)

            @pl.when(jj != j)
            def _():
                send(sm, sma.at[p], ms.at[jj], mr, **member(jj))

        loop(LINE, to)

    for l in range(LAYERS):
        gather_start(l, me, wqkv, win, wo, wfc, w1, w2, cs, cr, as_, ar)
    for k in range(1, LINE):
        jj = rem(j + k, LINE)
        send(tab, tabs.at[j], ts.at[k], tr.at[j], **member(jj))
    local(tab, tabs.at[j], tr.at[j])
    landed(sma.at[p], mr)

    def small_out(k):
        send(sma.at[p], sma.at[p], ns.at[k], nr.at[p], **plane_member(y, x, k))

    loop(15, lambda k: small_out(k + 1))
    gather_plane(0, me, w1, ar, bs, br)

    def small_in(k):
        q = rem(p + k, 16)
        landed(sma.at[q], nr.at[q])

    loop(15, lambda k: small_in(k + 1))
    half = lanes((16, 128)) < 64
    for t in range(8):
        vec[:, 128 * t : 128 * t + 128] = jnp.where(half, sma[2 * t, :, :128], sma[2 * t + 1, :, :128])
    for l in range(LAYERS):
        at = 8 * l + 3
        bins[8 * l : 8 * l + 1, 0:256] = sma[2 * j, at : at + 1, :]
        bins[8 * l : 8 * l + 1, 256:512] = sma[2 * j + 1, at : at + 1, :]

    def sums_of(n):
        return (
            own, sibout, sibin, out, inn, sbs.at[n], sbr.at[n], rss.at[n], rsr.at[n],
        )

    def rows_of(n):
        return rows_s.at[n], rows_r.at[n]

    def done(n, buf):
        rows_left(buf, rows_s.at[n])
        sums_left(sibout, out, sbs.at[n], rss.at[n])

    loop(LINE, lambda k: landed(tabs.at[k], tr.at[k]))
    gather_wait(0, me, w1, w2, cr, br)
    gather_plane(1, me, w1, ar, bs, br)
    x1[...] = forward_pass(
        0, z, c, x0, vec, bins, w1.at[0], w2.at[0], tabs, nall.at[0], qkv.at[0], prob, a2.at[0], pre,
        raw, sums_of(0), rows_of(0), (prob_o, pre_o, spill),
    )
    done(0, nall.at[0])
    for k in range(4):
        landed(prob.at[pl.ds(0, 4)], spill.at[k, 0])
        landed(pre.at[pl.ds(0, 2)], spill.at[k, 1])
    gather_wait(1, me, w1, w2, cr, br)
    x2_ref[...] = forward_pass(
        1, z, c, x1, vec, bins, w1.at[1], w2.at[1], tabs, nall.at[1], qkv.at[1], prob, a2.at[1], pre,
        raw, sums_of(1), rows_of(1), None,
    )
    done(1, nall.at[1])
    g0_ref[...] = cot[...] * tab[:, 96:97]

    def hook1(n):
        if n == 1:
            local(prob_o, prob, fill.at[0])
            local(pre_o, pre, fill.at[1])
        if n == 2:
            second_start(1, me, g2, r2, s2, q2)
        if n == 3:
            first_start(1, me, g1q, g1i, r1, s1, q1)

    g0_ref[...] = backward_pass(
        1, z, c, g0_ref, x1, vec, w1.at[1], w2.at[1], tabs, nall.at[1], qkv.at[1], prob, a2.at[1], pre,
        raw, gall.at[1], dp, g1q, g1i, g2, lns.at[1], loc.at[1], sums_of(2), rows_of(2), hook1,
    )
    done(2, gall.at[1])
    small_start(1, me, lns, zs, s5, q5)

    def hook0(n):
        if n == 0:
            landed(prob, fill.at[0])
            landed(pre, fill.at[1])
        if n == 1:
            small_spread(1, me, lns, loc, zs, ps, q5, s6, q6)
            second_sum(1, me, r2, red2, fo, ff, q2, s4, q4)
            second_left(1, me, r2, s2)
        if n == 2:
            second_start(0, me, g2, r2, s2, q2)
            first_sum(1, me, r1, red1, fq, fi, q1, s3, q3)
            first_left(1, me, r1, s1)
        if n == 3:
            first_start(0, me, g1q, g1i, r1, s1, q1)

    g0_ref[...] = backward_pass(
        0, z, c, g0_ref, x0, vec, w1.at[0], w2.at[0], tabs, nall.at[0], qkv.at[0], prob, a2.at[0], pre,
        raw, gall.at[0], dp, g1q, g1i, g2, lns.at[0], loc.at[0], sums_of(3), rows_of(3), hook0,
    )
    small_start(0, me, lns, zs, s5, q5)
    done(3, gall.at[0])
    first_share(1, me, fq, fi, q3, s7, q7)
    small_last(1, me, ps, tot, q6, s8, q8)
    small_spread(0, me, lns, loc, zs, ps, q5, s6, q6)
    second_sum(0, me, r2, red2, fo, ff, q2, s4, q4)
    first_sum(0, me, r1, red1, fq, fi, q1, s3, q3)
    first_share(0, me, fq, fi, q3, s7, q7)
    small_last(0, me, ps, tot, q6, s8, q8)
    for l in (1, 0):
        landed(tot.at[l, 1 - c], q8.at[l])
        fs_ref[l] = tot[l]
        owners_in(l, me, fq, fi, fo, ff, q4, q7)
    second_left(0, me, r2, s2)
    first_left(0, me, r1, s1)
    for l in range(LAYERS):
        owners_left(l, me, lns, ps, tot, red1, red2, fq, fi, s3, s4, s5, s6, s7, s8)
        gather_left(l, me, wqkv, win, wo, wfc, w1, cs, as_, bs)
    for k in range(1, LINE):
        landed(tab, ts.at[k])
    loop(15, lambda k: landed(sma.at[0], ns.at[k + 1]))

    @pl.when(source)
    def _():
        def gone(jj):
            @pl.when(jj != j)
            def _():
                landed(sm, ms.at[jj])

        loop(LINE, gone)


def whole(wqkv, win, wo, wfc, sm, tab, x0, cot):
    n = LAYERS
    return pl.pallas_call(
        whole_kernel,
        out_shape=(
            jax.ShapeDtypeStruct((CAP, D), F32),
            jax.ShapeDtypeStruct((CAP, D), F32),
            jax.ShapeDtypeStruct((n, 2, 8, 128), F32),
            jax.ShapeDtypeStruct((n, 64, 3 * D), BF),
            jax.ShapeDtypeStruct((n, 64, FF), BF),
            jax.ShapeDtypeStruct((n, 64, D), BF),
            jax.ShapeDtypeStruct((n, 256, D), BF),
            jax.ShapeDtypeStruct((2 * LINE, CAP, CAP), F32),
            jax.ShapeDtypeStruct((LINE, CAP, HID), F32),
        ),
        in_specs=[ANY] * 4 + [INV] * 4,
        out_specs=(INV,) * 3 + (ANY,) * 6,
        scratch_shapes=[
            VMEM((n, D, WIDE), BF), VMEM((n, DEEP, D), BF), VMEM((16, 16, 256), F32),
            VMEM((LINE, CAP, 128), F32), VMEM((16, D), F32), VMEM((16, HID), F32),
            VMEM((n, LINE, CAP, D), BF), VMEM((n, LINE, CAP, QKV), BF), VMEM((n, LINE, CAP, DEEP), BF),
            VMEM((2 * LINE, CAP, CAP), F32), VMEM((LINE, CAP, HID), F32), VMEM((2 * CAP, DEEP), F32),
            VMEM((n, LINE, CAP, D), BF), VMEM((LINE, CAP, WIDE), BF),
            VMEM((CAP, D), F32),
            VMEM((CAP, D), F32), VMEM((4, CAP, D), BF), VMEM((4, CAP, D), BF),
            VMEM((3, CAP, D), BF), VMEM((3, CAP, D), BF),
            VMEM((2, 4, 128, QKV), BF), VMEM((2, 4, 128, HID), BF), VMEM((2, 4, 80, D), BF),
            VMEM((n, LINE, 8, 128), F32), VMEM((n, 8, 128), F32),
            VMEM((n, 16, 128, HID), BF), VMEM((n, 16, 80, D), BF),
            VMEM((n, 128, HID), BF), VMEM((n, 80, D), BF),
            VMEM((n, LINE, 8, 128), F32), VMEM((n, 16, 8, 128), F32), VMEM((n, 2, 8, 128), F32),
            DMA((n, 2, 2)), DMA((n, 2, 2)), DMA((LINE, n, 4)), DMA((n, 4)),
            DMA((n, 16)), DMA((n, 16)), DMA((LINE,)), DMA((LINE,)),
            DMA((LINE,)), DMA, DMA((16,)), DMA((16,)),
            DMA((4, 10)), DMA((4, 10)), DMA((4, 4)), DMA((4, 4)), DMA((4, 3)), DMA((4, 3)),
            DMA((4, 2)), DMA((2,)),
            DMA((n, 16)), DMA((n, 16)),
            DMA((n, 8)), DMA((n, 16)),
            DMA((n, LINE, 3)), DMA((n, LINE, 3)),
            DMA((n, 8, 2)), DMA((n, 4, 2)),
            DMA((n, LINE)), DMA((n, LINE)),
            DMA((n, 16)), DMA((n, 16)),
            DMA((n, 8)), DMA((n, 4, 2)),
            DMA((n,)), DMA((n,)),
        ],
        compiler_params=pltpu.CompilerParams(
            collective_id=0, has_side_effects=True, vmem_limit_bytes=63 * 2**20
        ),
        name="whole",
    )(wqkv, win, wo, wfc, sm, tab, x0, cot)


def per_device(
    inputs, cotangent, lengths, ln_gain, ln_bias, w_qkv, w_attn_out, w_in, b_in, w_fc, b_fc
):
    xh, c = (lax.axis_index(a) for a in ("xh", "c"))
    offsets = jnp.arange(CAP, dtype=jnp.int32)
    seq_ends = jnp.cumsum(lengths[0])
    passed = (offsets[:, None] >= seq_ends[None, :]).astype(jnp.int32)
    segment = jnp.sum(passed, axis=1)
    start = jnp.sum(passed * lengths[0][None, :], axis=1)
    position = offsets - start
    frequency = 10000.0 ** (-jnp.arange(ROT // 2, dtype=F32) * 2.0 / ROT)
    angles = position.astype(F32)[:, None] * frequency
    cosine, sine = jnp.cos(angles), jnp.sin(angles)
    valid = (segment < SLOTS).astype(F32)
    tab = jnp.concatenate(
        [cosine, cosine, -sine, sine]
        + [jnp.broadcast_to(v[:, None], (CAP, 32)) for v in (start.astype(F32), valid)],
        axis=1,
    )
    wide = [jnp.concatenate([v] * (256 // v.shape[1]), axis=1) for v in (ln_gain, ln_bias, b_fc, b_in)]
    sm = jnp.stack(wide + [jnp.zeros_like(b_in)] * 4, axis=1).reshape(16, 256).astype(F32)

    hidden, grad, fs, fq, fi, fo, ff, _, _ = whole(
        w_qkv, w_in, w_attn_out, w_fc, sm, tab, inputs, cotangent
    )
    mine = lax.dynamic_index_in_dim(fs, xh, 1, keepdims=False)
    pick = lax.dynamic_slice(mine[:, 0:3], (0, 0, 64 * c), (LAYERS, 3, 64))
    b_in_grad = lax.dynamic_slice(mine[:, 3:7].reshape(LAYERS, HID), (0, 256 * c), (LAYERS, 256))
    return (
        hidden,
        grad,
        pick[:, 0],
        pick[:, 1],
        fq.astype(F32),
        fo.astype(F32),
        fi.astype(F32),
        b_in_grad,
        ff.astype(F32),
        pick[:, 2],
    )


def solution(mesh):
    fine = Mesh(mesh.devices.reshape(4, 2, 4, 2, 2), AXES)
    rows = P(AXES, None)
    shard = ("z", "xh", "c")
    vector, matrix = P(None, shard), P(None, shard, None)
    in_specs = (
        rows, rows, rows, vector, vector, matrix, matrix, matrix, vector, matrix, vector,
    )
    out_specs = (
        rows, rows, vector, vector, matrix, matrix, matrix, vector, matrix, vector,
    )
    return jax.shard_map(
        per_device, mesh=fine, in_specs=in_specs, out_specs=out_specs, check_vma=False
    )
```

time: 446 us -> 326 us (0.73); the launches traced: 440 us -> 326 us
  Pallas kernels: 397 us -> 308 us
  local copies, waits for them, and re-layouts: 30.9 us -> 5.55 us
    pallas_call x6 -> x1, Pallas kernels: 397 us -> 308 us  [whole(): pl.pallas_call(whole_kernel, out_shape=(jax.ShapeDtypeStruct((CAP, D), F3...]
    unnamed x43 -> x14, local copies, waits for them, and re-layouts: 10.9 us -> 1.79 us
    squeeze x3 -> x0, local copies, waits for them, and re-layouts: 6.74 us -> none  [per_device(): nxt, *saved = forward_layer(l, hidden, vec[l], bins[l], w1[l], w2[l], table)]
    concatenate x2 -> x1, local copies, waits for them, and re-layouts: 7.17 us -> 0.84 us  [per_device(): jnp.concatenate([cosine, cosine, -sine, sine] + [jnp.broadcast_to(v[:, No...]
where the time goes in v2:
time: 326 us
  Pallas kernels  308 us (94%)
  other arithmetic  11.7 us (4%)
  local copies, waits for them, and re-layouts  5.55 us (2%)
    pallas_call x1, Pallas kernels, whole(): pl.pallas_call(whole_kernel, out_shape=(jax.ShapeDtypeStruct((CAP, D), F3...  308 us

profile of v2, /device:TPU:32, one launch (start us, length us, event | category | flops | bytes accessed | tf_op | source)
XLA Modules:
  0.0 325.8 jit_solution(3060148265342279368)
XLA Ops:
  0.6 0.8 reduce-window.8
  1.5 0.7 convert_reduce_fusion
  2.2 0.4 multiply_sine_fusion
  2.7 0.1 broadcast_in_dim.4
  2.8 0.1 broadcast_in_dim.5
  2.9 0.8 concatenate.15.tab
  3.7 0.9 maximum_bitcast_fusion
  4.6 0.9 maximum_bitcast_fusion.1
  5.5 0.9 maximum_bitcast_fusion.2
  6.4 0.7 copy.37
  7.1 0.6 bitcast_convert_fusion.sm
  7.7 307.8 %whole.1 = (f32[192,1024]{1,0:T(8,128)}, f32[192,1024]{1,0:T(8,128)}, f32[2,2,8,128]{3,2,1,0:T(8,128)}, bf16[2,64,3072]{2,1,0:T(8,128)(2,1)}, bf16[2,64,4096]{2,...) custom-call(bf16[2,64,3072]{2,1,0:T(8,128)(2,1)} %wqkv.1, ...), custom_call_target="tpu_custom_call" | custom-call | tf_op jit(solution)/shard_map/whole/pallas_call | solution.py:940
  315.5 0.0 copy-start
  315.5 0.8 dynamic-slice_bitcast_fusion
  316.3 0.6 constant_dynamic-slice_fusion.3
  316.9 0.6 constant_dynamic-slice_fusion.2
  317.5 2.8 convert_element_type.49
  320.3 0.0 copy-start.3
  320.3 0.0 copy-done
  320.3 0.0 copy-start.4
  320.3 1.6 convert_element_type.50
  321.9 0.0 copy-start.2
  321.9 0.0 copy-done.3
  321.9 0.0 copy-start.1
  321.9 1.3 convert_element_type.47
  323.2 0.0 copy-done.4
  323.2 0.8 convert_element_type.48
  324.0 0.0 copy-done.2
  324.0 0.9 copy.44
  324.9 0.0 copy-done.1
  324.9 0.9 copy.45
  (11 shorter events, 0.1 us)
Async XLA Ops:
  315.5 4.8 %copy-start = (bf16[2,256,1024]{2,1,0:T(8,128)(2,1)S(1)}, bf16[2,256,1024]{2,1,0:T(8,128)(2,1)}, u32[]{:S(2)}) copy-start(bf16[2,256,1024]{2,1,0:T(8,128)(2,1)} %get-tuple-element.23) | copy-start | bytes 3145732
  320.3 1.6 copy-start.3
  320.3 2.9 copy-start.4
  321.9 2.2 copy-start.2
  321.9 3.0 copy-start.1

commit v3 on v2

--- a/solution.py
+++ b/solution.py
@@ -85,9 +85,27 @@
         signal(bar, y=yy, xh=div(xx, 2), xl=rem(xx, 2))
 
 
-def gather_start(l, me, wqkv, win, wo, wfc, w1, w2, cs, cr, as_, ar):
-    y, xl, z, xh, c, x, p, j = me
-    mine = pl.ds(pl.multiple_of(64 * p, 64), 64)
+def rows64(q):
+    return pl.ds(pl.multiple_of(64 * q, 64), 64)
+
+
+def second_rows(s, y):
+    return (
+        pl.ds(pl.multiple_of(64 * s + 16 * y, 16), 16),
+        pl.ds(pl.multiple_of(128 + 256 * s + 64 * y, 16), 64),
+    )
+
+
+def half_cols(h):
+    return pl.ds(pl.multiple_of(512 * h, 512), 512)
+
+
+PARTS = (pl.ds(QKV, HID), pl.ds(0, QKV))
+
+
+def weights_z(l, me, wqkv, win, wo, wfc, w1, w2, as_, ar, cs, cr):
+    y, xl, z, xh, c, x, p, j = me
+    mine = rows64(p)
 
     @pl.when((z == y) & (c == xl))
     def _():
@@ -97,7 +115,7 @@
                 cols = pl.ds(pl.multiple_of(part * D + jj * 128, 128), 128)
                 pairs.append((wqkv.at[l, :, cols], w1.at[l, mine, pl.ds(part * 128, 128)]))
             cols = pl.ds(pl.multiple_of(jj * HID, HID), HID)
-            pairs.append((win.at[l, :, cols], w1.at[l, mine, pl.ds(QKV, HID)]))
+            pairs.append((win.at[l, :, cols], w1.at[l, mine, PARTS[0]]))
 
             @pl.when(jj == j)
             def _():
@@ -111,64 +129,151 @@
 
         loop(LINE, to)
 
-    pieces = (
-        (wo.at[l], w2.at[l, pl.ds(pl.multiple_of(64 * c, 64), 64)]),
-        (wfc.at[l], w2.at[l, pl.ds(pl.multiple_of(128 + 256 * c, 64), 256)]),
+    quarter = (pl.ds(pl.multiple_of(16 * y, 16), 16), pl.ds(pl.multiple_of(64 * y, 64), 64))
+    whole_rows = (
+        pl.ds(pl.multiple_of(64 * c, 64), 64), pl.ds(pl.multiple_of(128 + 256 * c, 64), 256)
     )
-    for i, (src, dst) in enumerate(pieces):
-        send(src, dst, cs.at[l, 0, i], cr.at[l, c, i], xl=1 - xl, xh=1 - xh, c=xh)
+    place_rows = second_rows(c, y)
+    for i, w in enumerate((wo, wfc)):
+        cols = half_cols(xl)
+        dst = w2.at[l, place_rows[i], cols]
+        send(
+            w.at[l, quarter[i], cols], dst, cs.at[l, 0, i], cr.at[l, c, i], xl=1 - xl, xh=1 - xh, c=xh
+        )
+        full = w2.at[l, whole_rows[i]]
 
         @pl.when(c == xh)
         def _():
-            local(src, dst, cr.at[l, c, i])
+            local(w.at[l], full, cr.at[l, c, i])
 
         @pl.when(c != xh)
         def _():
-            send(src, dst, cs.at[l, 1, i], cr.at[l, c, i], c=xh)
+            send(w.at[l], full, cs.at[l, 1, i], cr.at[l, c, i], c=xh)
+
+
+def along_y(y, d):
+    return dict(y=rem(y + d, 4))
+
+
+def along_x(x, d):
+    xx = rem(x + d, 4)
+    return dict(xh=div(xx, 2), xl=rem(xx, 2))
 
 
 def plane_member(y, x, k):
-    xx = rem(x + rem(k, 4), 4)
-    return dict(y=rem(y + div(k, 4), 4), xh=div(xx, 2), xl=rem(xx, 2))
-
-
-def gather_plane(l, me, w1, ar, bs, br):
-    y, xl, z, xh, c, x, p, j = me
-    mine = pl.ds(pl.multiple_of(64 * p, 64), 64)
+    return {**along_y(y, div(k, 4)), **along_x(x, rem(k, 4))}
+
+
+def pass_block(l, part, q, b, stage, me, w1, bs, br):
+    y, xl, z, xh, c, x, p, j = me
+    block = w1.at[l, rows64(q), PARTS[part]]
+    for d in (1, 2, 3):
+        first = along_y(y, d) if part == 0 else along_x(x, d)
+        second = along_x(x, d) if part == 0 else along_y(y, d)
+        dev = first if stage == 0 else second
+        at = d - 1 + (0 if stage == 0 else 3 + 3 * b)
+        send(block, block, bs.at[l, part, at], br.at[l, q, part], **dev)
+
+
+def weights_p1(l, me, w1, ar, bs, br):
+    y, xl, z, xh, c, x, p, j = me
     for part in range(3):
-        landed(w1.at[l, mine, pl.ds(part * 128, 128)], ar.at[l, part])
-    landed(w1.at[l, mine, pl.ds(QKV, HID)], ar.at[l, 3])
-
-    def across(k):
-        block = w1.at[l, mine]
-        send(block, block, bs.at[l, k], br.at[l, p], **plane_member(y, x, k))
-
-    loop(15, lambda k: across(k + 1))
-
-
-def gather_wait(l, me, w1, w2, cr, br):
+        landed(w1.at[l, rows64(p), pl.ds(part * 128, 128)], ar.at[l, part])
+    landed(w1.at[l, rows64(p), PARTS[0]], ar.at[l, 3])
+    for part in range(2):
+        pass_block(l, part, p, 0, 0, me, w1, bs, br)
+    for part in range(2):
+        pass_block(l, part, p, 0, 1, me, w1, bs, br)
+
+
+def weights_p2(l, me, w1, bs, br):
+    y, xl, z, xh, c, x, p, j = me
+    for b in (1, 3, 2):
+        for part in range(2):
+            q = 4 * rem(y + b, 4) + x if part == 0 else 4 * y + rem(x + b, 4)
+            landed(w1.at[l, rows64(q), PARTS[part]], br.at[l, q, part])
+            pass_block(l, part, q, b, 1, me, w1, bs, br)
+
+
+def weights_f1(l, me, w2, cr, xs, xr):
+    y, xl, z, xh, c, x, p, j = me
+
+    @pl.when(xh != c)
+    def _():
+        for s in range(2):
+            for i, at in enumerate(second_rows(s, y)):
+                block = w2.at[l, at, half_cols(1 - xl)]
+                landed(block, cr.at[l, s, i])
+                send(block, block, xs.at[l, s, i], xr.at[l, s, i], xl=1 - xl)
+
+
+def weights_f2(l, me, w2, xr, ys, yr):
+    y, xl, z, xh, c, x, p, j = me
+
+    @pl.when(xh != c)
+    def _():
+        for s in range(2):
+            for i, at in enumerate(second_rows(s, y)):
+                landed(w2.at[l, at, half_cols(xl)], xr.at[l, s, i])
+                block = w2.at[l, at]
+                for d in (1, 2, 3):
+                    send(block, block, ys.at[l, d, s, i], yr.at[l, y, s, i], **along_y(y, d))
+
+
+def weights_in1(l, me, w1, br):
     y, xl, z, xh, c, x, p, j = me
 
     def arrive(k):
-        q = rem(p + k, 16)
-        landed(w1.at[l, pl.ds(pl.multiple_of(64 * q, 64), 64)], br.at[l, q])
-
-    loop(15, lambda k: arrive(k + 1))
-    for s in range(2):
-        landed(w2.at[l, pl.ds(64 * s, 64)], cr.at[l, s, 0])
-        landed(w2.at[l, pl.ds(128 + 256 * s, 256)], cr.at[l, s, 1])
-
-
-def gather_left(l, me, wqkv, win, wo, wfc, w1, cs, as_, bs):
-    y, xl, z, xh, c, x, p, j = me
-    loop(15, lambda k: landed(w1.at[l, pl.ds(0, 64)], bs.at[l, k + 1]))
-    landed(wo.at[l], cs.at[l, 0, 0])
-    landed(wfc.at[l], cs.at[l, 0, 1])
+        b, d = div(k, 4), rem(k, 4)
+        q = 4 * rem(y + b, 4) + rem(x + d, 4)
+
+        @pl.when(d != 0)
+        def _():
+            landed(w1.at[l, rows64(q), PARTS[0]], br.at[l, q, 0])
+
+        @pl.when(b != 0)
+        def _():
+            landed(w1.at[l, rows64(q), PARTS[1]], br.at[l, q, 1])
+
+    loop(16, arrive)
+
+
+def weights_in2(l, me, w2, cr, yr):
+    y, xl, z, xh, c, x, p, j = me
+
+    @pl.when(xh == c)
+    def _():
+        for s in range(2):
+            landed(w2.at[l, pl.ds(64 * s, 64)], cr.at[l, s, 0])
+            landed(w2.at[l, pl.ds(128 + 256 * s, 256)], cr.at[l, s, 1])
+
+    @pl.when(xh != c)
+    def _():
+        def arrive(k):
+            yy = rem(y + k, 4)
+            for s in range(2):
+                for i, at in enumerate(second_rows(s, yy)):
+                    landed(w2.at[l, at], yr.at[l, yy, s, i])
+
+        loop(3, lambda k: arrive(k + 1))
+
+
+def weights_left(l, me, wqkv, win, wo, wfc, w1, w2, as_, cs, bs, xs, ys):
+    y, xl, z, xh, c, x, p, j = me
+    for part in range(2):
+        loop(15, lambda k: landed(w1.at[l, pl.ds(0, 64), PARTS[part]], bs.at[l, part, k]))
+    for i, n in enumerate((16, 64)):
+        landed(w2.at[l, pl.ds(0, n), pl.ds(0, 512)], cs.at[l, 0, i])
 
     @pl.when(c != xh)
     def _():
         landed(wo.at[l], cs.at[l, 1, 0])
         landed(wfc.at[l], cs.at[l, 1, 1])
+        for s in range(2):
+            for i, n in enumerate((16, 64)):
+                landed(w2.at[l, pl.ds(0, n), pl.ds(0, 512)], xs.at[l, s, i])
+                for d in (1, 2, 3):
+                    landed(w2.at[l, pl.ds(0, n)], ys.at[l, d, s, i])
 
     @pl.when((z == y) & (c == xl))
     def _():
@@ -189,10 +294,13 @@
     return 2 * rem(z + k, 4) + c
 
 
-def rows_start(buf, z, c, ss, rs):
+def rows_sibling(buf, z, c, ss, rs):
     own = buf.at[2 * z + c]
+    send(own, own, ss.at[0], rs.at[0], c=1 - c)
+
+
+def rows_send(buf, z, c, ss, rs):
     a, b = buf.at[2 * z + c, pl.ds(0, HALF)], buf.at[2 * z + c, pl.ds(HALF, HALF)]
-    send(own, own, ss.at[0], rs.at[0], c=1 - c)
     up, down = dict(z=rem(z + 1, 4)), dict(z=rem(z + 3, 4))
     send(a, a, ss.at[1], rs.at[1], **up)
     send(b, b, ss.at[3], rs.at[3], **down)
@@ -200,7 +308,7 @@
     send(a, a, ss.at[4], rs.at[4], **down)
 
 
-def rows_near(buf, z, c, ss, rs):
+def rows_pass(buf, z, c, ss, rs):
     lo, hi = slot_of(z, c, 3), slot_of(z, c, 1)
     a = buf.at[lo, pl.ds(0, HALF)]
     b = buf.at[hi, pl.ds(HALF, HALF)]
@@ -208,10 +316,19 @@
     send(a, a, ss.at[5], rs.at[5], z=rem(z + 1, 4))
     landed(b, rs.at[3])
     send(b, b, ss.at[6], rs.at[6], z=rem(z + 3, 4))
-    landed(b, rs.at[2])
+
+
+def rows_near(buf, z, c, ss, rs):
+    lo, hi = slot_of(z, c, 3), slot_of(z, c, 1)
+    landed(buf.at[lo, pl.ds(HALF, HALF)], rs.at[2])
     send(buf.at[lo], buf.at[lo], ss.at[7], rs.at[7], c=1 - c)
-    landed(a, rs.at[4])
+    landed(buf.at[hi, pl.ds(0, HALF)], rs.at[4])
     send(buf.at[hi], buf.at[hi], ss.at[8], rs.at[8], c=1 - c)
+
+
+def rows_near_in(buf, z, c, rs):
+    landed(buf.at[slot_of(z, 1 - c, 3)], rs.at[7])
+    landed(buf.at[slot_of(z, 1 - c, 1)], rs.at[8])
 
 
 def rows_far(buf, z, c, ss, rs):
@@ -221,26 +338,6 @@
     send(buf.at[far], buf.at[far], ss.at[9], rs.at[9], c=1 - c)
 
 
-def rows_ready(k, buf, z, c, ss, rs):
-    @pl.when(k == 0)
-    def _():
-        landed(buf.at[2 * z + 1 - c], rs.at[0])
-
-    @pl.when(k == 1)
-    def _():
-        rows_near(buf, z, c, ss, rs)
-        landed(buf.at[slot_of(z, 1 - c, 3)], rs.at[7])
-
-    @pl.when(k == 2)
-    def _():
-        rows_far(buf, z, c, ss, rs)
-        landed(buf.at[slot_of(z, 1 - c, 1)], rs.at[8])
-
-    @pl.when(k == 3)
-    def _():
-        landed(buf.at[slot_of(z, 1 - c, 2)], rs.at[9])
-
-
 def rows_left(buf, ss):
     for i in (0, 7, 8, 9):
         landed(buf.at[0], ss.at[i])
@@ -248,25 +345,97 @@
         landed(buf.at[0, pl.ds(0, HALF)], ss.at[i])
 
 
-def chip_of(z, k):
-    return rem(z + jnp.where(k == 1, 3, jnp.where(k == 0, 0, k - 1)), 4)
-
-
-def sums_send(k, zz, partial, c, own, sibout, sibin, out, inn, sbs, sbr, rss, rsr):
-    sibout[k] = partial(2 * zz + 1 - c).astype(BF)
-    send(sibout.at[k], sibin.at[k], sbs.at[k], sbr.at[k], c=1 - c)
-    term = partial(2 * zz + c)
-    landed(sibin.at[k], sbr.at[k])
-    term = term + sibin[k].astype(F32)
-
+def rows_before(k, buf, z, c, ss, rs):
     @pl.when(k == 0)
     def _():
-        own[...] = term
-
-    @pl.when(k > 0)
-    def _():
-        out[k - 1] = term.astype(BF)
-        send(out.at[k - 1], inn.at[k - 1], rss.at[k - 1], rsr.at[k - 1], z=zz)
+        landed(buf.at[2 * z + 1 - c], rs.at[0])
+
+    @pl.when((k == 1) & (c == 0))
+    def _():
+        rows_pass(buf, z, c, ss, rs)
+        rows_near(buf, z, c, ss, rs)
+
+    @pl.when((k == 2) & (c == 1))
+    def _():
+        rows_near(buf, z, c, ss, rs)
+
+    @pl.when(((k == 1) & (c == 1)) | ((k == 2) & (c == 0)))
+    def _():
+        rows_near_in(buf, z, c, rs)
+
+    @pl.when(k == 3)
+    def _():
+        @pl.when(c == 1)
+        def _():
+            rows_far(buf, z, c, ss, rs)
+
+        landed(buf.at[slot_of(z, 1 - c, 2)], rs.at[9])
+
+
+def rows_midway(k, buf, z, c, ss, rs):
+    @pl.when((k == 0) & (c == 1))
+    def _():
+        rows_send(buf, z, c, ss, rs)
+
+    @pl.when((k == 1) & (c == 1))
+    def _():
+        rows_pass(buf, z, c, ss, rs)
+
+    @pl.when((k == 2) & (c == 0))
+    def _():
+        rows_far(buf, z, c, ss, rs)
+
+
+def slots(k, z):
+    near = (k == 1) | (k == 2)
+    chip = rem(z + jnp.where(k == 3, 2, 0), 4)
+    first = jnp.where(near, 2 * rem(z + 3, 4) + k - 1, 2 * chip)
+    second = jnp.where(near, 2 * rem(z + 1, 4) + k - 1, 2 * chip + 1)
+    return near, first, second
+
+
+def sums_send(k, z, c, partial, own, sibout, sibin, out, inn, sbs, sbr, rss, rsr):
+    near, first, second = slots(k, z)
+    far = jnp.where(k == 0, 0, 1)
+    mine = near & (c == k - 1)
+    base = first - jnp.where(near, 0, rem(first, 2))
+    t0 = partial(jnp.where(near, first, base + 1 - c))
+    m0 = jnp.where(near, 2, far)
+
+    @pl.when(jnp.logical_not(mine))
+    def _():
+        sibout[m0] = t0.astype(BF)
+        send(sibout.at[m0], sibin.at[m0], sbs.at[m0], sbr.at[m0], c=1 - c)
+
+    @pl.when(mine)
+    def _():
+        landed(sibin.at[2], sbr.at[2])
+        out[0] = (t0 + sibin[2].astype(F32)).astype(BF)
+        send(out.at[0], inn.at[0], rss.at[0], rsr.at[0], z=rem(z + 3, 4))
+
+    t1 = partial(jnp.where(near, second, base + c))
+    theirs = near & (c != k - 1)
+
+    @pl.when(theirs)
+    def _():
+        sibout[3] = t1.astype(BF)
+        send(sibout.at[3], sibin.at[3], sbs.at[3], sbr.at[3], c=1 - c)
+
+    @pl.when(jnp.logical_not(theirs))
+    def _():
+        m1 = jnp.where(near, 3, far)
+        landed(sibin.at[m1], sbr.at[m1])
+        both = t1 + sibin[m1].astype(F32)
+
+        @pl.when(k == 0)
+        def _():
+            own[...] = both
+
+        @pl.when(k != 0)
+        def _():
+            o = jnp.where(near, 1, 2)
+            out[o] = both.astype(BF)
+            send(out.at[o], inn.at[o], rss.at[o], rsr.at[o], z=rem(z + jnp.where(near, 1, 2), 4))
 
 
 def sums_total(own, inn, rsr):
@@ -321,31 +490,50 @@
     return cos, sin, t[:, 64:65]
 
 
-def forward_pass(l, z, c, x, vec, bins, w1, w2, tabs, nall, qkv, prob, a2, pre, raw, sums, rows, spill):
+def expand(t):
+    lane = lanes(t.shape)
+    rot = rem(lane, 64) < ROT
+    first = lane < 64
+    cos = jnp.where(rot, jnp.where(first, t, pltpu.roll(t, 64, 1)), 1.0)
+    sin = jnp.where(rot, jnp.where(first, pltpu.roll(t, 96, 1), pltpu.roll(t, 32, 1)), 0.0)
+    return cos, sin, t[:, 64:65]
+
+
+def normed_rows(l, x, vec):
+    centre, r = stats(x[...])
+    return (centre * r * vec[8 * l : 8 * l + 1, :] + vec[8 * l + 1 : 8 * l + 2, :]).astype(BF)
+
+
+def forward_pass(
+    l, z, c, x, vec, bins, w1, w2, tabs, nall, qkv, prob, a2, pre, raw, sums, rows, spill, early, hook
+):
     ss, rs = rows
-    centre, r = stats(x[...])
     row = 8 * l
-    nall[2 * z + c] = (centre * r * vec[row : row + 1, :] + vec[row + 1 : row + 2, :]).astype(BF)
-    rows_start(nall, z, c, ss, rs)
-
-    def step(k):
-        zz = chip_of(z, k)
-        rows_ready(k, nall, z, c, ss, rs)
-        two = pl.ds(2 * zz, 2)
-        n = nall[two].reshape(2 * CAP, D)
+
+    def step(i):
+        k = jnp.where(i == 0, 3, jnp.where(i == 3, 0, i)) if early else i
+        hook(i)
+        if not early:
+            rows_before(k, nall, z, c, ss, rs)
+        _, sa, sb = slots(k, z)
+        n = jnp.concatenate([nall[sa], nall[sb]], axis=0)
         raw[:, 0:QKV] = nn(n, w1[:, :QKV])
-        pre[two] = (nn(n, w1[:, QKV:]) + bins[row : row + 1, :]).reshape(2, CAP, HID)
+        val = nn(n, w1[:, QKV:]) + bins[row : row + 1, :]
+        pre[sa] = val[:CAP]
+        pre[sb] = val[CAP:]
 
         def act(i):
             u, t = div(i, 6), rem(i, 6)
+            s = jnp.where(u == 0, sa, sb)
             at = pl.ds(pl.multiple_of(t * 32, 32), 32)
-            v = pre[2 * zz + u, at, :]
+            v = pre[s, at, :]
             g = 0.5 * v * (1.0 + jnp.tanh(C0 * (v + C1 * v * v * v)))
-            a2[2 * zz + u, at, 128:] = g.astype(BF)
+            a2[s, at, 128:] = g.astype(BF)
 
         loop(12, act)
-        for u in range(2):
-            s = 2 * zz + u
+        if not early:
+            rows_midway(k, nall, z, c, ss, rs)
+        for u, s in enumerate((sa, sb)):
             at = slice(u * CAP, (u + 1) * CAP)
             cos, sin, start = expand(tabs[s])
             q = turn(raw[at, 0:128], cos, sin).astype(BF)
@@ -370,9 +558,11 @@
             a2[s, :, 0:128] = jnp.where(head, mixed[0], mixed[1]).astype(BF)
         if spill is not None:
             prob_o, pre_o, sem = spill
-            local(prob.at[pl.ds(4 * zz, 4)], prob_o.at[pl.ds(4 * zz, 4)], sem.at[k, 0])
-            local(pre.at[two], pre_o.at[two], sem.at[k, 1])
-        sums_send(k, zz, lambda s: nn(a2[s], w2[...]), c, *sums)
+            for u, s in enumerate((sa, sb)):
+                local(prob.at[pl.ds(2 * s, 2)], prob_o.at[pl.ds(2 * s, 2)], sem.at[k, 0, u])
+                local(pre.at[s], pre_o.at[s], sem.at[k, 1, u])
+        hook(i, 1)
+        sums_send(k, z, c, lambda s: nn(a2[s], w2[...]), *sums)
 
     loop(4, step)
     own, _, _, out, inn, _, _, rss, rsr = sums
@@ -385,28 +575,34 @@
 ):
     ss, rs = rows
     gall[2 * z + c] = g_ref[...].astype(BF)
-    rows_start(gall, z, c, ss, rs)
+    rows_sibling(gall, z, c, ss, rs)
+
+    @pl.when(c == 0)
+    def _():
+        rows_send(gall, z, c, ss, rs)
+
     hook(0)
 
     def step(k):
-        zz = chip_of(z, k)
-        rows_ready(k, gall, z, c, ss, rs)
-        two = pl.ds(2 * zz, 2)
-        g = gall[two].reshape(2 * CAP, D)
+        hook(k, 1)
+        rows_before(k, gall, z, c, ss, rs)
+        _, sa, sb = slots(k, z)
+        g = jnp.concatenate([gall[sa], gall[sb]], axis=0)
         raw[...] = nt(g, w2[...])
 
         def act(i):
             u, t = div(i, 12), rem(i, 12)
+            s = jnp.where(u == 0, sa, sb)
             at = pl.ds(pl.multiple_of(t * 16, 16), 16)
-            v = pre[2 * zz + u, at, :]
+            v = pre[s, at, :]
             d = raw[pl.ds(pl.multiple_of(u * CAP + t * 16, 16), 16), 128:]
             t1 = jnp.tanh(C0 * (v + C1 * v * v * v))
             slope = 0.5 * (1.0 + t1) + 0.5 * v * (1.0 - t1 * t1) * (C0 + (3.0 * C0 * C1) * v * v)
-            dp[2 * zz + u, at, QKV:] = (d * slope).astype(BF)
+            dp[s, at, QKV:] = (d * slope).astype(BF)
 
         loop(24, act)
-        for u in range(2):
-            s = 2 * zz + u
+        rows_midway(k, gall, z, c, ss, rs)
+        for u, s in enumerate((sa, sb)):
             at = slice(u * CAP, (u + 1) * CAP)
             cos, sin, _ = expand(tabs[s])
             m = raw[at, 0:128].astype(BF)
@@ -429,10 +625,10 @@
             dp[s, :, 0:128] = turn(dq, cos, -sin).astype(BF)
             dp[s, :, 128:256] = turn(dk, cos, -sin).astype(BF)
             dp[s, :, 256:384] = (dv[0] + dv[1]).astype(BF)
-        sums_send(k, zz, lambda s: nt(dp[s], w1[...]), c, *sums)
+        sums_send(k, z, c, lambda s: nt(dp[s], w1[...]), *sums)
 
     loop(4, step)
-    hook(1)
+    hook(4)
 
     rows = LINE * CAP
     g = gall[...].reshape(rows, D)
@@ -442,7 +638,7 @@
             g2[s, q, 0:16, :] = val[64 * s + 16 * q : 64 * s + 16 * q + 16].astype(BF)
             base = 128 + 256 * s + 64 * q
             g2[s, q, 16:80, :] = val[base : base + 64].astype(BF)
-    hook(2)
+    hook(5)
     d = dp[...].reshape(rows, WIDE)
     for t in range(2):
         val = tn(nall[:, :, t * 512 : (t + 1) * 512].reshape(rows, 512), d).astype(BF)
@@ -454,7 +650,7 @@
                 at = (2 * zz + cc) * 16
                 g1q[hh, q, at : at + 16, :] = part[:, :QKV]
                 g1i[hh, q, at : at + 16, :] = part[:, QKV:]
-    hook(3)
+    hook(6)
 
     zero = jnp.zeros((1, 128), F32)
     col = pl.ds(pl.multiple_of((2 * z + c) * 128, 128), 128)
@@ -529,68 +725,82 @@
     send(tot.at[l, c], tot.at[l, c], s8.at[l], q8.at[l], c=1 - c)
 
 
-def second_start(l, me, g2, r2, s2, q2):
-    y, xl, z, xh, c, x, p, j = me
-
-    def second(i):
-        yy, cc = rem(y + div(i, 2), 4), rem(xl + rem(i, 2), 2)
-        src, dst = g2.at[cc, yy], r2.at[l, p]
-        here = (i == 0) & (xh == c)
-
-        @pl.when(here)
-        def _():
-            local(src, dst, q2.at[l, p])
-
-        @pl.when(jnp.logical_not(here))
-        def _():
-            send(src, dst, s2.at[l, i], q2.at[l, p], y=yy, xl=cc, xh=c)
-
-    loop(8, second)
-
-
-def first_start(l, me, g1q, g1i, r1, s1, q1):
-    y, xl, z, xh, c, x, p, j = me
-
-    def first(k):
-        yy = rem(y + div(k, 4), 4)
-        xx = rem(x + rem(k, 4), 4)
-        hh, ll = div(xx, 2), rem(xx, 2)
-
-        @pl.when(ll == 0)
-        def _():
-            dst = r1.at[l, p, :, pl.ds(0, QKV)]
-            send(g1q.at[hh, yy], dst, s1.at[l, k], q1.at[l, p], y=yy, xh=hh, xl=ll)
-
-        @pl.when(ll == 1)
-        def _():
-            send(g1i.at[hh, yy], r1.at[l, p], s1.at[l, k], q1.at[l, p], y=yy, xh=hh, xl=ll)
-
-    loop(15, lambda k: first(k + 1))
-
-    @pl.when(xl == 0)
-    def _():
-        local(g1q.at[xh, y], r1.at[l, p, :, pl.ds(0, QKV)], q1.at[l, p])
-
-    @pl.when(xl == 1)
-    def _():
-        local(g1i.at[xh, y], r1.at[l, p], q1.at[l, p])
-
-
-def second_sum(l, me, r2, red2, fo, ff, q2, s4, q4):
+def second_p1(l, me, g2, ga1, gb1, s, q):
+    y, xl, z, xh, c, x, p, j = me
+    left, right = pl.ds(0, 512), pl.ds(512, 512)
+    for d in (1, 2, 3):
+        dev = along_x(x, d)
+
+        @pl.when(dev["xh"] == c)
+        def _():
+            send(
+                g2.at[dev["xl"], :, :, left], ga1.at[l, d - 1], s.at[l, 0, d], q.at[l, 0, d], **dev
+            )
+
+        yy = along_y(y, d)
+        send(g2.at[:, yy["y"], :, right], gb1.at[l, d - 1], s.at[l, 1, d], q.at[l, 1, d], **yy)
+
+
+def second_p2(l, me, g2, ga1, gb1, ga2, gb2, sga, sgb, s, q):
+    y, xl, z, xh, c, x, p, j = me
+    for d in (1, 2, 3):
+        landed(gb1.at[l, d - 1], q.at[l, 1, d])
+
+    def add_right(i):
+        h, t = div(i, 5), rem(i, 5)
+        at = pl.ds(pl.multiple_of(16 * t, 16), 16)
+        acc = g2[h, y, at, 512:].astype(F32)
+        for d in range(3):
+            acc = acc + gb1[l, d, h, at, :].astype(F32)
+        sgb[h, at, :] = acc.astype(BF)
+
+    loop(10, add_right)
+    for d in (1, 2, 3):
+        dev = along_x(x, d)
+
+        @pl.when(dev["xh"] == c)
+        def _():
+            send(sgb.at[dev["xl"]], gb2.at[l, d - 1], s.at[l, 2, d], q.at[l, 2, d], **dev)
+
+    @pl.when(xh == c)
+    def _():
+        for d in (1, 2, 3):
+            landed(ga1.at[l, d - 1], q.at[l, 0, d])
+
+        def add_left(i):
+            yy, t = div(i, 5), rem(i, 5)
+            at = pl.ds(pl.multiple_of(16 * t, 16), 16)
+            acc = g2[xl, yy, at, 0:512].astype(F32)
+            for d in range(3):
+                acc = acc + ga1[l, d, yy, at, :].astype(F32)
+            sga[yy, at, :] = acc.astype(BF)
+
+        loop(20, add_left)
+        for d in (1, 2, 3):
+            yy = along_y(y, d)
+            send(sga.at[yy["y"]], ga2.at[l, d - 1], s.at[l, 3, d], q.at[l, 3, d], **yy)
+
+
+def second_p3(l, me, ga2, gb2, sga, sgb, red2, fo, ff, s, q, s4, q4):
     y, xl, z, xh, c, x, p, j = me
     row16 = pl.ds(pl.multiple_of(16 * y, 16), 16)
     row64 = pl.ds(pl.multiple_of(64 * y, 64), 64)
 
     @pl.when(xh == c)
     def _():
-        loop(16, lambda q: landed(r2.at[l, q], q2.at[l, q]))
+        for d in (1, 2, 3):
+            landed(gb2.at[l, d - 1], q.at[l, 2, d])
+            landed(ga2.at[l, d - 1], q.at[l, 3, d])
 
         def add(t):
             at = pl.ds(pl.multiple_of(16 * t, 16), 16)
-            acc = r2[l, 0, at, :].astype(F32)
-            for q in range(1, 16):
-                acc = acc + r2[l, q, at, :].astype(F32)
-            red2[l, at, :] = acc.astype(BF)
+            a = sga[y, at, :].astype(F32)
+            b = sgb[xl, at, :].astype(F32)
+            for d in range(3):
+                a = a + ga2[l, d, at, :].astype(F32)
+                b = b + gb2[l, d, at, :].astype(F32)
+            red2[l, at, 0:512] = a.astype(BF)
+            red2[l, at, 512:1024] = b.astype(BF)
 
         loop(5, add)
 
@@ -614,29 +824,127 @@
         loop(8, out)
 
 
-def first_sum(l, me, r1, red1, fq, fi, q1, s3, q3):
-    y, xl, z, xh, c, x, p, j = me
-    row16 = pl.ds(pl.multiple_of(16 * y, 16), 16)
-
-    def arrive(q):
-        @pl.when(xl == 0)
-        def _():
-            landed(r1.at[l, q, :, pl.ds(0, QKV)], q1.at[l, q])
-
-        @pl.when(xl == 1)
-        def _():
-            landed(r1.at[l, q], q1.at[l, q])
-
-    loop(16, arrive)
+def second_left(l, me, g2, sga, sgb, s):
+    y, xl, z, xh, c, x, p, j = me
+    left, right = pl.ds(0, 512), pl.ds(512, 512)
+    for d in (1, 2, 3):
+        landed(g2.at[:, 0, :, right], s.at[l, 1, d])
+
+        @pl.when(along_x(x, d)["xh"] == c)
+        def _():
+            landed(g2.at[0, :, :, left], s.at[l, 0, d])
+            landed(sgb.at[0], s.at[l, 2, d])
+
+        @pl.when(xh == c)
+        def _():
+            landed(sga.at[0], s.at[l, 3, d])
+
+
+def by_kind(ll, f):
+    @pl.when(ll == 0)
+    def _():
+        f(pl.ds(0, QKV), 0)
+
+    @pl.when(ll == 1)
+    def _():
+        f(pl.ds(0, HID), 1)
+
+
+TOP, LOW = pl.ds(0, 64), pl.ds(64, 64)
+
+
+def first_p1(l, me, g1q, g1i, ra1, rbq, rbi, s, q):
+    y, xl, z, xh, c, x, p, j = me
+    for d in (1, 2, 3):
+        dev = along_x(x, d)
+        hh = dev["xh"]
+
+        def go(cols, kind):
+            src = (g1q, g1i)[kind].at[hh, :, TOP]
+            send(src, ra1.at[l, d - 1, :, :, cols], s.at[l, 0, d], q.at[l, 0, d], **dev)
+
+        by_kind(dev["xl"], go)
+        yy = along_y(y, d)
+        send(g1q.at[:, yy["y"], LOW], rbq.at[l, d - 1], s.at[l, 1, d], q.at[l, 1, d], **yy)
+        send(g1i.at[:, yy["y"], LOW], rbi.at[l, d - 1], s.at[l, 2, d], q.at[l, 2, d], **yy)
+
+
+def first_p2(l, me, g1q, g1i, ra1, rbq, rbi, ra2, rb2, sra, sbq, sbi, s, q):
+    y, xl, z, xh, c, x, p, j = me
+    for d in (1, 2, 3):
+        by_kind(xl, lambda cols, kind: landed(ra1.at[l, d - 1, :, :, cols], q.at[l, 0, d]))
+
+    def add_top(i):
+        yy, t = div(i, 4), rem(i, 4)
+        at = pl.ds(pl.multiple_of(16 * t, 16), 16)
+
+        def go(cols, kind):
+            acc = (g1q, g1i)[kind][xh, yy, at, :].astype(F32)
+            for d in range(3):
+                acc = acc + ra1[l, d, yy, at, cols].astype(F32)
+            sra[yy, at, cols] = acc.astype(BF)
+
+        by_kind(xl, go)
+
+    loop(16, add_top)
+    for d in (1, 2, 3):
+        yy = along_y(y, d)
+
+        def go(cols, kind):
+            src = sra.at[yy["y"], :, cols]
+            send(src, ra2.at[l, d - 1, :, cols], s.at[l, 3, d], q.at[l, 3, d], **yy)
+
+        by_kind(xl, go)
+    for d in (1, 2, 3):
+        landed(rbq.at[l, d - 1], q.at[l, 1, d])
+        landed(rbi.at[l, d - 1], q.at[l, 2, d])
+
+    def add_low(i):
+        h, t = div(i, 4), rem(i, 4)
+        at = pl.ds(pl.multiple_of(16 * t, 16), 16)
+        here = pl.ds(pl.multiple_of(64 + 16 * t, 16), 16)
+        a = g1q[h, y, here, :].astype(F32)
+        b = g1i[h, y, here, :].astype(F32)
+        for d in range(3):
+            a = a + rbq[l, d, h, at, :].astype(F32)
+            b = b + rbi[l, d, h, at, :].astype(F32)
+        sbq[h, at, :] = a.astype(BF)
+        sbi[h, at, :] = b.astype(BF)
+
+    loop(8, add_low)
+    for d in (1, 2, 3):
+        dev = along_x(x, d)
+        hh = dev["xh"]
+
+        def go(cols, kind):
+            src = (sbq, sbi)[kind].at[hh]
+            send(src, rb2.at[l, d - 1, :, cols], s.at[l, 4, d], q.at[l, 4, d], **dev)
+
+        by_kind(dev["xl"], go)
+
+
+def first_p3(l, me, ra2, rb2, sra, sbq, sbi, red1, fq, fi, s, q, s3, q3):
+    y, xl, z, xh, c, x, p, j = me
+    for d in (1, 2, 3):
+        by_kind(xl, lambda cols, kind: landed(ra2.at[l, d - 1, :, cols], q.at[l, 3, d]))
+        by_kind(xl, lambda cols, kind: landed(rb2.at[l, d - 1, :, cols], q.at[l, 4, d]))
 
     def add(t):
         at = pl.ds(pl.multiple_of(16 * t, 16), 16)
-        acc = r1[l, 0, at, :].astype(F32)
-        for q in range(1, 16):
-            acc = acc + r1[l, q, at, :].astype(F32)
-        red1[l, at, :] = acc.astype(BF)
-
-    loop(8, add)
+
+        def go(cols, kind):
+            a = sra[y, at, cols].astype(F32)
+            b = (sbq, sbi)[kind][xh, at, :].astype(F32)
+            for d in range(3):
+                a = a + ra2[l, d, at, cols].astype(F32)
+                b = b + rb2[l, d, at, cols].astype(F32)
+            red1[l, at, cols] = a.astype(BF)
+            red1[l, pl.ds(pl.multiple_of(64 + 16 * t, 16), 16), cols] = b.astype(BF)
+
+        by_kind(xl, go)
+
+    loop(4, add)
+    row16 = pl.ds(pl.multiple_of(16 * y, 16), 16)
 
     def back(jj):
         at = pl.ds(pl.multiple_of(16 * jj, 16), 16)
@@ -662,6 +970,17 @@
             move(red1.at[l, at], fi.at[l, row16, cols], 0)
 
     loop(LINE, back)
+
+
+def first_left(l, me, g1q, g1i, sra, sbq, sbi, s):
+    y, xl, z, xh, c, x, p, j = me
+    for d in (1, 2, 3):
+        there = along_x(x, d)["xl"]
+        by_kind(there, lambda cols, kind: landed((g1q, g1i)[kind].at[0, :, TOP], s.at[l, 0, d]))
+        landed(g1q.at[:, 0, LOW], s.at[l, 1, d])
+        landed(g1i.at[:, 0, LOW], s.at[l, 2, d])
+        by_kind(xl, lambda cols, kind: landed(sra.at[0, :, cols], s.at[l, 3, d]))
+        by_kind(there, lambda cols, kind: landed((sbq, sbi)[kind].at[0], s.at[l, 4, d]))
 
 
 def first_share(l, me, fq, fi, q3, s7, q7):
@@ -706,34 +1025,6 @@
                 landed(f.at[l, pl.ds(16 * q, 16)], q7.at[l, q, v])
 
 
-def first_left(l, me, r1, s1):
-    x = me[5]
-
-    def go(k):
-        ll = rem(rem(x + rem(k, 4), 4), 2)
-
-        @pl.when(ll == 0)
-        def _():
-            landed(r1.at[l, 0, :, pl.ds(0, QKV)], s1.at[l, k])
-
-        @pl.when(ll == 1)
-        def _():
-            landed(r1.at[l, 0], s1.at[l, k])
-
-    loop(15, lambda k: go(k + 1))
-
-
-def second_left(l, me, r2, s2):
-    y, xl, z, xh, c, x, p, j = me
-
-    def go(i):
-        @pl.when(jnp.logical_not((i == 0) & (xh == c)))
-        def _():
-            landed(r2.at[l, 0], s2.at[l, i])
-
-    loop(8, go)
-
-
 def owners_left(l, me, lns, ps, tot, red1, red2, fq, fi, s3, s4, s5, s6, s7, s8):
     y, xl, z, xh, c, x, p, j = me
     row16 = pl.ds(pl.multiple_of(16 * y, 16), 16)
@@ -769,6 +1060,10 @@
 
     loop(7, lambda i: left_share(i + 1))
     landed(tot.at[l, c], s8.at[l])
+
+
+def no_hook(*a):
+    pass
 
 
 def whole_kernel(
@@ -777,8 +1072,9 @@
     w1, w2, sma, tabs, vec, bins,
     nall, qkv, a2, prob, pre, raw, gall, dp, x1,
     own, sibout, sibin, out, inn,
-    g1q, g1i, g2, lns, loc, r1, r2, red1, red2, zs, ps, tot,
-    cs, cr, as_, ar, bs, br, ts, tr, ms, mr, ns, nr,
+    g1q, g1i, g2, lns, loc, ga1, gb1, ga2, gb2, sga, sgb, ra1, rbq, rbi, ra2, rb2, sra, sbq, sbi,
+    red1, red2, zs, ps, tot,
+    as_, ar, bs, br, cs, cr, xs, xr, ys, yr, ts, tr, ms, mr, ns, nr,
     rows_s, rows_r, sbs, sbr, rss, rsr, spill, fill,
     s1, q1, s2, q2, s3, q3, s4, q4, s5, q5, s6, q6, s7, q7, s8, q8,
 ):
@@ -810,19 +1106,18 @@
 
         loop(LINE, to)
 
-    for l in range(LAYERS):
-        gather_start(l, me, wqkv, win, wo, wfc, w1, w2, cs, cr, as_, ar)
+    weights_z(0, me, wqkv, win, wo, wfc, w1, w2, as_, ar, cs, cr)
+    landed(sma.at[p], mr)
+
+    def small_out(k):
+        send(sma.at[p], sma.at[p], ns.at[k], nr.at[p], **plane_member(y, x, k))
+
+    loop(15, lambda k: small_out(k + 1))
+    weights_p1(0, me, w1, ar, bs, br)
     for k in range(1, LINE):
         jj = rem(j + k, LINE)
         send(tab, tabs.at[j], ts.at[k], tr.at[j], **member(jj))
     local(tab, tabs.at[j], tr.at[j])
-    landed(sma.at[p], mr)
-
-    def small_out(k):
-        send(sma.at[p], sma.at[p], ns.at[k], nr.at[p], **plane_member(y, x, k))
-
-    loop(15, lambda k: small_out(k + 1))
-    gather_plane(0, me, w1, ar, bs, br)
 
     def small_in(k):
         q = rem(p + k, 16)
@@ -849,90 +1144,159 @@
         rows_left(buf, rows_s.at[n])
         sums_left(sibout, out, sbs.at[n], rss.at[n])
 
+    n0 = nall.at[0]
+    ss, rs = rows_of(0)
+    n0[2 * z + c] = normed_rows(0, x0, vec)
+    rows_sibling(n0, z, c, ss, rs)
+    rows_send(n0, z, c, ss, rs)
+    weights_p2(0, me, w1, bs, br)
+    weights_f1(0, me, w2, cr, xs, xr)
+    rows_pass(n0, z, c, ss, rs)
+    weights_f2(0, me, w2, xr, ys, yr)
+    rows_near(n0, z, c, ss, rs)
+    rows_far(n0, z, c, ss, rs)
+    landed(n0.at[2 * z + 1 - c], rs.at[0])
+    rows_near_in(n0, z, c, rs)
     loop(LINE, lambda k: landed(tabs.at[k], tr.at[k]))
-    gather_wait(0, me, w1, w2, cr, br)
-    gather_plane(1, me, w1, ar, bs, br)
+    weights_in1(0, me, w1, br)
+    landed(n0.at[slot_of(z, 1 - c, 2)], rs.at[9])
+    weights_z(1, me, wqkv, win, wo, wfc, w1, w2, as_, ar, cs, cr)
+
+    def hook_f0(i, late=0):
+        if late:
+
+            @pl.when(i == 0)
+            def _():
+                weights_in2(0, me, w2, cr, yr)
+
+        else:
+
+            @pl.when(i == 1)
+            def _():
+                weights_p1(1, me, w1, ar, bs, br)
+
+            @pl.when(i == 2)
+            def _():
+                weights_f1(1, me, w2, cr, xs, xr)
+                weights_p2(1, me, w1, bs, br)
+
+            @pl.when(i == 3)
+            def _():
+                weights_f2(1, me, w2, xr, ys, yr)
+
     x1[...] = forward_pass(
-        0, z, c, x0, vec, bins, w1.at[0], w2.at[0], tabs, nall.at[0], qkv.at[0], prob, a2.at[0], pre,
-        raw, sums_of(0), rows_of(0), (prob_o, pre_o, spill),
+        0, z, c, x0, vec, bins, w1.at[0], w2.at[0], tabs, n0, qkv.at[0], prob, a2.at[0], pre,
+        raw, sums_of(0), rows_of(0), (prob_o, pre_o, spill), True, hook_f0,
     )
-    done(0, nall.at[0])
+
+    n1 = nall.at[1]
+    ss, rs = rows_of(1)
+    n1[2 * z + c] = normed_rows(1, x1, vec)
+    rows_sibling(n1, z, c, ss, rs)
+
+    @pl.when(c == 0)
+    def _():
+        rows_send(n1, z, c, ss, rs)
+
+    done(0, n0)
     for k in range(4):
-        landed(prob.at[pl.ds(0, 4)], spill.at[k, 0])
-        landed(pre.at[pl.ds(0, 2)], spill.at[k, 1])
-    gather_wait(1, me, w1, w2, cr, br)
+        for u in range(2):
+            landed(prob.at[pl.ds(0, 2)], spill.at[k, 0, u])
+            landed(pre.at[0], spill.at[k, 1, u])
+    weights_in1(1, me, w1, br)
+    weights_in2(1, me, w2, cr, yr)
     x2_ref[...] = forward_pass(
-        1, z, c, x1, vec, bins, w1.at[1], w2.at[1], tabs, nall.at[1], qkv.at[1], prob, a2.at[1], pre,
-        raw, sums_of(1), rows_of(1), None,
+        1, z, c, x1, vec, bins, w1.at[1], w2.at[1], tabs, n1, qkv.at[1], prob, a2.at[1], pre,
+        raw, sums_of(1), rows_of(1), None, False, no_hook,
     )
-    done(1, nall.at[1])
+    done(1, n1)
+
     g0_ref[...] = cot[...] * tab[:, 96:97]
 
-    def hook1(n):
-        if n == 1:
+    def hook1(n, inside=0):
+        if inside:
+            return
+        if n == 4:
             local(prob_o, prob, fill.at[0])
             local(pre_o, pre, fill.at[1])
-        if n == 2:
-            second_start(1, me, g2, r2, s2, q2)
-        if n == 3:
-            first_start(1, me, g1q, g1i, r1, s1, q1)
+        if n == 5:
+            second_p1(1, me, g2, ga1, gb1, s2, q2)
+        if n == 6:
+            first_p1(1, me, g1q, g1i, ra1, rbq, rbi, s1, q1)
 
     g0_ref[...] = backward_pass(
-        1, z, c, g0_ref, x1, vec, w1.at[1], w2.at[1], tabs, nall.at[1], qkv.at[1], prob, a2.at[1], pre,
+        1, z, c, g0_ref, x1, vec, w1.at[1], w2.at[1], tabs, n1, qkv.at[1], prob, a2.at[1], pre,
         raw, gall.at[1], dp, g1q, g1i, g2, lns.at[1], loc.at[1], sums_of(2), rows_of(2), hook1,
     )
+    small_start(1, me, lns, zs, s5, q5)
     done(2, gall.at[1])
-    small_start(1, me, lns, zs, s5, q5)
-
-    def hook0(n):
+
+    def hook0(n, inside=0):
+        if inside:
+
+            @pl.when(n == 1)
+            def _():
+                small_spread(1, me, lns, loc, zs, ps, q5, s6, q6)
+
+            @pl.when(n == 2)
+            def _():
+                second_p2(1, me, g2, ga1, gb1, ga2, gb2, sga, sgb, s2, q2)
+                first_p2(1, me, g1q, g1i, ra1, rbq, rbi, ra2, rb2, sra, sbq, sbi, s1, q1)
+
+            @pl.when(n == 3)
+            def _():
+                second_p3(1, me, ga2, gb2, sga, sgb, red2, fo, ff, s2, q2, s4, q4)
+                first_p3(1, me, ra2, rb2, sra, sbq, sbi, red1, fq, fi, s1, q1, s3, q3)
+
+            return
         if n == 0:
             landed(prob, fill.at[0])
             landed(pre, fill.at[1])
-        if n == 1:
-            small_spread(1, me, lns, loc, zs, ps, q5, s6, q6)
-            second_sum(1, me, r2, red2, fo, ff, q2, s4, q4)
-            second_left(1, me, r2, s2)
-        if n == 2:
-            second_start(0, me, g2, r2, s2, q2)
-            first_sum(1, me, r1, red1, fq, fi, q1, s3, q3)
-            first_left(1, me, r1, s1)
-        if n == 3:
-            first_start(0, me, g1q, g1i, r1, s1, q1)
+        if n == 4:
+            second_left(1, me, g2, sga, sgb, s2)
+            first_left(1, me, g1q, g1i, sra, sbq, sbi, s1)
+            first_share(1, me, fq, fi, q3, s7, q7)
+        if n == 5:
+            second_p1(0, me, g2, ga1, gb1, s2, q2)
+        if n == 6:
+            first_p1(0, me, g1q, g1i, ra1, rbq, rbi, s1, q1)
 
     g0_ref[...] = backward_pass(
-        0, z, c, g0_ref, x0, vec, w1.at[0], w2.at[0], tabs, nall.at[0], qkv.at[0], prob, a2.at[0], pre,
+        0, z, c, g0_ref, x0, vec, w1.at[0], w2.at[0], tabs, n0, qkv.at[0], prob, a2.at[0], pre,
         raw, gall.at[0], dp, g1q, g1i, g2, lns.at[0], loc.at[0], sums_of(3), rows_of(3), hook0,
     )
     small_start(0, me, lns, zs, s5, q5)
+    second_p2(0, me, g2, ga1, gb1, ga2, gb2, sga, sgb, s2, q2)
+    first_p2(0, me, g1q, g1i, ra1, rbq, rbi, ra2, rb2, sra, sbq, sbi, s1, q1)
+    small_spread(0, me, lns, loc, zs, ps, q5, s6, q6)
+    second_p3(0, me, ga2, gb2, sga, sgb, red2, fo, ff, s2, q2, s4, q4)
+    first_p3(0, me, ra2, rb2, sra, sbq, sbi, red1, fq, fi, s1, q1, s3, q3)
+    small_last(1, me, ps, tot, q6, s8, q8)
+    small_last(0, me, ps, tot, q6, s8, q8)
+    first_share(0, me, fq, fi, q3, s7, q7)
     done(3, gall.at[0])
-    first_share(1, me, fq, fi, q3, s7, q7)
-    small_last(1, me, ps, tot, q6, s8, q8)
-    small_spread(0, me, lns, loc, zs, ps, q5, s6, q6)
-    second_sum(0, me, r2, red2, fo, ff, q2, s4, q4)
-    first_sum(0, me, r1, red1, fq, fi, q1, s3, q3)
-    first_share(0, me, fq, fi, q3, s7, q7)
-    small_last(0, me, ps, tot, q6, s8, q8)
+    second_left(0, me, g2, sga, sgb, s2)
+    first_left(0, me, g1q, g1i, sra, sbq, sbi, s1)
+    for l in range(LAYERS):
+        weights_left(l, me, wqkv, win, wo, wfc, w1, w2, as_, cs, bs, xs, ys)
+    for k in range(1, LINE):
+        landed(tab, ts.at[k])
+    loop(15, lambda k: landed(sma.at[0], ns.at[k + 1]))
+
+    @pl.when(source)
+    def _():
+        def gone(jj):
+            @pl.when(jj != j)
+            def _():
+                landed(sm, ms.at[jj])
+
+        loop(LINE, gone)
+
     for l in (1, 0):
         landed(tot.at[l, 1 - c], q8.at[l])
         fs_ref[l] = tot[l]
         owners_in(l, me, fq, fi, fo, ff, q4, q7)
-    second_left(0, me, r2, s2)
-    first_left(0, me, r1, s1)
-    for l in range(LAYERS):
         owners_left(l, me, lns, ps, tot, red1, red2, fq, fi, s3, s4, s5, s6, s7, s8)
-        gather_left(l, me, wqkv, win, wo, wfc, w1, cs, as_, bs)
-    for k in range(1, LINE):
-        landed(tab, ts.at[k])
-    loop(15, lambda k: landed(sma.at[0], ns.at[k + 1]))
-
-    @pl.when(source)
-    def _():
-        def gone(jj):
-            @pl.when(jj != j)
-            def _():
-                landed(sm, ms.at[jj])
-
-        loop(LINE, gone)
 
 
 def whole(wqkv, win, wo, wfc, sm, tab, x0, cot):
@@ -963,16 +1327,21 @@
             VMEM((3, CAP, D), BF), VMEM((3, CAP, D), BF),
             VMEM((2, 4, 128, QKV), BF), VMEM((2, 4, 128, HID), BF), VMEM((2, 4, 80, D), BF),
             VMEM((n, LINE, 8, 128), F32), VMEM((n, 8, 128), F32),
-            VMEM((n, 16, 128, HID), BF), VMEM((n, 16, 80, D), BF),
+            VMEM((n, 3, 4, 80, 512), BF), VMEM((n, 3, 2, 80, 512), BF),
+            VMEM((n, 3, 80, 512), BF), VMEM((n, 3, 80, 512), BF),
+            VMEM((4, 80, 512), BF), VMEM((2, 80, 512), BF),
+            VMEM((n, 3, 4, 64, HID), BF), VMEM((n, 3, 2, 64, QKV), BF), VMEM((n, 3, 2, 64, HID), BF),
+            VMEM((n, 3, 64, HID), BF), VMEM((n, 3, 64, HID), BF),
+            VMEM((4, 64, HID), BF), VMEM((2, 64, QKV), BF), VMEM((2, 64, HID), BF),
             VMEM((n, 128, HID), BF), VMEM((n, 80, D), BF),
             VMEM((n, LINE, 8, 128), F32), VMEM((n, 16, 8, 128), F32), VMEM((n, 2, 8, 128), F32),
-            DMA((n, 2, 2)), DMA((n, 2, 2)), DMA((LINE, n, 4)), DMA((n, 4)),
-            DMA((n, 16)), DMA((n, 16)), DMA((LINE,)), DMA((LINE,)),
-            DMA((LINE,)), DMA, DMA((16,)), DMA((16,)),
+            DMA((LINE, n, 4)), DMA((n, 4)), DMA((n, 2, 15)), DMA((n, 16, 2)),
+            DMA((n, 2, 2)), DMA((n, 2, 2)), DMA((n, 2, 2)), DMA((n, 2, 2)),
+            DMA((n, 4, 2, 2)), DMA((n, 4, 2, 2)),
+            DMA((LINE,)), DMA((LINE,)), DMA((LINE,)), DMA, DMA((16,)), DMA((16,)),
             DMA((4, 10)), DMA((4, 10)), DMA((4, 4)), DMA((4, 4)), DMA((4, 3)), DMA((4, 3)),
-            DMA((4, 2)), DMA((2,)),
-            DMA((n, 16)), DMA((n, 16)),
-            DMA((n, 8)), DMA((n, 16)),
+            DMA((4, 2, 2)), DMA((2,)),
+            DMA((n, 5, 4)), DMA((n, 5, 4)), DMA((n, 4, 4)), DMA((n, 4, 4)),
             DMA((n, LINE, 3)), DMA((n, LINE, 3)),
             DMA((n, 8, 2)), DMA((n, 4, 2)),
             DMA((n, LINE)), DMA((n, LINE)),

time: 326 us -> 272 us (0.83)
  Pallas kernels: 308 us -> 252 us
    pallas_call x1, Pallas kernels: 308 us -> 252 us  [whole(): pl.pallas_call(whole_kernel, out_shape=(jax.ShapeDtypeStruct((CAP, D), F3...]
where the time goes in v3:
time: 272 us; the launch traced here: 270 us
  Pallas kernels  252 us (93%)
  other arithmetic  11.7 us (4%)
  local copies, waits for them, and re-layouts  5.55 us (2%)
    pallas_call x1, Pallas kernels, whole(): pl.pallas_call(whole_kernel, out_shape=(jax.ShapeDtypeStruct((CAP, D), F3...  252 us

profile of v3, /device:TPU:32, one launch (start us, length us, event | category | flops | bytes accessed | tf_op | source)
XLA Modules:
  0.0 269.7 jit_solution(16611708418205707327)
XLA Ops:
  0.6 0.8 reduce-window.8
  1.5 0.7 convert_reduce_fusion
  2.2 0.4 multiply_sine_fusion
  2.7 0.1 broadcast_in_dim.4
  2.8 0.1 broadcast_in_dim.5
  2.9 0.8 concatenate.15.tab
  3.7 0.9 maximum_bitcast_fusion
  4.6 0.9 maximum_bitcast_fusion.1
  5.5 0.9 maximum_bitcast_fusion.2
  6.4 0.7 copy.37
  7.1 0.6 bitcast_convert_fusion.sm
  7.7 251.7 %whole.1 = (f32[192,1024]{1,0:T(8,128)}, f32[192,1024]{1,0:T(8,128)}, f32[2,2,8,128]{3,2,1,0:T(8,128)}, bf16[2,64,3072]{2,1,0:T(8,128)(2,1)}, bf16[2,64,4096]{2,...) custom-call(bf16[2,64,3072]{2,1,0:T(8,128)(2,1)} %wqkv.1, ...), custom_call_target="tpu_custom_call" | custom-call | tf_op jit(solution)/shard_map/whole/pallas_call | solution.py:1304
  259.4 0.0 copy-start
  259.4 0.8 dynamic-slice_bitcast_fusion
  260.2 0.6 constant_dynamic-slice_fusion.3
  260.9 0.6 constant_dynamic-slice_fusion.2
  261.5 2.8 %convert_element_type.49 = f32[2,64,4096]{2,1,0:T(8,128)} convert(bf16[2,64,4096]{2,1,0:T(8,128)(2,1)} %get-tuple-element.22) | non-fusion elementwise | flops 524288 | bytes 3145728 | tf_op jit(solution)/shard_map/convert_element_type | solution.py:1394
  264.2 0.0 copy-start.3
  264.2 0.0 copy-done
  264.2 0.0 copy-start.4
  264.2 1.6 convert_element_type.50
  265.8 0.0 copy-start.2
  265.8 0.0 copy-done.3
  265.8 0.0 copy-start.1
  265.8 1.3 convert_element_type.47
  267.1 0.0 copy-done.4
  267.1 0.8 convert_element_type.48
  267.9 0.0 copy-done.2
  267.9 0.9 copy.44
  268.8 0.0 copy-done.1
  268.8 0.9 copy.45
  (11 shorter events, 0.1 us)
Async XLA Ops:
  259.4 4.8 %copy-start = (bf16[2,256,1024]{2,1,0:T(8,128)(2,1)S(1)}, bf16[2,256,1024]{2,1,0:T(8,128)(2,1)}, u32[]{:S(2)}) copy-start(bf16[2,256,1024]{2,1,0:T(8,128)(2,1)} %get-tuple-element.23) | copy-start | bytes 3145732
  264.2 1.6 copy-start.3
  264.2 2.9 %copy-start.4 = (bf16[2,64,1024]{2,1,0:T(8,128)(2,1)S(1)}, bf16[2,64,1024]{2,1,0:T(8,128)(2,1)}, u32[]{:S(2)}) copy-start(bf16[2,64,1024]{2,1,0:T(8,128)(2,1)} %get-tuple-element.21) | copy-start | bytes 786436
  265.8 2.2 copy-start.2
  265.8 3.0 %copy-start.1 = (f32[192,1024]{1,0:T(8,128)S(1)}, f32[192,1024]{1,0:T(8,128)}, u32[]{:S(2)}) copy-start(f32[192,1024]{1,0:T(8,128)} %get-tuple-element.45) | copy-start | bytes 2359300

commit v4 on v3

v4 whole, which is shorter than its diff:
```python
import functools
import math

import jax
import jax.numpy as jnp
from jax import lax
from jax.experimental import pallas as pl
from jax.experimental.pallas import tpu as pltpu
from jax.sharding import Mesh
from jax.sharding import PartitionSpec as P

D = 1024
HEADS = 16
HEAD = 64
ROT = 32
FF = 4096
LAYERS = 2
SLOTS = 4
CAP = 192
LINE = 8
QKV = 384
HID = 512
WIDE = QKV + HID
DEEP = 128 + HID
EPSILON = 1e-05
NEGATIVE = -1e30
AXES = ("y", "xl", "z", "xh", "c")
BF = jnp.bfloat16
F32 = jnp.float32
MESH = pl.DeviceIdType.MESH
VMEM = pltpu.VMEM
DMA = pltpu.SemaphoreType.DMA
ANY = pl.BlockSpec(memory_space=pl.ANY)
INV = pl.BlockSpec(memory_space=pltpu.VMEM)
C0 = 0.7978845608028654
C1 = 0.044715


def div(a, b):
    return lax.div(a, jnp.int32(b))


def rem(a, b):
    return lax.rem(a, jnp.int32(b))


def place():
    y, xl, z, xh, c = (lax.axis_index(a) for a in AXES)
    return y, xl, z, xh, c


def send(src, dst, ss, rs, **dev):
    cp = pltpu.make_async_remote_copy(
        src_ref=src, dst_ref=dst, send_sem=ss, recv_sem=rs, device_id=dev, device_id_type=MESH
    )
    cp.start()


def local(src, dst, sem):
    pltpu.make_async_copy(src, dst, sem).start()


def landed(ref, sem):
    pltpu.make_async_copy(ref, ref, sem).wait()


def loop(n, body):
    lax.fori_loop(0, n, lambda i, _: (body(i), 0)[1], 0)


def signal(sem, **dev):
    pl.semaphore_signal(sem, inc=1, device_id=dev, device_id_type=MESH)


def greet_line(bar, z, c):
    for k in range(1, LINE):
        j = rem(2 * z + c + k, LINE)
        signal(bar, z=div(j, 2), c=rem(j, 2))


def greet_plane(bar, y, x):
    for k in range(1, 16):
        yy = rem(y + k // 4, 4)
        xx = rem(x + k % 4, 4)
        signal(bar, y=yy, xh=div(xx, 2), xl=rem(xx, 2))


def rows64(q):
    return pl.ds(pl.multiple_of(64 * q, 64), 64)


def second_rows(s, y):
    return (
        pl.ds(pl.multiple_of(64 * s + 16 * y, 16), 16),
        pl.ds(pl.multiple_of(128 + 256 * s + 64 * y, 16), 64),
    )


def half_cols(h):
    return pl.ds(pl.multiple_of(512 * h, 512), 512)


PARTS = (pl.ds(QKV, HID), pl.ds(0, QKV))


def weights_z(l, me, wqkv, win, wo, wfc, w1, w2, as_, ar, cs, cr):
    y, xl, z, xh, c, x, p, j = me
    mine = rows64(p)

    @pl.when((z == y) & (c == xl))
    def _():
        def to(jj):
            pairs = []
            for part in range(3):
                cols = pl.ds(pl.multiple_of(part * D + jj * 128, 128), 128)
                pairs.append((wqkv.at[l, :, cols], w1.at[l, mine, pl.ds(part * 128, 128)]))
            cols = pl.ds(pl.multiple_of(jj * HID, HID), HID)
            pairs.append((win.at[l, :, cols], w1.at[l, mine, PARTS[0]]))

            @pl.when(jj == j)
            def _():
                for i, (src, dst) in enumerate(pairs):
                    local(src, dst, ar.at[l])

            @pl.when(jj != j)
            def _():
                for i, (src, dst) in enumerate(pairs):
                    send(src, dst, as_.at[l], ar.at[l], z=div(jj, 2), c=rem(jj, 2))

        loop(LINE, to)

    quarter = (pl.ds(pl.multiple_of(16 * y, 16), 16), pl.ds(pl.multiple_of(64 * y, 64), 64))
    whole_rows = (
        pl.ds(pl.multiple_of(64 * c, 64), 64), pl.ds(pl.multiple_of(128 + 256 * c, 64), 256)
    )
    place_rows = second_rows(c, y)
    for i, w in enumerate((wo, wfc)):
        cols = half_cols(xl)
        dst = w2.at[l, place_rows[i], cols]
        send(
            w.at[l, quarter[i], cols], dst, cs.at[l, 0], cr.at[l], xl=1 - xl, xh=1 - xh, c=xh
        )
        full = w2.at[l, whole_rows[i]]

        @pl.when(c == xh)
        def _():
            local(w.at[l], full, cr.at[l])

        @pl.when(c != xh)
        def _():
            send(w.at[l], full, cs.at[l, 1], cr.at[l], c=xh)


def along_y(y, d):
    return dict(y=rem(y + d, 4))


def along_x(x, d):
    xx = rem(x + d, 4)
    return dict(xh=div(xx, 2), xl=rem(xx, 2))


def plane_member(y, x, k):
    return {**along_y(y, div(k, 4)), **along_x(x, rem(k, 4))}


def pass_block(l, part, q, stage, me, w1, bs, br):
    y, xl, z, xh, c, x, p, j = me
    block = w1.at[l, rows64(q), PARTS[part]]
    for d in (1, 2, 3):
        dev = along_y(y, d) if part == stage else along_x(x, d)
        rs = br.at[l, 3 * part + d] if stage == 0 else br.at[l, 0]
        send(block, block, bs.at[l], rs, **dev)


def weights_p1(l, me, w1, ar, bs, br):
    y, xl, z, xh, c, x, p, j = me
    landed(w1.at[l, rows64(p)], ar.at[l])
    for stage in range(2):
        for part in range(2):
            pass_block(l, part, p, stage, me, w1, bs, br)


def weights_p2(l, me, w1, bs, br):
    y, xl, z, xh, c, x, p, j = me
    for d in (1, 3, 2):
        for part in range(2):
            q = 4 * rem(y + 4 - d, 4) + x if part == 0 else 4 * y + rem(x + 4 - d, 4)
            landed(w1.at[l, rows64(q), PARTS[part]], br.at[l, 3 * part + d])
            pass_block(l, part, q, 1, me, w1, bs, br)


def weights_f1(l, me, w2, cr, xs, xr):
    y, xl, z, xh, c, x, p, j = me

    @pl.when(xh != c)
    def _():
        landed(w2.at[l, pl.ds(0, 80)], cr.at[l])
        for s in range(2):
            for at in second_rows(s, y):
                block = w2.at[l, at, half_cols(1 - xl)]
                send(block, block, xs.at[l], xr.at[l], xl=1 - xl)


def weights_f2(l, me, w2, xr, ys, yr):
    y, xl, z, xh, c, x, p, j = me

    @pl.when(xh != c)
    def _():
        landed(w2.at[l, pl.ds(0, 80)], xr.at[l])
        for s in range(2):
            for at in second_rows(s, y):
                block = w2.at[l, at]
                for d in (1, 2, 3):
                    send(block, block, ys.at[l], yr.at[l], **along_y(y, d))


def weights_in1(l, w1, br):
    landed(w1.at[l, pl.ds(0, 768)], br.at[l, 0])


def weights_in2(l, me, w2, cr, yr):
    y, xl, z, xh, c, x, p, j = me

    @pl.when(xh == c)
    def _():
        landed(w2.at[l], cr.at[l])

    @pl.when(xh != c)
    def _():
        landed(w2.at[l, pl.ds(0, 480)], yr.at[l])


def weights_left(l, me, w1, w2, as_, cs, bs, xs, ys):
    y, xl, z, xh, c, x, p, j = me
    landed(w1.at[l, pl.ds(0, 960)], bs.at[l])
    landed(w2.at[l, pl.ds(0, 80), pl.ds(0, 512)], cs.at[l, 0])

    @pl.when(c != xh)
    def _():
        landed(w2.at[l, pl.ds(0, 320)], cs.at[l, 1])
        landed(w2.at[l, pl.ds(0, 80)], xs.at[l])
        landed(w2.at[l, pl.ds(0, 480)], ys.at[l])

    @pl.when((z == y) & (c == xl))
    def _():
        landed(w1.at[l, pl.ds(0, 448)], as_.at[l])


HALF = CAP // 2


def slot_of(z, c, k):
    return 2 * rem(z + k, 4) + c


def rows_sibling(buf, z, c, ss, rs):
    own = buf.at[2 * z + c]
    send(own, own, ss, rs.at[0], c=1 - c)


def rows_send(buf, z, c, ss, rs):
    a, b = buf.at[2 * z + c, pl.ds(0, HALF)], buf.at[2 * z + c, pl.ds(HALF, HALF)]
    up, down = dict(z=rem(z + 1, 4)), dict(z=rem(z + 3, 4))
    send(a, a, ss, rs.at[1], **up)
    send(b, b, ss, rs.at[3], **down)
    send(b, b, ss, rs.at[2], **up)
    send(a, a, ss, rs.at[4], **down)


def rows_pass(buf, z, c, ss, rs):
    lo, hi = slot_of(z, c, 3), slot_of(z, c, 1)
    a = buf.at[lo, pl.ds(0, HALF)]
    b = buf.at[hi, pl.ds(HALF, HALF)]
    landed(a, rs.at[1])
    send(a, a, ss, rs.at[5], z=rem(z + 1, 4))
    landed(b, rs.at[3])
    send(b, b, ss, rs.at[5], z=rem(z + 3, 4))


def rows_near(buf, z, c, ss, rs):
    lo, hi = slot_of(z, c, 3), slot_of(z, c, 1)
    landed(buf.at[lo, pl.ds(HALF, HALF)], rs.at[2])
    send(buf.at[lo], buf.at[lo], ss, rs.at[6], c=1 - c)
    landed(buf.at[hi, pl.ds(0, HALF)], rs.at[4])
    send(buf.at[hi], buf.at[hi], ss, rs.at[6], c=1 - c)


def rows_near_in(buf, rs):
    landed(buf.at[pl.ds(0, 2)], rs.at[6])


def rows_far(buf, z, c, ss, rs):
    far = buf.at[slot_of(z, c, 2)]
    landed(far, rs.at[5])
    send(far, far, ss, rs.at[7], c=1 - c)


def rows_far_in(buf, rs):
    landed(buf.at[0], rs.at[7])


def rows_left(buf, ss):
    landed(buf.at[pl.ds(0, 7)], ss)


def rows_before(k, buf, z, c, ss, rs):
    @pl.when(k == 0)
    def _():
        landed(buf.at[2 * z + 1 - c], rs.at[0])

    @pl.when((k == 1) & (c == 0))
    def _():
        rows_pass(buf, z, c, ss, rs)
        rows_near(buf, z, c, ss, rs)

    @pl.when((k == 2) & (c == 1))
    def _():
        rows_near(buf, z, c, ss, rs)

    @pl.when(((k == 1) & (c == 1)) | ((k == 2) & (c == 0)))
    def _():
        rows_near_in(buf, rs)

    @pl.when(k == 3)
    def _():
        @pl.when(c == 1)
        def _():
            rows_far(buf, z, c, ss, rs)

        rows_far_in(buf, rs)


def rows_midway(k, buf, z, c, ss, rs):
    @pl.when((k == 0) & (c == 1))
    def _():
        rows_send(buf, z, c, ss, rs)

    @pl.when((k == 1) & (c == 1))
    def _():
        rows_pass(buf, z, c, ss, rs)

    @pl.when((k == 2) & (c == 0))
    def _():
        rows_far(buf, z, c, ss, rs)


def slots(k, z):
    near = (k == 1) | (k == 2)
    chip = rem(z + jnp.where(k == 3, 2, 0), 4)
    first = jnp.where(near, 2 * rem(z + 3, 4) + k - 1, 2 * chip)
    second = jnp.where(near, 2 * rem(z + 1, 4) + k - 1, 2 * chip + 1)
    return near, first, second


def sums_send(k, z, c, partial, own, sibout, sibin, out, inn, sbs, sbr, rss, rsr):
    near, first, second = slots(k, z)
    far = jnp.where(k == 0, 0, 1)
    mine = near & (c == k - 1)
    base = first - jnp.where(near, 0, rem(first, 2))
    t0 = partial(jnp.where(near, first, base + 1 - c))
    m0 = jnp.where(near, 2, far)

    @pl.when(jnp.logical_not(mine))
    def _():
        sibout[m0] = t0.astype(BF)
        send(sibout.at[m0], sibin.at[m0], sbs, sbr.at[m0], c=1 - c)

    @pl.when(mine)
    def _():
        landed(sibin.at[2], sbr.at[2])
        out[0] = (t0 + sibin[2].astype(F32)).astype(BF)
        send(out.at[0], inn.at[0], rss, rsr, z=rem(z + 3, 4))

    t1 = partial(jnp.where(near, second, base + c))
    theirs = near & (c != k - 1)

    @pl.when(theirs)
    def _():
        sibout[3] = t1.astype(BF)
        send(sibout.at[3], sibin.at[3], sbs, sbr.at[3], c=1 - c)

    @pl.when(jnp.logical_not(theirs))
    def _():
        m1 = jnp.where(near, 3, far)
        landed(sibin.at[m1], sbr.at[m1])
        both = t1 + sibin[m1].astype(F32)

        @pl.when(k == 0)
        def _():
            own[...] = both

        @pl.when(k != 0)
        def _():
            o = jnp.where(near, 1, 2)
            out[o] = both.astype(BF)
            send(out.at[o], inn.at[o], rss, rsr, z=rem(z + jnp.where(near, 1, 2), 4))


def sums_total(own, inn, rsr):
    landed(inn, rsr)
    total = own[...]
    for i in range(3):
        total = total + inn[i].astype(F32)
    return total


def lanes(shape):
    return lax.broadcasted_iota(jnp.int32, shape, len(shape) - 1)


def turn(v, cos, sin):
    low = rem(lanes(v.shape), 64) < 16
    partner = jnp.where(low, pltpu.roll(v, 112, 1), pltpu.roll(v, 16, 1))
    return v * cos + partner * sin


def nt(a, b):
    return lax.dot_general(a, b, (((1,), (1,)), ((), ())), preferred_element_type=F32)


def tn(a, b):
    return lax.dot_general(a, b, (((0,), (0,)), ((), ())), preferred_element_type=F32)


def nn(a, b):
    return jnp.dot(a, b, preferred_element_type=F32)


def stats(x):
    centre = x - jnp.mean(x, axis=-1, keepdims=True)
    r = lax.rsqrt(jnp.mean(centre * centre, axis=-1, keepdims=True) + EPSILON)
    return centre, r


def expand(t):
    lane = lanes(t.shape)
    rot = rem(lane, 64) < ROT
    first = lane < 64
    cos = jnp.where(rot, jnp.where(first, t, pltpu.roll(t, 64, 1)), 1.0)
    sin = jnp.where(rot, jnp.where(first, pltpu.roll(t, 96, 1), pltpu.roll(t, 32, 1)), 0.0)
    return cos, sin, t[:, 64:65]


def expand(t):
    lane = lanes(t.shape)
    rot = rem(lane, 64) < ROT
    first = lane < 64
    cos = jnp.where(rot, jnp.where(first, t, pltpu.roll(t, 64, 1)), 1.0)
    sin = jnp.where(rot, jnp.where(first, pltpu.roll(t, 96, 1), pltpu.roll(t, 32, 1)), 0.0)
    return cos, sin, t[:, 64:65]


def normed_rows(l, x, vec):
    centre, r = stats(x[...])
    return (centre * r * vec[8 * l : 8 * l + 1, :] + vec[8 * l + 1 : 8 * l + 2, :]).astype(BF)


def forward_pass(
    l, z, c, vec, bins, w1, w2, tabs, nall, qkv, prob, a2, pre, raw, sums, rows, spill, early, hook
):
    ss, rs = rows
    row = 8 * l

    def step(i):
        k = jnp.where(i == 0, 3, jnp.where(i == 3, 0, i)) if early else i
        hook(i)
        if not early:
            rows_before(k, nall, z, c, ss, rs)
        _, sa, sb = slots(k, z)
        n = jnp.concatenate([nall[sa], nall[sb]], axis=0)
        raw[:, 0:QKV] = nn(n, w1[:, :QKV])
        val = nn(n, w1[:, QKV:]) + bins[row : row + 1, :]
        pre[sa] = val[:CAP]
        pre[sb] = val[CAP:]

        def act(i):
            u, t = div(i, 6), rem(i, 6)
            s = jnp.where(u == 0, sa, sb)
            at = pl.ds(pl.multiple_of(t * 32, 32), 32)
            v = pre[s, at, :]
            g = 0.5 * v * (1.0 + jnp.tanh(C0 * (v + C1 * v * v * v)))
            a2[s, at, 128:] = g.astype(BF)

        loop(12, act)
        if not early:
            rows_midway(k, nall, z, c, ss, rs)
        for u, s in enumerate((sa, sb)):
            at = slice(u * CAP, (u + 1) * CAP)
            cos, sin, start = expand(tabs[s])
            q = turn(raw[at, 0:128], cos, sin).astype(BF)
            kk = turn(raw[at, 128:256], cos, sin).astype(BF)
            v = raw[at, 256:384].astype(BF)
            qkv[s, :, 0:128] = q
            qkv[s, :, 128:256] = kk
            qkv[s, :, 256:384] = v
            q = q * jnp.asarray(1.0 / math.sqrt(HEAD), BF)
            key_at = lanes((CAP, CAP))
            query_at = lax.broadcasted_iota(jnp.int32, (CAP, CAP), 0)
            allowed = (key_at >= start.astype(jnp.int32)) & (key_at <= query_at)
            head = lanes((CAP, 128)) < HEAD
            mixed = []
            for h in range(2):
                qh = jnp.where(head if h == 0 else ~head, q, jnp.zeros_like(q))
                score = jnp.where(allowed, nt(qh, kk), NEGATIVE)
                e = jnp.exp(score - jnp.max(score, axis=-1, keepdims=True))
                w = e / jnp.sum(e, axis=-1, keepdims=True)
                prob[2 * s + h] = w
                mixed.append(nn(w.astype(BF), v))
            a2[s, :, 0:128] = jnp.where(head, mixed[0], mixed[1]).astype(BF)
        if spill is not None:
            prob_o, pre_o, sem = spill
            for s in (sa, sb):
                local(prob.at[pl.ds(2 * s, 2)], prob_o.at[pl.ds(2 * s, 2)], sem.at[0])
                local(pre.at[s], pre_o.at[s], sem.at[1])
        hook(i, 1)
        sums_send(k, z, c, lambda s: nn(a2[s], w2[...]), *sums)

    loop(4, step)


def forward_rows(l, x, vec, sums):
    own, _, _, out, inn, _, _, rss, rsr = sums
    return x[...] + (sums_total(own, inn, rsr) + vec[8 * l + 2 : 8 * l + 3, :])


def backward_pass(
    z, c, w1, w2, tabs, qkv, prob, pre, raw, gall, dp, sums, rows, early, hook
):
    ss, rs = rows

    def step(i):
        k = jnp.where(i == 0, 3, jnp.where(i == 3, 0, i)) if early else i
        hook(i)
        if not early:
            rows_before(k, gall, z, c, ss, rs)
        _, sa, sb = slots(k, z)
        g = jnp.concatenate([gall[sa], gall[sb]], axis=0)
        raw[...] = nt(g, w2[...])

        def act(i):
            u, t = div(i, 12), rem(i, 12)
            s = jnp.where(u == 0, sa, sb)
            at = pl.ds(pl.multiple_of(t * 16, 16), 16)
            v = pre[s, at, :]
            d = raw[pl.ds(pl.multiple_of(u * CAP + t * 16, 16), 16), 128:]
            t1 = jnp.tanh(C0 * (v + C1 * v * v * v))
            slope = 0.5 * (1.0 + t1) + 0.5 * v * (1.0 - t1 * t1) * (C0 + (3.0 * C0 * C1) * v * v)
            dp[s, at, QKV:] = (d * slope).astype(BF)

        loop(24, act)
        if not early:
            rows_midway(k, gall, z, c, ss, rs)
        for u, s in enumerate((sa, sb)):
            at = slice(u * CAP, (u + 1) * CAP)
            cos, sin, _ = expand(tabs[s])
            m = raw[at, 0:128].astype(BF)
            q, kk, v = qkv[s, :, 0:128], qkv[s, :, 128:256], qkv[s, :, 256:384]
            head = lanes((CAP, 128)) < HEAD
            dq, dk, dv = [], [], []
            for h in range(2):
                mine = head if h == 0 else ~head
                mh = jnp.where(mine, m, jnp.zeros_like(m))
                w = prob[2 * s + h]
                soft = nt(mh, v)
                dv.append(tn(w.astype(BF), mh))
                wd = w * soft
                ds = (wd - w * jnp.sum(wd, axis=-1, keepdims=True)).astype(BF)
                dq.append(nn(ds, kk))
                dk.append(tn(ds, jnp.where(mine, q, jnp.zeros_like(q))))
            scale = 1.0 / math.sqrt(HEAD)
            dq = jnp.where(head, dq[0], dq[1]) * scale
            dk = (dk[0] + dk[1]) * scale
            dp[s, :, 0:128] = turn(dq, cos, -sin).astype(BF)
            dp[s, :, 128:256] = turn(dk, cos, -sin).astype(BF)
            dp[s, :, 256:384] = (dv[0] + dv[1]).astype(BF)
        sums_send(k, z, c, lambda s: nt(dp[s], w1[...]), *sums)

    loop(4, step)


def second_grads(a2, gall, g2):
    rows = LINE * CAP
    g = gall[...].reshape(rows, D)
    val = tn(a2[...].reshape(rows, DEEP), g)
    for s in range(2):
        for q in range(4):
            g2[s, q, 0:16, :] = val[64 * s + 16 * q : 64 * s + 16 * q + 16].astype(BF)
            base = 128 + 256 * s + 64 * q
            g2[s, q, 16:80, :] = val[base : base + 64].astype(BF)


def first_grads(nall, dp, g1q, g1i):
    rows = LINE * CAP
    d = dp[...].reshape(rows, WIDE)
    for t in range(2):
        val = tn(nall[:, :, t * 512 : (t + 1) * 512].reshape(rows, 512), d).astype(BF)
        for s in range(8):
            sh = 8 * t + s
            zz, hh, cc = sh // 4, (sh // 2) % 2, sh % 2
            for q in range(4):
                part = val[64 * s + 16 * q : 64 * s + 16 * q + 16]
                at = (2 * zz + cc) * 16
                g1q[hh, q, at : at + 16, :] = part[:, :QKV]
                g1i[hh, q, at : at + 16, :] = part[:, QKV:]


def backward_rows(l, z, c, g_ref, x, vec, gall, dp, lns, loc, sums):
    zero = jnp.zeros((1, 128), F32)
    col = pl.ds(pl.multiple_of((2 * z + c) * 128, 128), 128)
    bfc = jnp.zeros((1, 128), F32)
    b_in = jnp.zeros((1, HID), F32)
    for s in range(LINE):
        bfc = bfc + jnp.sum(gall[s, :, col].astype(F32), axis=0, keepdims=True)
        b_in = b_in + jnp.sum(dp[s, :, QKV:].astype(F32), axis=0, keepdims=True)
    loc[...] = jnp.concatenate(
        [zero, zero, bfc] + [b_in[:, 128 * i : 128 * i + 128] for i in range(4)] + [zero], axis=0
    )
    own, _, _, out, inn, _, _, rss, rsr = sums
    ngrad = sums_total(own, inn, rsr)
    centre, r = stats(x[...])
    xhat = centre * r
    e = ngrad * vec[8 * l : 8 * l + 1, :]
    ex = jnp.mean(e * xhat, axis=-1, keepdims=True)
    gain = jnp.sum(ngrad * xhat, axis=0, keepdims=True)
    bias = jnp.sum(ngrad, axis=0, keepdims=True)
    both = jnp.concatenate([gain, bias] + [jnp.zeros((6, D), F32)], axis=0)
    for i in range(LINE):
        lns[i] = both[:, 128 * i : 128 * i + 128]
    return g_ref[...] + r * (e - jnp.mean(e, axis=-1, keepdims=True) - xhat * ex)


def member(jj):
    return dict(z=div(jj, 2), c=rem(jj, 2))


def small_start(l, me, lns, zs, s5, q5):
    j = me[7]

    def go(k):
        jj = rem(j + k, LINE)
        send(lns.at[l, jj], zs.at[l, j], s5.at[l], q5.at[l], **member(jj))

    loop(LINE - 1, lambda k: go(k + 1))


def small_spread(l, me, lns, loc, zs, ps, q5, s6, q6):
    y, xl, z, xh, c, x, p, j = me

    landed(zs.at[l, pl.ds(0, LINE - 1)], q5.at[l])
    zs[l, j] = lns[l, j] + loc[l]
    total = zs[l, 0]
    for i in range(1, LINE):
        total = total + zs[l, i]
    ps[l, p] = total

    def spread(k):
        send(ps.at[l, p], ps.at[l, p], s6.at[l], q6.at[l], **plane_member(y, x, k))

    loop(15, lambda k: spread(k + 1))


def small_last(l, me, ps, tot, q6, s8, q8):
    y, xl, z, xh, c, x, p, j = me

    landed(ps.at[l, pl.ds(0, 15)], q6.at[l])
    total = ps[l, 0]
    for i in range(1, 16):
        total = total + ps[l, i]
    tot[l, c] = total
    send(tot.at[l, c], tot.at[l, c], s8.at[l], q8.at[l], c=1 - c)


def second_p1(l, me, g2, ga1, gb1, s, q):
    y, xl, z, xh, c, x, p, j = me
    left, right = pl.ds(0, 512), pl.ds(512, 512)
    for d in (1, 2, 3):
        dev = along_x(x, d)

        @pl.when(dev["xh"] == c)
        def _():
            send(
                g2.at[dev["xl"], :, :, left], ga1.at[l, d - 1], s.at[l, 0], q.at[l, 0], **dev
            )

        yy = along_y(y, d)
        send(g2.at[:, yy["y"], :, right], gb1.at[l, d - 1], s.at[l, 1], q.at[l, 1], **yy)


def second_p2(l, me, g2, ga1, gb1, ga2, gb2, sga, sgb, s, q):
    y, xl, z, xh, c, x, p, j = me
    landed(gb1.at[l], q.at[l, 1])

    def add_right(i):
        h, t = div(i, 5), rem(i, 5)
        at = pl.ds(pl.multiple_of(16 * t, 16), 16)
        acc = g2[h, y, at, 512:].astype(F32)
        for d in range(3):
            acc = acc + gb1[l, d, h, at, :].astype(F32)
        sgb[h, at, :] = acc.astype(BF)

    loop(10, add_right)
    for d in (1, 2, 3):
        dev = along_x(x, d)

        @pl.when(dev["xh"] == c)
        def _():
            send(sgb.at[dev["xl"]], gb2.at[l, d - 1], s.at[l, 2], q.at[l, 2], **dev)

    @pl.when(xh == c)
    def _():
        landed(ga1.at[l], q.at[l, 0])

        def add_left(i):
            yy, t = div(i, 5), rem(i, 5)
            at = pl.ds(pl.multiple_of(16 * t, 16), 16)
            acc = g2[xl, yy, at, 0:512].astype(F32)
            for d in range(3):
                acc = acc + ga1[l, d, yy, at, :].astype(F32)
            sga[yy, at, :] = acc.astype(BF)

        loop(20, add_left)
        for d in (1, 2, 3):
            yy = along_y(y, d)
            send(sga.at[yy["y"]], ga2.at[l, d - 1], s.at[l, 3], q.at[l, 3], **yy)


def second_p3(l, me, ga2, gb2, sga, sgb, red2, fo, ff, s, q, s4, q4):
    y, xl, z, xh, c, x, p, j = me
    row16 = pl.ds(pl.multiple_of(16 * y, 16), 16)
    row64 = pl.ds(pl.multiple_of(64 * y, 64), 64)

    @pl.when(xh == c)
    def _():
        landed(gb2.at[l], q.at[l, 2])
        landed(ga2.at[l], q.at[l, 3])

        def add(t):
            at = pl.ds(pl.multiple_of(16 * t, 16), 16)
            a = sga[y, at, :].astype(F32)
            b = sgb[xl, at, :].astype(F32)
            for d in range(3):
                a = a + ga2[l, d, at, :].astype(F32)
                b = b + gb2[l, d, at, :].astype(F32)
            red2[l, at, 0:512] = a.astype(BF)
            red2[l, at, 512:1024] = b.astype(BF)

        loop(5, add)

        parts = (
            (red2.at[l, pl.ds(0, 16)], fo.at[l, row16]),
            (red2.at[l, pl.ds(16, 64)], ff.at[l, row64]),
        )
        for src, dst in parts:
            send(src, dst, s4.at[l, 0], q4.at[l, 0], xl=1 - xl, c=xl)

            @pl.when(xl == c)
            def _():
                local(src, dst, q4.at[l, 0])

            @pl.when(xl != c)
            def _():
                send(src, dst, s4.at[l, 1], q4.at[l, 0], c=xl)


def second_share(l, me, w2, fo, ff, q4, s4):
    y = me[0]
    row16 = pl.ds(pl.multiple_of(16 * y, 16), 16)
    row64 = pl.ds(pl.multiple_of(64 * y, 64), 64)
    landed(w2.at[l, pl.ds(0, 80)], q4.at[l, 0])
    for block in (fo.at[l, row16], ff.at[l, row64]):
        for d in (1, 2, 3):
            send(block, block, s4.at[l, 2], q4.at[l, 1], **along_y(y, d))


def second_left(l, me, ga1, gb1, ga2, gb2, s):
    y, xl, z, xh, c, x, p, j = me
    landed(gb1.at[l], s.at[l, 1])
    for same, n in ((True, 1), (False, 2)):

        @pl.when((xh == c) if same else (xh != c))
        def _():
            landed(ga1.at[l, pl.ds(0, n)], s.at[l, 0])
            landed(gb2.at[l, pl.ds(0, n)], s.at[l, 2])

    @pl.when(xh == c)
    def _():
        landed(ga2.at[l], s.at[l, 3])


def by_kind(ll, f):
    @pl.when(ll == 0)
    def _():
        f(pl.ds(0, QKV), 0)

    @pl.when(ll == 1)
    def _():
        f(pl.ds(0, HID), 1)


TOP, LOW = pl.ds(0, 64), pl.ds(64, 64)


def first_p1(l, me, g1q, g1i, ra1, rbq, rbi, s, q):
    y, xl, z, xh, c, x, p, j = me
    for d in (1, 2, 3):
        dev = along_x(x, d)
        hh = dev["xh"]

        def go(cols, kind):
            src = (g1q, g1i)[kind].at[hh, :, TOP]
            send(src, ra1.at[l, d - 1, :, :, cols], s.at[l, d], q.at[l, 0], **dev)

        by_kind(dev["xl"], go)
        yy = along_y(y, d)
        send(g1q.at[:, yy["y"], LOW], rbq.at[l, d - 1], s.at[l, 0], q.at[l, 1], **yy)
        send(g1i.at[:, yy["y"], LOW], rbi.at[l, d - 1], s.at[l, 0], q.at[l, 1], **yy)


def first_p2(l, me, w1, g1q, g1i, ra1, rbq, rbi, ra2, rb2, sra, sbq, sbi, s, q):
    y, xl, z, xh, c, x, p, j = me
    by_kind(xl, lambda cols, kind: landed(ra1.at[l, :, :, :, cols], q.at[l, 0]))

    def add_top(i):
        yy, t = div(i, 4), rem(i, 4)
        at = pl.ds(pl.multiple_of(16 * t, 16), 16)

        def go(cols, kind):
            acc = (g1q, g1i)[kind][xh, yy, at, :].astype(F32)
            for d in range(3):
                acc = acc + ra1[l, d, yy, at, cols].astype(F32)
            sra[yy, at, cols] = acc.astype(BF)

        by_kind(xl, go)

    loop(16, add_top)
    for d in (1, 2, 3):
        yy = along_y(y, d)

        def go(cols, kind):
            src = sra.at[yy["y"], :, cols]
            send(src, ra2.at[l, d - 1, :, cols], s.at[l, 4], q.at[l, 2], **yy)

        by_kind(xl, go)
    landed(w1.at[l, pl.ds(0, 384)], q.at[l, 1])

    def add_low(i):
        h, t = div(i, 4), rem(i, 4)
        at = pl.ds(pl.multiple_of(16 * t, 16), 16)
        here = pl.ds(pl.multiple_of(64 + 16 * t, 16), 16)
        a = g1q[h, y, here, :].astype(F32)
        b = g1i[h, y, here, :].astype(F32)
        for d in range(3):
            a = a + rbq[l, d, h, at, :].astype(F32)
            b = b + rbi[l, d, h, at, :].astype(F32)
        sbq[h, at, :] = a.astype(BF)
        sbi[h, at, :] = b.astype(BF)

    loop(8, add_low)
    for d in (1, 2, 3):
        dev = along_x(x, d)
        hh = dev["xh"]

        def go(cols, kind):
            src = (sbq, sbi)[kind].at[hh]
            send(src, rb2.at[l, d - 1, :, cols], s.at[l, 4 + d], q.at[l, 3], **dev)

        by_kind(dev["xl"], go)


def first_p3(l, me, ra2, rb2, sra, sbq, sbi, red1, fq, fi, s, q, s3, q3):
    y, xl, z, xh, c, x, p, j = me
    by_kind(xl, lambda cols, kind: landed(ra2.at[l, :, :, cols], q.at[l, 2]))
    by_kind(xl, lambda cols, kind: landed(rb2.at[l, :, :, cols], q.at[l, 3]))

    def add(t):
        at = pl.ds(pl.multiple_of(16 * t, 16), 16)

        def go(cols, kind):
            a = sra[y, at, cols].astype(F32)
            b = (sbq, sbi)[kind][xh, at, :].astype(F32)
            for d in range(3):
                a = a + ra2[l, d, at, cols].astype(F32)
                b = b + rb2[l, d, at, cols].astype(F32)
            red1[l, at, cols] = a.astype(BF)
            red1[l, pl.ds(pl.multiple_of(64 + 16 * t, 16), 16), cols] = b.astype(BF)

        by_kind(xl, go)

    loop(4, add)
    row16 = pl.ds(pl.multiple_of(16 * y, 16), 16)

    def back(jj):
        at = pl.ds(pl.multiple_of(16 * jj, 16), 16)

        def move(src, dst):
            @pl.when(jj == j)
            def _():
                local(src, dst, q3.at[l])

            @pl.when(jj != j)
            def _():
                send(src, dst, s3.at[l], q3.at[l], **member(jj))

        @pl.when(xl == 0)
        def _():
            for n in range(3):
                cols = pl.ds(pl.multiple_of(n * D + 128 * j, 128), 128)
                move(red1.at[l, at, pl.ds(128 * n, 128)], fq.at[l, row16, cols])

        @pl.when(xl == 1)
        def _():
            cols = pl.ds(pl.multiple_of(HID * j, HID), HID)
            move(red1.at[l, at], fi.at[l, row16, cols])

    loop(LINE, back)


def first_left(l, me, w1, ra1, ra2, rb2, s):
    y, xl, z, xh, c, x, p, j = me
    landed(w1.at[l, pl.ds(0, 384)], s.at[l, 0])
    for d in (1, 2, 3):
        there = along_x(x, d)["xl"]
        by_kind(there, lambda cols, kind: landed(ra1.at[l, 0, :, :, cols], s.at[l, d]))
        by_kind(there, lambda cols, kind: landed(rb2.at[l, 0, :, cols], s.at[l, 4 + d]))
    by_kind(xl, lambda cols, kind: landed(ra2.at[l, :, :, cols], s.at[l, 4]))


def first_share(l, me, fq, fi, q3, s7, q7):
    y, xl, z, xh, c, x, p, j = me
    row16 = pl.ds(pl.multiple_of(16 * y, 16), 16)

    for v, f in ((0, fq), (1, fi)):

        @pl.when(xl == v)
        def _():
            landed(f.at[l, row16], q3.at[l])

            at = f.at[l, row16]
            for d in (1, 2, 3):
                send(at, at, s7.at[l], q7.at[l, d], **along_y(y, d))
            send(at, at, s7.at[l], q7.at[l, 0], xl=1 - xl)


def first_pass(l, me, fq, fi, s7, q7):
    y, xl, z, xh, c, x, p, j = me
    for v, f in ((0, fq), (1, fi)):

        @pl.when(xl == v)
        def _():
            for d in (1, 3, 2):
                at = f.at[l, pl.ds(pl.multiple_of(16 * rem(y + 4 - d, 4), 16), 16)]
                landed(at, q7.at[l, d])
                send(at, at, s7.at[l], q7.at[l, 0], xl=1 - xl)


def owners_in(l, me, w2, fq, fi, q4, q7):
    xl = me[1]
    landed(w2.at[l, pl.ds(0, 240)], q4.at[l, 1])
    for v, f in ((0, fq), (1, fi)):

        @pl.when(xl != v)
        def _():
            landed(f.at[l], q7.at[l, 0])


def owners_left(l, me, w2, lns, ps, tot, red1, s3, s4, s5, s6, s7, s8):
    y, xl, z, xh, c, x, p, j = me
    landed(lns.at[l, pl.ds(0, LINE - 1)], s5.at[l])
    landed(ps.at[l, pl.ds(0, 15)], s6.at[l])
    landed(w2.at[l, pl.ds(0, 240)], s4.at[l, 2])

    @pl.when(xh == c)
    def _():
        landed(w2.at[l, pl.ds(0, 80)], s4.at[l, 0])

        @pl.when(xl != c)
        def _():
            landed(w2.at[l, pl.ds(0, 80)], s4.at[l, 1])

    by_kind(xl, lambda cols, kind: landed(red1.at[l, pl.ds(0, 112), cols], s3.at[l]))
    for v, unit in ((0, 48), (1, 64)):

        @pl.when(xl == v)
        def _():
            landed(w2.at[l, pl.ds(0, 7 * unit)], s7.at[l])

    landed(tot.at[l, c], s8.at[l])


def no_hook(*a):
    pass


def used_rows(len_ref):
    total = len_ref[0, 0]
    for k in range(1, SLOTS):
        total = total + len_ref[0, k]
    return lax.broadcasted_iota(jnp.int32, (CAP, 128), 0) < total


def make_table(row_of_lengths):
    shape = (CAP, 128)
    row = lax.broadcasted_iota(jnp.int32, shape, 0).astype(F32)
    lane = lanes(shape)
    start = jnp.zeros(shape, F32)
    end = jnp.zeros((1, 1), F32)
    for k in range(SLOTS):
        n = row_of_lengths[:, k : k + 1]
        end = end + n
        start = start + jnp.where(row >= end, n, 0.0)
    which = rem(lane, ROT // 2).astype(F32)
    angle = (row - start) * jnp.exp(which * (-2.0 * math.log(10000.0) / ROT))
    sine = jnp.sin(angle)
    sine = jnp.where(rem(lane, ROT) < ROT // 2, -sine, sine)
    return jnp.where(lane < 32, jnp.cos(angle), jnp.where(lane < 64, sine, start))


def whole_kernel(
    wqkv, win, wo, wfc, len_ref, gain_ref, bias_ref, bfc_ref, bin_ref, x0, cot,
    x2_o, g0_ref, fs_ref, fq, fi, fo, ff, prob_o, pre_o,
    w1, w2, sm, lens, sma, tabs, vec, bins,
    nall, qkv, a2, prob, pre, raw, gall, dp, x1,
    own, sibout, sibin, out, inn, own1, out1, inn1,
    g1q, g1i, g2, lns, loc, ga1, gb1, ga2, gb2, sga, sgb, ra1, rbq, rbi, ra2, rb2, sra, sbq, sbi,
    red1, red2, zs, ps, tot,
    as_, ar, bs, br, cs, cr, xs, xr, ys, yr, ts, tr, ms, mr, ns, nr,
    rows_s, rows_r, sbs, sbr, rss, rsr, spill, fill, x2s,
    s1, q1, s2, q2, s3, q3, s4, q4, s5, q5, s6, q6, s7, q7, s8, q8,
):
    y, xl, z, xh, c = place()
    x = 2 * xh + xl
    p = 4 * y + x
    j = 2 * z + c
    me = (y, xl, z, xh, c, x, p, j)
    bar = pltpu.get_barrier_semaphore()
    greet_line(bar, z, c)
    greet_plane(bar, y, x)
    for k in range(1, 8):
        signal(bar, y=rem(y + k // 2, 4), xl=rem(xl + k % 2, 2), c=1 - c)
    signal(bar, xl=1 - xl, xh=1 - xh, c=1 - c)

    source = (z == y) & (c == xl)
    sm[...] = jnp.zeros(sm.shape, F32)
    for r, ref in enumerate((gain_ref, bias_ref, bfc_ref)):
        v = ref[...].astype(F32)
        v = jnp.concatenate([v, v], axis=1)
        for l in range(LAYERS):
            sm[8 * l + r : 8 * l + r + 1, 0:128] = v[l : l + 1]
    v = bin_ref[...].astype(F32)
    for l in range(LAYERS):
        sm[8 * l + 3 : 8 * l + 4, :] = v[l : l + 1]
    tile = lanes((8, 128))
    mine = jnp.zeros((8, 128), F32)
    for k in range(SLOTS):
        mine = mine + jnp.where(tile == k, len_ref[0, k].astype(F32), 0.0)
    lens[j] = mine
    used = used_rows(len_ref)[:, 0:1]
    gall[1, 2 * z + c] = jnp.where(used, cot[...], 0.0).astype(BF)
    pl.semaphore_wait(bar, 30)

    @pl.when(source)
    def _():
        def to(jj):
            @pl.when(jj == j)
            def _():
                local(sm, sma.at[p], mr)

            @pl.when(jj != j)
            def _():
                send(sm, sma.at[p], ms, mr, **member(jj))

        loop(LINE, to)

    for k in range(1, LINE):
        send(lens.at[j], lens.at[j], ts, tr, **member(rem(j + k, LINE)))
    weights_z(0, me, wqkv, win, wo, wfc, w1, w2, as_, ar, cs, cr)
    g1 = gall.at[1]
    gs, gr = rows_s.at[2], rows_r.at[2]
    rows_sibling(g1, z, c, gs, gr)
    rows_send(g1, z, c, gs, gr)
    landed(sma.at[p], mr)

    def small_out(k):
        send(sma.at[p], sma.at[p], ns, nr, **plane_member(y, x, k))

    loop(15, lambda k: small_out(k + 1))
    weights_f1(0, me, w2, cr, xs, xr)
    weights_p1(0, me, w1, ar, bs, br)
    landed(sma.at[pl.ds(0, 15)], nr)
    half = lanes((16, 128)) < 64
    for t in range(8):
        vec[:, 128 * t : 128 * t + 128] = jnp.where(half, sma[2 * t, :, :128], sma[2 * t + 1, :, :128])
    for l in range(LAYERS):
        at = 8 * l + 3
        bins[8 * l : 8 * l + 1, 0:256] = sma[2 * j, at : at + 1, :]
        bins[8 * l : 8 * l + 1, 256:512] = sma[2 * j + 1, at : at + 1, :]

    def sums_of(n):
        sems = sbs.at[n], sbr.at[n], rss.at[n], rsr.at[n]
        if n == 1:
            return (own1, gall.at[0, pl.ds(0, 4)], gall.at[0, pl.ds(4, 4)], out1, inn1) + sems
        return (own, sibout, sibin, out, inn) + sems

    def rows_of(n):
        return rows_s.at[n], rows_r.at[n]

    n0 = nall.at[0]
    ss, rs = rows_of(0)
    n0[2 * z + c] = normed_rows(0, x0, vec)
    rows_sibling(n0, z, c, ss, rs)
    rows_send(n0, z, c, ss, rs)
    weights_f2(0, me, w2, xr, ys, yr)
    rows_pass(g1, z, c, gs, gr)
    landed(lens.at[pl.ds(0, LINE - 1)], tr)

    def table(s):
        tabs[s] = make_table(lens[s, 0:1, :])

    loop(LINE, table)
    weights_p2(0, me, w1, bs, br)
    rows_near(g1, z, c, gs, gr)
    rows_pass(n0, z, c, ss, rs)
    rows_far(g1, z, c, gs, gr)
    rows_near(n0, z, c, ss, rs)
    rows_far(n0, z, c, ss, rs)
    for buf, rr in ((n0, rs), (g1, gr)):
        landed(buf.at[0], rr.at[0])
        rows_near_in(buf, rr)
    weights_in1(0, w1, br)
    for buf, rr in ((n0, rs), (g1, gr)):
        rows_far_in(buf, rr)
    weights_z(1, me, wqkv, win, wo, wfc, w1, w2, as_, ar, cs, cr)

    def hook_f0(i, late=0):
        if late:

            @pl.when(i == 0)
            def _():
                weights_in2(0, me, w2, cr, yr)

        else:

            @pl.when(i == 1)
            def _():
                weights_p1(1, me, w1, ar, bs, br)

            @pl.when(i == 2)
            def _():
                weights_f1(1, me, w2, cr, xs, xr)
                weights_p2(1, me, w1, bs, br)

            @pl.when(i == 3)
            def _():
                weights_f2(1, me, w2, xr, ys, yr)

    forward_pass(
        0, z, c, vec, bins, w1.at[0], w2.at[0], tabs, n0, qkv.at[0], prob, a2.at[0], pre,
        raw, sums_of(0), rows_of(0), (prob_o, pre_o, spill), True, hook_f0,
    )
    x1[...] = forward_rows(0, x0, vec, sums_of(0))

    n1 = nall.at[1]
    ss, rs = rows_of(1)
    n1[2 * z + c] = normed_rows(1, x1, vec)
    rows_sibling(n1, z, c, ss, rs)

    @pl.when(c == 0)
    def _():
        rows_send(n1, z, c, ss, rs)

    rows_left(n0, rows_s.at[0])
    rows_left(g1, gs)
    landed(sibout, sbs.at[0])
    landed(out, rss.at[0])
    landed(prob, spill.at[0])
    landed(pre, spill.at[1])
    weights_in1(1, w1, br)
    weights_in2(1, me, w2, cr, yr)
    forward_pass(
        1, z, c, vec, bins, w1.at[1], w2.at[1], tabs, n1, qkv.at[1], prob, a2.at[1], pre,
        raw, sums_of(1), rows_of(1), None, False, no_hook,
    )

    second_grads(a2.at[1], g1, g2)
    second_p1(1, me, g2, ga1, gb1, s2, q2)
    landed(sibout, sbs.at[1])

    def hook1(i):
        @pl.when(i == 2)
        def _():
            second_p2(1, me, g2, ga1, gb1, ga2, gb2, sga, sgb, s2, q2)

        @pl.when(i == 3)
        def _():
            second_p3(1, me, ga2, gb2, sga, sgb, red2, fo, ff, s2, q2, s4, q4)

    backward_pass(
        z, c, w1.at[1], w2.at[1], tabs, qkv.at[1], prob, pre, raw, g1, dp, sums_of(2), rows_of(2), True,
        hook1,
    )
    local(prob_o, prob, fill.at[0])
    local(pre_o, pre, fill.at[1])
    first_grads(n1, dp, g1q, g1i)
    first_p1(1, me, g1q, g1i, ra1, rbq, rbi, s1, q1)
    second_share(1, me, w2, fo, ff, q4, s4)
    own1[...] = forward_rows(1, x1, vec, sums_of(1))
    local(own1, x2_o, x2s)
    g0_ref[...] = jnp.where(used_rows(len_ref)[:, 0:1], cot[...], 0.0)
    g0_ref[...] = backward_rows(1, z, c, g0_ref, x1, vec, g1, dp, lns.at[1], loc.at[1], sums_of(2))

    g0 = gall.at[0]
    ss, rs = rows_of(3)
    g0[2 * z + c] = g0_ref[...].astype(BF)
    rows_sibling(g0, z, c, ss, rs)

    @pl.when(c == 0)
    def _():
        rows_send(g0, z, c, ss, rs)

    small_start(1, me, lns, zs, s5, q5)
    rows_left(n1, rows_s.at[1])
    landed(out1, rss.at[1])
    landed(sibout, sbs.at[2])
    landed(out, rss.at[2])
    landed(prob, fill.at[0])
    landed(pre, fill.at[1])

    def hook0(i):
        @pl.when(i == 1)
        def _():
            small_spread(1, me, lns, loc, zs, ps, q5, s6, q6)
            first_p2(1, me, w1, g1q, g1i, ra1, rbq, rbi, ra2, rb2, sra, sbq, sbi, s1, q1)

        @pl.when(i == 2)
        def _():
            second_left(1, me, ga1, gb1, ga2, gb2, s2)
            first_p3(1, me, ra2, rb2, sra, sbq, sbi, red1, fq, fi, s1, q1, s3, q3)

        @pl.when(i == 3)
        def _():
            first_share(1, me, fq, fi, q3, s7, q7)
            first_left(1, me, w1, ra1, ra2, rb2, s1)

    backward_pass(
        z, c, w1.at[0], w2.at[0], tabs, qkv.at[0], prob, pre, raw, g0, dp, sums_of(3), rows_of(3), False,
        hook0,
    )
    second_grads(a2.at[0], g0, g2)
    second_p1(0, me, g2, ga1, gb1, s2, q2)
    first_pass(1, me, fq, fi, s7, q7)
    first_grads(n0, dp, g1q, g1i)
    first_p1(0, me, g1q, g1i, ra1, rbq, rbi, s1, q1)
    small_last(1, me, ps, tot, q6, s8, q8)
    second_p2(0, me, g2, ga1, gb1, ga2, gb2, sga, sgb, s2, q2)
    g0_ref[...] = backward_rows(0, z, c, g0_ref, x0, vec, g0, dp, lns.at[0], loc.at[0], sums_of(3))
    small_start(0, me, lns, zs, s5, q5)
    second_p3(0, me, ga2, gb2, sga, sgb, red2, fo, ff, s2, q2, s4, q4)
    first_p2(0, me, w1, g1q, g1i, ra1, rbq, rbi, ra2, rb2, sra, sbq, sbi, s1, q1)
    small_spread(0, me, lns, loc, zs, ps, q5, s6, q6)
    second_share(0, me, w2, fo, ff, q4, s4)
    first_p3(0, me, ra2, rb2, sra, sbq, sbi, red1, fq, fi, s1, q1, s3, q3)
    small_last(0, me, ps, tot, q6, s8, q8)
    first_share(0, me, fq, fi, q3, s7, q7)
    first_pass(0, me, fq, fi, s7, q7)

    rows_left(g0, rows_s.at[3])
    landed(sibout, sbs.at[3])
    landed(out, rss.at[3])
    second_left(0, me, ga1, gb1, ga2, gb2, s2)
    first_left(0, me, w1, ra1, ra2, rb2, s1)
    for l in range(LAYERS):
        weights_left(l, me, w1, w2, as_, cs, bs, xs, ys)
    landed(lens.at[pl.ds(0, LINE - 1)], ts)
    landed(sma.at[pl.ds(0, 15)], ns)
    landed(own1, x2s)

    @pl.when(source)
    def _():
        landed(sma.at[pl.ds(0, LINE - 1)], ms)

    for l in (1, 0):
        landed(tot.at[l, 1 - c], q8.at[l])
        fs_ref[l] = tot[l]
        owners_in(l, me, w2, fq, fi, q4, q7)
        owners_left(l, me, w2, lns, ps, tot, red1, s3, s4, s5, s6, s7, s8)


def whole(wqkv, win, wo, wfc, lengths, gain, bias, b_fc, b_in, x0, cot):
    n = LAYERS
    return pl.pallas_call(
        whole_kernel,
        out_shape=(
            jax.ShapeDtypeStruct((CAP, D), F32),
            jax.ShapeDtypeStruct((CAP, D), F32),
            jax.ShapeDtypeStruct((n, 2, 8, 128), F32),
            jax.ShapeDtypeStruct((n, 64, 3 * D), BF),
            jax.ShapeDtypeStruct((n, 64, FF), BF),
            jax.ShapeDtypeStruct((n, 64, D), BF),
            jax.ShapeDtypeStruct((n, 256, D), BF),
            jax.ShapeDtypeStruct((2 * LINE, CAP, CAP), F32),
            jax.ShapeDtypeStruct((LINE, CAP, HID), F32),
        ),
        in_specs=[ANY] * 4 + [pl.BlockSpec(memory_space=pltpu.SMEM)] + [INV] * 6,
        out_specs=(ANY,) + (INV,) * 2 + (ANY,) * 6,
        scratch_shapes=[
            VMEM((n, D, WIDE), BF), VMEM((n, DEEP, D), BF), VMEM((16, 256), F32), VMEM((LINE, 8, 128), F32),
            VMEM((16, 16, 256), F32), VMEM((LINE, CAP, 128), F32), VMEM((16, D), F32), VMEM((16, HID), F32),
            VMEM((n, LINE, CAP, D), BF), VMEM((n, LINE, CAP, QKV), BF), VMEM((n, LINE, CAP, DEEP), BF),
            VMEM((2 * LINE, CAP, CAP), F32), VMEM((LINE, CAP, HID), F32), VMEM((2 * CAP, DEEP), F32),
            VMEM((n, LINE, CAP, D), BF), VMEM((LINE, CAP, WIDE), BF),
            VMEM((CAP, D), F32),
            VMEM((CAP, D), F32), VMEM((4, CAP, D), BF), VMEM((4, CAP, D), BF),
            VMEM((3, CAP, D), BF), VMEM((3, CAP, D), BF),
            VMEM((CAP, D), F32), VMEM((3, CAP, D), BF), VMEM((3, CAP, D), BF),
            VMEM((2, 4, 128, QKV), BF), VMEM((2, 4, 128, HID), BF), VMEM((2, 4, 80, D), BF),
            VMEM((n, LINE, 8, 128), F32), VMEM((n, 8, 128), F32),
            VMEM((n, 3, 4, 80, 512), BF), VMEM((n, 3, 2, 80, 512), BF),
            VMEM((n, 3, 80, 512), BF), VMEM((n, 3, 80, 512), BF),
            VMEM((4, 80, 512), BF), VMEM((2, 80, 512), BF),
            VMEM((n, 3, 4, 64, HID), BF), VMEM((n, 3, 2, 64, QKV), BF), VMEM((n, 3, 2, 64, HID), BF),
            VMEM((n, 3, 64, HID), BF), VMEM((n, 3, 64, HID), BF),
            VMEM((4, 64, HID), BF), VMEM((2, 64, QKV), BF), VMEM((2, 64, HID), BF),
            VMEM((n, 128, HID), BF), VMEM((n, 80, D), BF),
            VMEM((n, LINE, 8, 128), F32), VMEM((n, 16, 8, 128), F32), VMEM((n, 2, 8, 128), F32),
            DMA((n,)), DMA((n,)), DMA((n,)), DMA((n, 7)), DMA((n, 2)), DMA((n,)), DMA((n,)), DMA((n,)),
            DMA((n,)), DMA((n,)), DMA, DMA, DMA, DMA, DMA, DMA,
            DMA((4,)), DMA((4, 8)), DMA((4,)), DMA((4, 4)), DMA((4,)), DMA((4,)), DMA((2,)), DMA((2,)), DMA,
            DMA((n, 8)), DMA((n, 4)), DMA((n, 4)), DMA((n, 4)), DMA((n,)), DMA((n,)), DMA((n, 3)), DMA((n, 2)),
            DMA((n,)), DMA((n,)), DMA((n,)), DMA((n,)), DMA((n,)), DMA((n, 4)), DMA((n,)), DMA((n,)),
        ],
        compiler_params=pltpu.CompilerParams(
            collective_id=0, has_side_effects=True, vmem_limit_bytes=63 * 2**20
        ),
        name="whole",
    )(wqkv, win, wo, wfc, lengths, gain, bias, b_fc, b_in, x0, cot)


def per_device(
    inputs, cotangent, lengths, ln_gain, ln_bias, w_qkv, w_attn_out, w_in, b_in, w_fc, b_fc
):
    xh, c = (lax.axis_index(a) for a in ("xh", "c"))
    hidden, grad, fs, fq, fi, fo, ff, _, _ = whole(
        w_qkv, w_in, w_attn_out, w_fc, lengths, ln_gain, ln_bias, b_fc, b_in, inputs, cotangent
    )
    mine = lax.dynamic_index_in_dim(fs, xh, 1, keepdims=False)
    pick = lax.dynamic_slice(mine[:, 0:3], (0, 0, 64 * c), (LAYERS, 3, 64))
    b_in_grad = lax.dynamic_slice(mine[:, 3:7].reshape(LAYERS, HID), (0, 256 * c), (LAYERS, 256))
    return (
        hidden,
        grad,
        pick[:, 0],
        pick[:, 1],
        fq.astype(F32),
        fo.astype(F32),
        fi.astype(F32),
        b_in_grad,
        ff.astype(F32),
        pick[:, 2],
    )


def solution(mesh):
    fine = Mesh(mesh.devices.reshape(4, 2, 4, 2, 2), AXES)
    rows = P(AXES, None)
    shard = ("z", "xh", "c")
    vector, matrix = P(None, shard), P(None, shard, None)
    in_specs = (
        rows, rows, rows, vector, vector, matrix, matrix, matrix, vector, matrix, vector,
    )
    out_specs = (
        rows, rows, vector, vector, matrix, matrix, matrix, vector, matrix, vector,
    )
    return jax.shard_map(
        per_device, mesh=fine, in_specs=in_specs, out_specs=out_specs, check_vma=False
    )
```

time: 272 us -> 237 us (0.87)
  Pallas kernels: 252 us -> 224 us
  other arithmetic: 11.7 us -> 6.36 us
    pallas_call x1, Pallas kernels: 252 us -> 224 us  [whole(): pl.pallas_call(whole_kernel, out_shape=(jax.ShapeDtypeStruct((CAP, D), F3...]
    another operation x4 -> x0, other arithmetic: 3.47 us -> none  [the longest x3 2.64 us: per_device(): jnp.stack(wide + [jnp.zeros_like(b_in)] * 4, axis=1).reshape(16, 256)]
where the time goes in v4:
time: 237 us; the launch traced here: 235 us
  Pallas kernels  224 us (95%)
  other arithmetic  6.36 us (3%)
  local copies, waits for them, and re-layouts  3.83 us (2%)
    pallas_call x1, Pallas kernels, whole(): pl.pallas_call(whole_kernel, out_shape=(jax.ShapeDtypeStruct((CAP, D), F3...  224 us

profile of v4, /device:TPU:32, one launch (start us, length us, event | category | flops | bytes accessed | tf_op | source)
XLA Modules:
  0.0 234.8 jit_solution(7793305497520180622)
XLA Ops:
  0.6 223.9 %whole.1 = (f32[192,1024]{1,0:T(8,128)}, f32[192,1024]{1,0:T(8,128)}, f32[2,2,8,128]{3,2,1,0:T(8,128)}, bf16[2,64,3072]{2,1,0:T(8,128)(2,1)}, bf16[2,64,4096]{2,...) custom-call(bf16[2,64,3072]{2,1,0:T(8,128)(2,1)} %wqkv.1, ...), custom_call_target="tpu_custom_call" | custom-call | tf_op jit(solution)/shard_map/whole/pallas_call | solution.py:1291
  224.6 0.0 copy-start.4
  224.6 0.0 copy-start.1
  224.6 0.8 dynamic-slice_bitcast_fusion
  225.4 0.6 constant_dynamic-slice_fusion.3
  226.1 2.4 %convert_element_type.12 = f32[2,64,3072]{2,1,0:T(8,128)} convert(bf16[2,64,3072]{2,1,0:T(8,128)(2,1)} %get-tuple-element.20) | non-fusion elementwise | flops 393216 | bytes 2359296 | tf_op jit(solution)/shard_map/convert_element_type | solution.py:1354
  228.5 0.0 copy-start
  228.5 0.0 copy-done.4
  228.5 0.8 convert_element_type.13
  229.3 0.0 copy-done.1
  229.4 1.5 convert_element_type.14
  230.9 0.0 copy-start.3
  230.9 0.6 constant_dynamic-slice_fusion.2
  231.5 0.0 copy-done
  231.5 0.0 copy-start.2
  231.5 1.6 convert_element_type.15
  233.0 0.0 copy-done.3
  233.1 0.9 copy.27
  233.9 0.0 copy-done.2
  233.9 0.9 copy.28
  (3 shorter events, 0.0 us)
Async XLA Ops:
  224.6 3.9 %copy-start.4 = (bf16[2,64,1024]{2,1,0:T(8,128)(2,1)S(1)}, bf16[2,64,1024]{2,1,0:T(8,128)(2,1)}, u32[]{:S(2)}) copy-start(bf16[2,64,1024]{2,1,0:T(8,128)(2,1)} %get-tuple-element.21) | copy-start | bytes 786436
  224.6 4.8 %copy-start.1 = (bf16[2,64,4096]{2,1,0:T(8,128)(2,1)S(1)}, bf16[2,64,4096]{2,1,0:T(8,128)(2,1)}, u32[]{:S(2)}) copy-start(bf16[2,64,4096]{2,1,0:T(8,128)(2,1)} %get-tuple-element.22) | copy-start | bytes 3145732
  228.5 3.0 %copy-start = (bf16[2,256,1024]{2,1,0:T(8,128)(2,1)S(1)}, bf16[2,256,1024]{2,1,0:T(8,128)(2,1)}, u32[]{:S(2)}) copy-start(bf16[2,256,1024]{2,1,0:T(8,128)(2,1)} %get-tuple-element.23) | copy-start | bytes 3145732
  230.9 2.2 copy-start.3
  231.5 2.5 %copy-start.2 = (f32[192,1024]{1,0:T(8,128)S(1)}, f32[192,1024]{1,0:T(8,128)}, u32[]{:S(2)}) copy-start(f32[192,1024]{1,0:T(8,128)} %get-tuple-element.38) | copy-start | bytes 2359300
